TPU v7x, 32 devices: a whole 2x2x4 slice. The times are simulated.
32 devices in a mesh: expert: 4 (over y, core), ctx: 4 (over z), dp: 2 (over x).
Axes of the slice: x: 2, y: 2, z: 4, core: 2. Of those that a mesh axis runs over, the one named last changes fastest.
Arguments:
- layer_input: bfloat16 [8, 2048, 768], P(('expert', 'dp'), 'ctx'), may hold values from -6 to 6
- cotangent: bfloat16 [8, 2048, 768], P(('expert', 'dp'), 'ctx'), may hold values from -6 to 6
- norm_gain_one: float32 [768], replicated, may hold values from 0.5 to 1.5
- w_query: bfloat16 [768, 768], replicated, may hold values from -0.21875 to 0.21875
- w_key: bfloat16 [768, 768], replicated, may hold values from -0.21875 to 0.21875
- w_value: bfloat16 [768, 768], replicated, may hold values from -0.21875 to 0.21875
- w_output: bfloat16 [768, 768], replicated, may hold values from -0.875 to 0.875
- rel_table: bfloat16 [12, 32], replicated, may hold values from -4 to 4
- norm_gain_two: float32 [768], replicated, may hold values from 0.5 to 1.5
- w_router: bfloat16 [768, 4], replicated, may hold values from -0.1796875 to 0.1796875
- w_expert_in: bfloat16 [4, 768, 3072], P('expert', ('ctx', 'dp')), may hold values from -0.21875 to 0.21875
- w_expert_out: bfloat16 [4, 3072, 768], P('expert', ('ctx', 'dp')), may hold values from -0.21875 to 0.21875
- segment_ids: int32 [8, 2048], P(('expert', 'dp'), 'ctx'), may hold values from 0 to 8, as said below
- routes: int32 [8, 2048, 2], P(('expert', 'dp'), 'ctx'), may hold values from 0 to 3, all different within a row
- priority: int32 [8, 4, 512], P(('expert', 'dp'), 'ctx'), may hold values from 0 to 511, each once within a row
Outputs:
- layer_output: bfloat16 [8, 2048, 768], P(('expert', 'dp'), 'ctx')
- grad_input: float32 [8, 2048, 768], P(('expert', 'dp'), 'ctx')
- grad_norm_one: float32 [768], replicated
- grad_query: float32 [768, 768], replicated
- grad_key: float32 [768, 768], replicated
- grad_value: float32 [768, 768], replicated
- grad_projection: float32 [768, 768], replicated
- grad_table: float32 [12, 32], replicated
- grad_norm_two: float32 [768], replicated
- grad_router: float32 [768, 4], replicated
- grad_expert_in: float32 [4, 768, 3072], P('expert', ('ctx', 'dp'))
- grad_expert_out: float32 [4, 3072, 768], P('expert', ('ctx', 'dp'))
Inputs may be any that keep to these rules, and one draw needn't show every extreme that they name: `segment_ids`: along each sequence the numbers never fall and each sequence ends with the number 8; in one sequence a single document runs from within its first 512 tokens to its end. `routes`: the two experts of a token differ. `priority`: within each block of 512 tokens the priorities are a permutation.
All inputs are finite; a program needn't handle non-finite values.
Results may differ from a plain program's by a relative error of at most 0.014.
Values may be sent and summed in bfloat16 or wider, within the bound.
A program may use at most 192 MiB of HBM per device.

v0:
```python
from functools import partial

import jax
import jax.numpy as jnp
from jax import lax
from jax.sharding import PartitionSpec as P

BUCKETS = 32


HIGH_PRECISION = lax.Precision.HIGHEST
EPSILON = 1e-06
NEGATIVE = -1e30
THRESHOLDS = (19, 21, 24, 27, 31, 35, 40, 46, 52, 59, 67, 77, 87, 99, 113)


def rms_norm(values, gain):
    return values * lax.rsqrt(jnp.mean(values * values, axis=-1, keepdims=True) + EPSILON) * gain


def buckets(distance):
    far = 16 + sum(((distance >= limit).astype(jnp.int32) for limit in THRESHOLDS))
    return jnp.where(distance < 16, jnp.maximum(distance, 0), far)


def bucket_onehot(query_places, key_places, dtype):
    index = buckets(query_places[:, None] - key_places[None, :])
    return (index[:, :, None] == jnp.arange(BUCKETS, dtype=jnp.int32)[None, None, :]).astype(dtype)


def slot_tables(chosen, order, capacity, experts):
    count = chosen.shape[0]
    ranks = jnp.stack([order, order + count], axis=1).reshape(-1)
    flat = chosen.reshape(-1)
    same = flat[:, None] == flat[None, :]
    before = ranks[None, :] < ranks[:, None]
    slots = jnp.sum((same & before).astype(jnp.int32), axis=1)
    targets = jnp.where(slots < capacity, flat * capacity + slots, experts * capacity)
    pair_sources = jnp.full((experts * capacity + 1,), 2 * count, jnp.int32)
    pair_sources = pair_sources.at[targets].set(jnp.arange(2 * count, dtype=jnp.int32))
    return (targets, pair_sources[: experts * capacity])


def route_gates(router_logits, chosen):
    chances = jax.nn.softmax(router_logits, axis=-1)
    picks = (
        chosen[:, :, None] == jnp.arange(router_logits.shape[-1], dtype=jnp.int32)[None, None, :]
    ).astype(jnp.float32)
    picked = jnp.sum(chances[:, None, :] * picks, axis=2)
    return picked / jnp.sum(picked, axis=1, keepdims=True)


def scores_for(
    query_heads, key_rows, query_places, key_places, query_segments, key_segments, table
):
    raw = jnp.einsum("qhd,khd->hqk", query_heads, key_rows, preferred_element_type=jnp.float32)
    onehot = bucket_onehot(query_places, key_places, table.dtype)
    bias = jnp.einsum("qkb,hb->hqk", onehot, table, preferred_element_type=jnp.float32)
    allowed = (key_places[None, :] <= query_places[:, None]) & (
        query_segments[:, None] == key_segments[None, :]
    )
    return jnp.where(allowed[None], raw * 0.125 + bias, NEGATIVE)


def table_part(score_cot, query_places, key_places):
    query_rows = score_cot.shape[1]
    piece = min(query_rows, 128)

    def one_piece(index):
        start = index * piece
        rows = lax.dynamic_slice_in_dim(score_cot, start, piece, 1)
        places = lax.dynamic_slice_in_dim(query_places, start, piece, 0)
        onehot = bucket_onehot(places, key_places, jnp.float32)
        return jnp.einsum("hqk,qkb->hb", rows, onehot, precision=HIGH_PRECISION)

    return jnp.sum(lax.map(one_piece, jnp.arange(query_rows // piece, dtype=jnp.int32)), axis=0)


def local(
    layer_input,
    cotangent,
    norm_gain_one,
    w_query,
    w_key,
    w_value,
    w_output,
    rel_table,
    norm_gain_two,
    w_router,
    w_expert_in,
    w_expert_out,
    segment_ids,
    routes,
    priority,
):
    inputs = layer_input[0].astype(jnp.float32)
    rows, width = inputs.shape
    heads = rel_table.shape[0]
    head_size = width // heads
    length = rows * lax.axis_size("ctx")
    experts = lax.axis_size("expert")
    capacity = min(rows, 5 * rows // (2 * experts))
    query_places = lax.axis_index("ctx") * rows + jnp.arange(rows, dtype=jnp.int32)
    key_places_all = jnp.arange(length, dtype=jnp.int32)
    query_segments = segment_ids[0]
    normed_input, norm_back = jax.vjp(rms_norm, inputs, norm_gain_one)
    normed_low = normed_input.astype(jnp.bfloat16)
    queries = jnp.dot(normed_low, w_query, preferred_element_type=jnp.float32).astype(jnp.bfloat16)
    keys = jnp.dot(normed_low, w_key, preferred_element_type=jnp.float32).astype(jnp.bfloat16)
    values = jnp.dot(normed_low, w_value, preferred_element_type=jnp.float32).astype(jnp.bfloat16)
    key_all, value_all, segment_all = (
        lax.all_gather(keys, "ctx", axis=0, tiled=True),
        lax.all_gather(values, "ctx", axis=0, tiled=True),
        lax.all_gather(query_segments, "ctx", axis=0, tiled=True),
    )
    query_heads = queries.reshape(rows, heads, head_size)
    key_heads = key_all.reshape(length, heads, head_size)
    value_heads = value_all.reshape(length, heads, head_size)
    key_block = min(length, 512)
    block_count = length // key_block
    block_indices = jnp.arange(block_count, dtype=jnp.int32)

    def block_inputs(index):
        start = index * key_block
        return (
            lax.dynamic_slice_in_dim(key_heads, start, key_block, 0),
            lax.dynamic_slice_in_dim(value_heads, start, key_block, 0),
            lax.dynamic_slice_in_dim(segment_all, start, key_block, 0),
            lax.dynamic_slice_in_dim(key_places_all, start, key_block, 0),
        )

    def block_scores(key_rows, key_segments, key_places):
        return scores_for(
            query_heads, key_rows, query_places, key_places, query_segments, key_segments, rel_table
        )

    def stats_step(carry, index):
        top, total = carry
        key_rows, value_rows, key_segments, key_places = block_inputs(index)
        scores = block_scores(key_rows, key_segments, key_places)
        new_top = jnp.maximum(top, jnp.max(scores, axis=2))
        total = total * jnp.exp(top - new_top) + jnp.sum(
            jnp.exp(scores - new_top[:, :, None]), axis=2
        )
        return ((new_top, total), None)

    start_top = jnp.full((heads, rows), NEGATIVE, jnp.float32)
    (top, total), _ = lax.scan(
        stats_step, (start_top, jnp.zeros((heads, rows), jnp.float32)), block_indices
    )

    def softmax_weights(scores):
        return jnp.exp(scores - top[:, :, None]) / total[:, :, None]

    def output_step(gathered, index):
        key_rows, value_rows, key_segments, key_places = block_inputs(index)
        weights_low = softmax_weights(block_scores(key_rows, key_segments, key_places)).astype(
            jnp.bfloat16
        )
        return (
            gathered
            + jnp.einsum(
                "hqk,khd->qhd", weights_low, value_rows, preferred_element_type=jnp.float32
            ),
            None,
        )

    attended, _ = lax.scan(
        output_step, jnp.zeros((rows, heads, head_size), jnp.float32), block_indices
    )
    mixed_output = attended.reshape(rows, width).astype(jnp.bfloat16)
    hidden = inputs + jnp.dot(mixed_output, w_output, preferred_element_type=jnp.float32)
    second_normed, norm_back_two = jax.vjp(rms_norm, hidden, norm_gain_two)
    normed_two_low = second_normed.astype(jnp.bfloat16)
    router_logits = jnp.dot(normed_two_low, w_router, preferred_element_type=jnp.float32)
    chosen = routes[0]
    gates, gate_back = jax.vjp(partial(route_gates, chosen=chosen), router_logits)
    targets, pair_sources = slot_tables(chosen, priority[0, 0], capacity, experts)
    token_sources = pair_sources // 2
    padded_rows = jnp.concatenate([normed_two_low, jnp.zeros((1, width), jnp.bfloat16)], axis=0)
    outgoing = padded_rows[token_sources].reshape(experts, capacity, width)
    arrived = lax.all_to_all(outgoing, "expert", split_axis=0, concat_axis=0, tiled=True)
    gathered_in, gathered_out = (
        lax.all_gather(w_expert_in, ("ctx", "dp"), axis=1, tiled=True),
        lax.all_gather(w_expert_out, ("ctx", "dp"), axis=1, tiled=True),
    )
    inner_weight = gathered_in[0]
    outer_weight = gathered_out[0]
    expert_rows = arrived.reshape(experts * capacity, width)
    pre = jnp.dot(expert_rows, inner_weight, preferred_element_type=jnp.float32)
    activated, gelu_back = jax.vjp(jax.nn.gelu, pre)
    activated_low = activated.astype(jnp.bfloat16)
    produced = jnp.dot(activated_low, outer_weight, preferred_element_type=jnp.float32).astype(
        jnp.bfloat16
    )
    returned = lax.all_to_all(
        produced.reshape(experts, capacity, width),
        "expert",
        split_axis=0,
        concat_axis=0,
        tiled=True,
    )
    padded_back = jnp.concatenate(
        [returned.reshape(experts * capacity, width), jnp.zeros((1, width), jnp.bfloat16)], axis=0
    )
    paired = padded_back[targets].reshape(rows, 2, width).astype(jnp.float32)
    layer_output = (hidden + jnp.sum(gates[:, :, None] * paired, axis=1)).astype(jnp.bfloat16)
    out_cot = cotangent[0].astype(jnp.float32)
    gate_cot = jnp.sum(out_cot[:, None, :] * paired, axis=2)
    pair_cot = (
        (gates[:, :, None] * out_cot[:, None, :]).astype(jnp.bfloat16).reshape(2 * rows, width)
    )
    pair_padded = jnp.concatenate([pair_cot, jnp.zeros((1, width), jnp.bfloat16)], axis=0)
    outgoing_cot = pair_padded[pair_sources].reshape(experts, capacity, width)
    arrived_cot = lax.all_to_all(
        outgoing_cot, "expert", split_axis=0, concat_axis=0, tiled=True
    ).reshape(experts * capacity, width)
    again_in, again_out = (
        lax.all_gather(w_expert_in, ("ctx", "dp"), axis=1, tiled=True),
        lax.all_gather(w_expert_out, ("ctx", "dp"), axis=1, tiled=True),
    )
    back_inner = again_in[0]
    back_outer = again_out[0]
    activated_cot = jnp.dot(arrived_cot, back_outer.T, preferred_element_type=jnp.float32)
    pre_cot = gelu_back(activated_cot)[0].astype(jnp.bfloat16)
    outer_grad = jnp.dot(activated_low.T, arrived_cot, preferred_element_type=jnp.float32)
    inner_grad = jnp.dot(expert_rows.T, pre_cot, preferred_element_type=jnp.float32)
    row_cot = jnp.dot(pre_cot, back_inner.T, preferred_element_type=jnp.float32).astype(
        jnp.bfloat16
    )
    back_rows = lax.all_to_all(
        row_cot.reshape(experts, capacity, width), "expert", split_axis=0, concat_axis=0, tiled=True
    )
    back_padded = jnp.concatenate(
        [back_rows.reshape(experts * capacity, width), jnp.zeros((1, width), jnp.bfloat16)], axis=0
    )
    token_cot = jnp.sum(back_padded[targets].reshape(rows, 2, width).astype(jnp.float32), axis=1)
    logit_cot = gate_back(gate_cot)[0]
    router_full = w_router.astype(jnp.float32)
    normed_two_cot = token_cot + jnp.dot(logit_cot, router_full.T, precision=HIGH_PRECISION)
    router_grad = jnp.dot(normed_two_low.astype(jnp.float32).T, logit_cot, precision=HIGH_PRECISION)
    hidden_part, gain_two_grad = norm_back_two(normed_two_cot)
    hidden_cot = out_cot + hidden_part
    hidden_cot_low = hidden_cot.astype(jnp.bfloat16)
    projection_grad = jnp.dot(mixed_output.T, hidden_cot_low, preferred_element_type=jnp.float32)
    mixed_cot = jnp.dot(hidden_cot_low, w_output.T, preferred_element_type=jnp.float32).astype(
        jnp.bfloat16
    )
    mixed_heads = mixed_cot.reshape(rows, heads, head_size)

    def delta_step(running, index):
        key_rows, value_rows, key_segments, key_places = block_inputs(index)
        weights_now = softmax_weights(block_scores(key_rows, key_segments, key_places))
        weight_cot = jnp.einsum(
            "qhd,khd->hqk", mixed_heads, value_rows, preferred_element_type=jnp.float32
        )
        return (running + jnp.sum(weights_now * weight_cot, axis=2), None)

    delta, _ = lax.scan(delta_step, jnp.zeros((heads, rows), jnp.float32), block_indices)
    start_carry = (
        jnp.zeros((rows, heads, head_size), jnp.float32),
        jnp.zeros((heads, BUCKETS), jnp.float32),
    )

    def grad_step(carry, index):
        query_sum, table_sum = carry
        key_rows, value_rows, key_segments, key_places = block_inputs(index)
        weights_now = softmax_weights(block_scores(key_rows, key_segments, key_places))
        weight_cot = jnp.einsum(
            "qhd,khd->hqk", mixed_heads, value_rows, preferred_element_type=jnp.float32
        )
        score_cot = weights_now * (weight_cot - delta[:, :, None])
        raw_cot = (0.125 * score_cot).astype(jnp.bfloat16)
        query_sum = query_sum + jnp.einsum(
            "hqk,khd->qhd", raw_cot, key_rows, preferred_element_type=jnp.float32
        )
        key_part = jnp.einsum(
            "hqk,qhd->khd", raw_cot, query_heads, preferred_element_type=jnp.float32
        )
        value_part = jnp.einsum(
            "hqk,qhd->khd",
            weights_now.astype(jnp.bfloat16),
            mixed_heads,
            preferred_element_type=jnp.float32,
        )
        table_sum = table_sum + table_part(score_cot, query_places, key_places)
        return ((query_sum, table_sum), (key_part, value_part))

    (query_sum, table_grad), (key_parts, value_parts) = lax.scan(
        grad_step, start_carry, block_indices
    )
    key_whole = key_parts.reshape(length, width)
    value_whole = value_parts.reshape(length, width)
    key_sum, value_sum = (
        lax.psum_scatter(key_whole, "ctx", scatter_dimension=0, tiled=True),
        lax.psum_scatter(value_whole, "ctx", scatter_dimension=0, tiled=True),
    )
    query_cot = query_sum.reshape(rows, width).astype(jnp.bfloat16)
    key_cot = key_sum.astype(jnp.bfloat16)
    value_cot = value_sum.astype(jnp.bfloat16)
    normed_cot = jnp.dot(query_cot, w_query.T, preferred_element_type=jnp.float32)
    normed_cot = normed_cot + jnp.dot(key_cot, w_key.T, preferred_element_type=jnp.float32)
    normed_cot = normed_cot + jnp.dot(value_cot, w_value.T, preferred_element_type=jnp.float32)
    query_grad = jnp.dot(normed_low.T, query_cot, preferred_element_type=jnp.float32)
    key_grad = jnp.dot(normed_low.T, key_cot, preferred_element_type=jnp.float32)
    value_grad = jnp.dot(normed_low.T, value_cot, preferred_element_type=jnp.float32)
    input_part, gain_one_grad = norm_back(normed_cot)
    input_grad = hidden_cot + input_part
    summed = lax.psum(
        (
            gain_one_grad,
            query_grad,
            key_grad,
            value_grad,
            projection_grad,
            table_grad,
            gain_two_grad,
            router_grad,
        ),
        ("expert", "ctx", "dp"),
    )
    expert_in_grad, expert_out_grad = (
        lax.psum_scatter(inner_grad[None], ("ctx", "dp"), scatter_dimension=1, tiled=True),
        lax.psum_scatter(outer_grad[None], ("ctx", "dp"), scatter_dimension=1, tiled=True),
    )
    return (
        layer_output[None],
        input_grad[None],
        summed[0],
        summed[1],
        summed[2],
        summed[3],
        summed[4],
        summed[5],
        summed[6],
        summed[7],
        expert_in_grad,
        expert_out_grad,
    )


def solution(mesh):
    placed = (
        P(("expert", "dp"), "ctx", None),
        P(("expert", "dp"), "ctx", None),
        P(),
        P(),
        P(),
        P(),
        P(),
        P(),
        P(),
        P(),
        P("expert", ("ctx", "dp"), None),
        P("expert", ("ctx", "dp"), None),
        P(("expert", "dp"), "ctx"),
        P(("expert", "dp"), "ctx", None),
        P(("expert", "dp"), "ctx", None),
    )
    return jax.shard_map(
        local,
        mesh=mesh,
        in_specs=placed,
        out_specs=(
            P(("expert", "dp"), "ctx", None),
            P(("expert", "dp"), "ctx", None),
            P(),
            P(),
            P(),
            P(),
            P(),
            P(),
            P(),
            P(),
            P("expert", ("ctx", "dp"), None),
            P("expert", ("ctx", "dp"), None),
        ),
        check_vma=False,
    )
```

profile of v0, /device:TPU:0, one launch (start us, length us, event | category | flops | bytes accessed | tf_op | source)
XLA Modules:
  0.0 2283.0 jit_solution(2355749674256636751)
XLA Ops:
  15.5 13.7 all-gather
  51.3 27.1 %all-gather.8.cloned.1.call-done = bf16[2048,768]{1,0:T(8,128)(2,1)} async-done(((bf16[512,768]{1,0:T(8,128)(2,1)}), bf16[2048,768]{1,0:T(8,128)(2,1)}) %all-gather.8.cloned.1.call-update) | async-done | bytes 3145744 | tf_op jit(solution)/shard_map/all_gather | solution.py:112
  83.2 170.3 %while.63 = (s32[]{:T(128)}, f32[12,512]{1,0:T(8,128)S(1)}, f32[12,512]{1,0:T(8,128)S(1)}, s32[4]{0:T(128)S(1)}, s32[2048]{0:T(1024)S(1)}, /*index=5*/s32[1,512]...) while((s32[]{:T(128)}, f32[12,512]{1,0:T(8,128)S(1)}, ...), condition=%wide.region_4.5_spmd.clone, body=%wide.region_1.4_spmd.clone.sunk | while | flops 644905472 | bytes 82131944 | solution.py:148
  99.6 17.8 copy.171
  142.1 17.9 copy.171
  184.8 17.8 copy.171
  227.3 17.8 copy.171
  258.2 184.0 %while.64 = (s32[]{:T(128)}, f32[512,12,64]{0,2,1:T(8,128)}, s32[4]{0:T(128)S(1)}, bf16[2048,12,64]{0,2,1:T(8,128)(2,1)}, s32[2048]{0:T(1024)S(1)}, /*index=5*/s...) while((s32[]{:T(128)}, f32[512,12,64]{0,2,1:T(8,128)}, ...), condition=%wide.region_6.7_spmd.clone, body=%wide.region_5.6_spmd.clone.sunk | while | flops 1048314368 | bytes 60629492 | solution.py:168
  274.8 17.8 copy.173
  320.4 17.8 copy.173
  338.2 12.0 bitcast_add_fusion.8
  366.5 17.8 copy.173
  384.3 12.0 bitcast_add_fusion.8
  412.5 17.8 copy.173
  430.3 12.0 bitcast_add_fusion.8
  469.3 12.7 all-to-all-done
  486.4 12.2 fusion.98
  498.6 14.8 fusion.103
  518.1 18.4 fusion.92
  611.2 206.1 %while.65 = (s32[]{:T(128)}, f32[12,512]{1,0:T(8,128)S(1)}, s32[4]{0:T(128)S(1)}, s32[2048]{0:T(1024)S(1)}, s32[1,512]{1,0:T(1,128)S(1)}, /*index=5*/s32[2048]{0...) while((s32[]{:T(128)}, f32[12,512]{1,0:T(8,128)S(1)}, ...), condition=%wide.region_23.24_spmd.clone, body=%wide.region_21.23_spmd.clone.sunk | while | flops 1050679808 | bytes 87727136 | solution.py:259
  634.6 17.6 copy.175
  686.0 17.6 copy.175
  737.5 17.6 copy.175
  788.9 17.6 copy.175
  817.4 682.2 %while.67 = (s32[]{:T(128)}, f32[512,12,64]{0,2,1:T(8,128)}, f32[12,32]{1,0:T(8,128)S(1)}, f32[4,512,12,64]{1,0,3,2:T(4,128)}, f32[4,512,12,64]{1,0,3,2:T(4,128)...) while((s32[]{:T(128)}, f32[512,12,64]{0,2,1:T(8,128)}, ...), condition=%wide.region_28.29_spmd.clone, body=%wide.region_24.28_spmd.clone.sunk | while | flops 2582448640 | bytes 221633456 | solution.py:289
  833.9 17.7 copy.177
  872.4 36.8 %while.68 = (s32[]{:T(128)}, f32[4,12,32]{2,1,0:T(8,128)S(1)}, s32[4]{0:T(128)S(1)}, f32[12,512,512]{1,2,0:T(8,128)}, s32[512]{0:T(512)S(1)}, /*index=5*/s32[512...) while((s32[]{:T(128)}, f32[4,12,32]{2,1,0:T(8,128)S(1)}, s32[4]{0:T(128)S(1)}, ...), condition=%wide.region_26.26_spmd, body=%wide.region_25.25_spmd.sunk | while | flops 307298304 | bytes 9973427 | solution.py:76
  925.6 31.0 %dynamic_update_slice.17 = f32[4,512,12,64]{1,0,3,2:T(4,128)} dynamic-update-slice(f32[4,512,12,64]{1,0,3,2:T(4,128)} %get-tuple-element.1390, f32[1,512,12,64]{1,0,3,2:T(1,128)} %copy.178, s32[]{:T(128)S(6)} %copy.216, s32[]{:T(128)} %constant.198.clone.1..sunk.3, s32[]{:T(128)} %constant.198.clone.1..sunk.3, s32[]{:T(128)} %constant.198.clone.1..sunk.3) | dynamic-update-slice | bytes 3145732 | tf_op jit(solution)/shard_map/while/body/jit(dynamic_update_index_in_dim)/dynamic_update_slice | solution.py:289
  956.6 31.0 %dynamic_update_slice.18 = f32[4,512,12,64]{1,0,3,2:T(4,128)} dynamic-update-slice(f32[4,512,12,64]{1,0,3,2:T(4,128)} %get-tuple-element.1391, f32[1,512,12,64]{1,0,3,2:T(1,128)} %copy.179, s32[]{:T(128)S(6)} %copy.216, s32[]{:T(128)} %constant.198.clone.1..sunk.3, s32[]{:T(128)} %constant.198.clone.1..sunk.3, s32[]{:T(128)} %constant.198.clone.1..sunk.3) | dynamic-update-slice | bytes 3145732 | tf_op jit(solution)/shard_map/while/body/jit(dynamic_update_index_in_dim)/dynamic_update_slice | solution.py:289
  1003.9 17.7 copy.177
  1042.4 36.8 %while.68 = (s32[]{:T(128)}, f32[4,12,32]{2,1,0:T(8,128)S(1)}, s32[4]{0:T(128)S(1)}, f32[12,512,512]{1,2,0:T(8,128)}, s32[512]{0:T(512)S(1)}, /*index=5*/s32[512...) while((s32[]{:T(128)}, f32[4,12,32]{2,1,0:T(8,128)S(1)}, s32[4]{0:T(128)S(1)}, ...), condition=%wide.region_26.26_spmd, body=%wide.region_25.25_spmd.sunk | while | flops 307298304 | bytes 9973427 | solution.py:76
  1096.1 31.0 %dynamic_update_slice.17 = f32[4,512,12,64]{1,0,3,2:T(4,128)} dynamic-update-slice(f32[4,512,12,64]{1,0,3,2:T(4,128)} %get-tuple-element.1390, f32[1,512,12,64]{1,0,3,2:T(1,128)} %copy.178, s32[]{:T(128)S(6)} %copy.216, s32[]{:T(128)} %constant.198.clone.1..sunk.3, s32[]{:T(128)} %constant.198.clone.1..sunk.3, s32[]{:T(128)} %constant.198.clone.1..sunk.3) | dynamic-update-slice | bytes 3145732 | tf_op jit(solution)/shard_map/while/body/jit(dynamic_update_index_in_dim)/dynamic_update_slice | solution.py:289
  1127.1 31.0 %dynamic_update_slice.18 = f32[4,512,12,64]{1,0,3,2:T(4,128)} dynamic-update-slice(f32[4,512,12,64]{1,0,3,2:T(4,128)} %get-tuple-element.1391, f32[1,512,12,64]{1,0,3,2:T(1,128)} %copy.179, s32[]{:T(128)S(6)} %copy.216, s32[]{:T(128)} %constant.198.clone.1..sunk.3, s32[]{:T(128)} %constant.198.clone.1..sunk.3, s32[]{:T(128)} %constant.198.clone.1..sunk.3) | dynamic-update-slice | bytes 3145732 | tf_op jit(solution)/shard_map/while/body/jit(dynamic_update_index_in_dim)/dynamic_update_slice | solution.py:289
  1174.5 17.7 copy.177
  1213.0 36.8 %while.68 = (s32[]{:T(128)}, f32[4,12,32]{2,1,0:T(8,128)S(1)}, s32[4]{0:T(128)S(1)}, f32[12,512,512]{1,2,0:T(8,128)}, s32[512]{0:T(512)S(1)}, /*index=5*/s32[512...) while((s32[]{:T(128)}, f32[4,12,32]{2,1,0:T(8,128)S(1)}, s32[4]{0:T(128)S(1)}, ...), condition=%wide.region_26.26_spmd, body=%wide.region_25.25_spmd.sunk | while | flops 307298304 | bytes 9973427 | solution.py:76
  1266.6 31.0 %dynamic_update_slice.17 = f32[4,512,12,64]{1,0,3,2:T(4,128)} dynamic-update-slice(f32[4,512,12,64]{1,0,3,2:T(4,128)} %get-tuple-element.1390, f32[1,512,12,64]{1,0,3,2:T(1,128)} %copy.178, s32[]{:T(128)S(6)} %copy.216, s32[]{:T(128)} %constant.198.clone.1..sunk.3, s32[]{:T(128)} %constant.198.clone.1..sunk.3, s32[]{:T(128)} %constant.198.clone.1..sunk.3) | dynamic-update-slice | bytes 3145732 | tf_op jit(solution)/shard_map/while/body/jit(dynamic_update_index_in_dim)/dynamic_update_slice | solution.py:289
  1297.6 31.0 %dynamic_update_slice.18 = f32[4,512,12,64]{1,0,3,2:T(4,128)} dynamic-update-slice(f32[4,512,12,64]{1,0,3,2:T(4,128)} %get-tuple-element.1391, f32[1,512,12,64]{1,0,3,2:T(1,128)} %copy.179, s32[]{:T(128)S(6)} %copy.216, s32[]{:T(128)} %constant.198.clone.1..sunk.3, s32[]{:T(128)} %constant.198.clone.1..sunk.3, s32[]{:T(128)} %constant.198.clone.1..sunk.3) | dynamic-update-slice | bytes 3145732 | tf_op jit(solution)/shard_map/while/body/jit(dynamic_update_index_in_dim)/dynamic_update_slice | solution.py:289
  1345.0 17.7 copy.177
  1383.5 36.8 %while.68 = (s32[]{:T(128)}, f32[4,12,32]{2,1,0:T(8,128)S(1)}, s32[4]{0:T(128)S(1)}, f32[12,512,512]{1,2,0:T(8,128)}, s32[512]{0:T(512)S(1)}, /*index=5*/s32[512...) while((s32[]{:T(128)}, f32[4,12,32]{2,1,0:T(8,128)S(1)}, s32[4]{0:T(128)S(1)}, ...), condition=%wide.region_26.26_spmd, body=%wide.region_25.25_spmd.sunk | while | flops 307298304 | bytes 9973427 | solution.py:76
  1437.1 31.0 %dynamic_update_slice.17 = f32[4,512,12,64]{1,0,3,2:T(4,128)} dynamic-update-slice(f32[4,512,12,64]{1,0,3,2:T(4,128)} %get-tuple-element.1390, f32[1,512,12,64]{1,0,3,2:T(1,128)} %copy.178, s32[]{:T(128)S(6)} %copy.216, s32[]{:T(128)} %constant.198.clone.1..sunk.3, s32[]{:T(128)} %constant.198.clone.1..sunk.3, s32[]{:T(128)} %constant.198.clone.1..sunk.3) | dynamic-update-slice | bytes 3145732 | tf_op jit(solution)/shard_map/while/body/jit(dynamic_update_index_in_dim)/dynamic_update_slice | solution.py:289
  1468.2 31.0 %dynamic_update_slice.18 = f32[4,512,12,64]{1,0,3,2:T(4,128)} dynamic-update-slice(f32[4,512,12,64]{1,0,3,2:T(4,128)} %get-tuple-element.1391, f32[1,512,12,64]{1,0,3,2:T(1,128)} %copy.179, s32[]{:T(128)S(6)} %copy.216, s32[]{:T(128)} %constant.198.clone.1..sunk.3, s32[]{:T(128)} %constant.198.clone.1..sunk.3, s32[]{:T(128)} %constant.198.clone.1..sunk.3) | dynamic-update-slice | bytes 3145732 | tf_op jit(solution)/shard_map/while/body/jit(dynamic_update_index_in_dim)/dynamic_update_slice | solution.py:289
  1523.6 94.4 %reduce-scatter.7.cloned.1.call-done = f32[512,768]{0,1:T(8,128)} async-done(((f32[2048,768]{0,1:T(8,128)}), f32[512,768]{0,1:T(8,128)}) %reduce-scatter.7.cloned.1.call-update) | async-done | bytes 1572880 | tf_op jit(solution)/shard_map/reduce_scatter | solution.py:296
  1621.8 109.7 %reduce-scatter.5.cloned.1.call-done = f32[512,768]{0,1:T(8,128)} async-done(((f32[2048,768]{0,1:T(8,128)}), f32[512,768]{0,1:T(8,128)}) %reduce-scatter.5.cloned.1.call-update) | async-done | bytes 1572880 | tf_op jit(solution)/shard_map/reduce_scatter | solution.py:295
  1747.1 14.6 convolution_bitcast_fusion
  1770.8 42.2 %all-reduce.4 = (f32[768]{0:T(1024)}, f32[12,32]{1,0:T(8,128)}, f32[768]{0:T(1024)}, f32[768,4]{0,1:T(4,128)}) all-reduce(f32[768]{0:T(1024)} %get-tuple-element.634, f32[12,32]{1,0:T(8,128)S(1)} %copy-done.41, f32[768]{0:T(1024)} %get-tuple-element.630, ...), channel_id=1, replica_groups=mesh['expert'=4,'ctx'=4,'dp'=2] {'expert','ctx','dp'}, use_global_device_ids=true, to_apply=%region_33.34 | all-reduce | flops 4992 | bytes 39936 | tf_op jit(solution)/shard_map/psum | solution.py:309
  1816.7 114.7 %all-reduce.8.cloned.1.call-done = (f32[768,768]{1,0:T(8,128)}, f32[768,768]{1,0:T(8,128)}, f32[768,768]{1,0:T(8,128)}, f32[768,768]{1,0:T(8,128)}) async-done(((f32[768,768]{1,0:T(8,128)}, f32[768,768]{1,0:T(8,128)}, f32[768,768]{1,0:T(8,128)}, f32[768,768]{1,0:T(8,128)}), (f32[768,768]{1,0:T(8,128)}, f32[768,768]{1,0:T(8,128)}, f32[768,768]{1,0:T(8,128)}, ...) | async-done | bytes 9437200 | tf_op jit(solution)/shard_map/psum | solution.py:309
  1931.4 168.1 %reduce-scatter.9.cloned.1.call-done = f32[1,96,3072]{2,1,0:T(8,128)} async-done(((f32[1,768,3072]{2,1,0:T(8,128)}), f32[1,96,3072]{2,1,0:T(8,128)}) %reduce-scatter.9.cloned.1.call-update) | async-done | bytes 1179664 | tf_op jit(solution)/shard_map/reduce_scatter | solution.py:323
  2099.4 167.2 %reduce-scatter.11.cloned.1.call-done = f32[1,384,768]{2,1,0:T(8,128)} async-done(((f32[1,3072,768]{2,1,0:T(8,128)}), f32[1,384,768]{2,1,0:T(8,128)}) %reduce-scatter.11.cloned.1.call-update) | async-done | bytes 1179664 | tf_op jit(solution)/shard_map/reduce_scatter | solution.py:324
  (573 shorter events, 867.5 us)
Async XLA Ops:
  7.2 5.0 copy-start
  7.2 5.0 copy-start.5
  7.2 4.9 copy-start.46
  7.2 71.2 %all-gather.8.cloned.1.call-start = ((), (), s32[]{:S(2)}) async-start(), calls=%async_computation.9 | async-start | bytes 3932160 | tf_op jit(solution)/shard_map/all_gather | solution.py:112
  8.8 5.1 copy-start.63
  8.8 26.7 %copy-start.49 = (f32[512]{0:T(512)}, f32[512]{0:T(512)S(1)}, u32[]{:S(2)}) copy-start(f32[512]{0:T(512)S(1)} %fusion.142) | copy-start | bytes 6148
  12.1 241.4 %all-gather.6.cloned.1.call-start = ((), (), s32[]{:S(2)}) async-start(), calls=%async_computation.8 | async-start | bytes 3932160 | tf_op jit(solution)/shard_map/all_gather | solution.py:113
  13.9 472.5 %all-gather.10.cloned.1.call-start = ((), (), s32[]{:S(2)}) async-start(), calls=%async_computation.10 | async-start | bytes 5308416 | tf_op jit(solution)/shard_map/all_gather | solution.py:184
  14.6 484.0 %all-gather.12.cloned.1.call-start = ((), (), s32[]{:S(2)}) async-start(), calls=%async_computation.11 | async-start | bytes 5308416 | tf_op jit(solution)/shard_map/all_gather | solution.py:185
  51.3 31.9 %copy-start.30 = (bf16[12,32]{1,0:T(8,128)(2,1)S(1)}, bf16[12,32]{1,0:T(8,128)(2,1)}, u32[]{:S(2)}) copy-start(bf16[12,32]{1,0:T(8,128)(2,1)} %param.32) | copy-start | bytes 2308
  258.2 185.6 %copy-start.6 = (bf16[1,512,768]{2,1,0:T(8,128)(2,1)S(1)}, bf16[1,512,768]{2,1,0:T(8,128)(2,1)}, u32[]{:S(2)}) copy-start(bf16[1,512,768]{2,1,0:T(8,128)(2,1)} %param.25) | copy-start | bytes 2359300
  442.3 5.3 copy-start.56
  447.7 9.9 copy-start.14
  452.8 4.8 copy-start.65
  452.8 4.8 copy-start.61
  452.8 5.3 copy-start.54
  452.8 29.1 %all-to-all-start = ((bf16[4,320,768]{2,1,0:T(8,128)(2,1)}), bf16[4,320,768]{2,1,0:T(8,128)(2,1)}, u32[]{:S(2)}, u32[]{:S(2)}) async-start(bf16[4,320,768]{2,1,0:T(8,128)(2,1)} %bitcast.298), calls=%async_computation | async-start | bytes 3932160 | tf_op jit(solution)/shard_map/all_to_all | solution.py:182
  458.0 143.6 %copy-start.37 = (f32[512,4]{0,1:T(4,128)}, f32[512,4]{0,1:T(4,128)S(1)}, u32[]{:S(2)}) copy-start(f32[512,4]{0,1:T(4,128)S(1)} %get-tuple-element.779) | copy-start | bytes 24580
  458.0 143.6 %copy-start.52 = (f32[512]{0:T(512)}, f32[512]{0:T(512)S(1)}, u32[]{:S(2)}) copy-start(f32[512]{0:T(512)S(1)} %get-tuple-element.778) | copy-start | bytes 6148
  458.1 143.5 %copy-start.55 = (f32[512]{0:T(512)}, f32[512]{0:T(512)S(1)}, u32[]{:S(2)}) copy-start(f32[512]{0:T(512)S(1)} %fusion.144) | copy-start | bytes 6148
  482.0 31.4 %all-to-all-start.2 = ((bf16[4,320,768]{2,1,0:T(8,128)(2,1)}), bf16[4,320,768]{2,1,0:T(8,128)(2,1)}, u32[]{:S(2)}, u32[]{:S(2)}) async-start(bf16[4,320,768]{2,1,0:T(8,128)(2,1)} %bitcast.299), calls=%async_computation.2 | async-start | bytes 3932160 | tf_op jit(solution)/shard_map/all_to_all | solution.py:215
  513.4 36.0 %all-to-all-start.1 = ((bf16[4,320,768]{2,1,0:T(8,128)(2,1)}), bf16[4,320,768]{2,1,0:T(8,128)(2,1)}, u32[]{:S(2)}, u32[]{:S(2)}) async-start(bf16[4,320,768]{2,1,0:T(8,128)(2,1)} %bitcast.307), calls=%async_computation.1 | async-start | bytes 3932160 | tf_op jit(solution)/shard_map/all_to_all | solution.py:196
  549.4 30.0 %all-to-all-start.3 = ((bf16[4,320,768]{2,1,0:T(8,128)(2,1)}), bf16[4,320,768]{2,1,0:T(8,128)(2,1)}, u32[]{:S(2)}, u32[]{:S(2)}) async-start(bf16[4,320,768]{2,1,0:T(8,128)(2,1)} %bitcast.306), calls=%async_computation.3 | async-start | bytes 3932160 | tf_op jit(solution)/shard_map/all_to_all | solution.py:231
  553.9 1064.2 %reduce-scatter.7.cloned.1.call-start = ((), (), s32[]{:S(2)}) async-start(), calls=%async_computation.13 | async-start | bytes 7864320 | tf_op jit(solution)/shard_map/reduce_scatter | solution.py:296
  579.3 22.2 copy-start.44
  579.4 22.2 copy-start.62
  594.8 6.8 copy-start.57
  594.8 6.8 copy-start.60
  611.2 206.1 %copy-start.39 = (f32[12,32]{1,0:T(8,128)S(1)}, f32[12,32]{1,0:T(8,128)}, u32[]{:S(2)}) copy-start(f32[12,32]{1,0:T(8,128)} %custom-call.5) | copy-start | bytes 4612
  618.6 7.6 copy-start.2
  670.0 7.6 copy-start.2
  721.4 7.6 copy-start.2
  772.9 7.6 copy-start.2
  861.9 7.7 copy-start.3
  909.2 9.0 copy-start.1
  1032.0 7.7 copy-start.3
  1079.3 9.4 copy-start.1
  1202.5 7.7 copy-start.3
  1249.8 9.4 copy-start.1
  1373.1 7.7 copy-start.3
  1420.4 9.4 copy-start.1
  1499.6 8.5 copy-start.40
  1508.1 223.4 %reduce-scatter.5.cloned.1.call-start = ((), (), s32[]{:S(2)}) async-start(), calls=%async_computation.12 | async-start | bytes 7864320 | tf_op jit(solution)/shard_map/reduce_scatter | solution.py:295
  1516.6 414.7 %all-reduce.8.cloned.1.call-start = ((), (), s32[]{:S(2)}) async-start(), calls=%async_computation.16 | async-start | bytes 18874368 | tf_op jit(solution)/shard_map/psum | solution.py:309
  1735.3 364.1 %reduce-scatter.9.cloned.1.call-start = ((), (), s32[]{:S(2)}) async-start(), calls=%async_computation.14 | async-start | bytes 10616832 | tf_op jit(solution)/shard_map/reduce_scatter | solution.py:323
  1747.1 519.6 %reduce-scatter.11.cloned.1.call-start = ((), (), s32[]{:S(2)}) async-start(), calls=%async_computation.15 | async-start | bytes 10616832 | tf_op jit(solution)/shard_map/reduce_scatter | solution.py:324
  1767.8 45.8 %copy-start.10 = (f32[512,768]{1,0:T(8,128)S(1)}, f32[512,768]{1,0:T(8,128)}, u32[]{:S(2)}) copy-start(f32[512,768]{1,0:T(8,128)} %copy-done.8) | copy-start | bytes 4718596
  1931.3 338.5 %copy-start.29 = (f32[768,768]{1,0:T(8,128)S(1)}, f32[768,768]{1,0:T(8,128)}, u32[]{:S(2)}) copy-start(f32[768,768]{1,0:T(8,128)} %get-tuple-element.1445) | copy-start | bytes 7077892
  (45 other events, 133.4 us)
Sparse Core Ops, SparseCore 0:
  12.2 66.2 all-gather.7
  80.6 62.1 all-gather.5
  144.9 78.5 all-gather.9
  225.5 78.0 all-gather.11
  1508.2 109.7 reduce-scatter.6
  1620.2 111.2 reduce-scatter.4
  1738.3 193.0 all-reduce.7
  1935.9 163.4 reduce-scatter.8
  2104.0 162.5 reduce-scatter.10
where the time goes:
time: 2300 us; the launch traced here: 2280 us
  local copies, waits for them, and re-layouts  771 us (34%)
  waiting for transfers between devices  695 us (30%)
  matrix products  611 us (27%)
  other arithmetic  93.5 us (4%)
  blocking collectives  55.8 us (2%)
  loops' own time  23 us (1%)
    dot_general x16, local copies, waits for them, and re-layouts, scores_for(): jnp.einsum('qkb,hb->hqk', onehot, table, preferred_element_type=jnp.float32)  283 us
    dynamic_update_slice x16, local copies, waits for them, and re-layouts, local(): lax.scan(grad_step, start_carry, block_indices)  276 us
    reduce_scatter x1, waiting for transfers between devices, local(): lax.psum_scatter(inner_grad[None], ('ctx', 'dp'), scatter_dimension=1, ti...  168 us
    reduce_scatter x1, waiting for transfers between devices, local(): lax.psum_scatter(outer_grad[None], ('ctx', 'dp'), scatter_dimension=1, ti...  167 us
    dot_general x16, matrix products, scores_for(): jnp.einsum('qkb,hb->hqk', onehot, table, preferred_element_type=jnp.float32)  147 us
    psum x1, waiting for transfers between devices, local(): lax.psum((gain_one_grad, query_grad, key_grad, value_grad, projection_gra...  115 us
    reduce_scatter x1, waiting for transfers between devices, local(): lax.psum_scatter(key_whole, 'ctx', scatter_dimension=0, tiled=True)  110 us
    reduce_scatter x1, waiting for transfers between devices, local(): lax.psum_scatter(value_whole, 'ctx', scatter_dimension=0, tiled=True)  94.4 us
  transfers between devices with their start and end apart: 13, of which 7 were waited for; matrix products, arithmetic and copies ran while one was open for 24% of the time, Pallas kernels for 0%

commit v1 on v0

v1 whole, which is shorter than its diff:
```python
import functools
from functools import partial

import jax
import jax.numpy as jnp
from jax import lax
from jax.experimental import pallas as pl
from jax.experimental.pallas import tpu as pltpu
from jax.sharding import PartitionSpec as P

bf16 = jnp.bfloat16
f32 = jnp.float32
HIGH_PRECISION = lax.Precision.HIGHEST
EPSILON = 1e-06
THRESHOLDS = (19, 21, 24, 27, 31, 35, 40, 46, 52, 59, 67, 77, 87, 99, 113)
BUCKETS=32
NEG=-1e30
BLK=256
NT=(((1,),(1,)),((),()))
TN=(((0,),(0,)),((),()))

def dot(a,b,dims=(((1,),(0,)),((),()))):
    return lax.dot_general(a,b,dims,preferred_element_type=f32)

def seg_mask_rows(seg):
    which = lax.broadcasted_iota(jnp.int32, seg.shape, 0).astype(f32)
    same = seg.astype(f32) == which
    return jnp.where(same, 0.0, NEG).astype(bf16), jnp.where(same, 1.0, 0.0).astype(bf16)

def attn_fwd_kernel(heads, n, rows, x_ref, f_ref, o_ref, of_ref, lse_ref, qa, ka, vn, bias, s_ref):
    size = 64
    group = heads*size
    length = n*rows
    def head(h, carry):
        base = pl.multiple_of(h*size, size)
        for s in range(n):
            at = slice(s*rows, (s+1)*rows)
            q = x_ref[s, pl.ds(base, size), :]
            k = x_ref[s, pl.ds(base+group, size), :]
            v = x_ref[s, pl.ds(base+2*group, size), :]
            seg = x_ref[s, 3*group:3*group+16, :]
            mask, hot = seg_mask_rows(seg)
            zeros = jnp.zeros((48, rows), bf16)
            qt = jnp.concatenate([q*jnp.asarray(0.125,bf16), mask, zeros], axis=0)
            qa[at, :] = qt.T
            ka[:, at] = jnp.concatenate([k, hot, zeros], axis=0)
            vn[at, :] = jnp.concatenate([v, jnp.zeros((64,rows),bf16)], axis=0).T
        line = jnp.broadcast_to(f_ref[pl.ds(h,1), :], (BLK, 2*BLK))
        rolled = pltpu.roll(line, 0, 1, stride=1, stride_axis=0)
        r = lax.broadcasted_iota(jnp.int32, (BLK,2*BLK), 0)
        c = lax.broadcasted_iota(jnp.int32, (BLK,2*BLK), 1)
        bias[...] = jnp.where(c - r > BLK, NEG, rolled)
        for t in range(length//BLK):
            qt = qa[t*BLK:(t+1)*BLK, :]
            near0 = max(t-1,0)*BLK
            end = (t+1)*BLK
            chunks = [(near0, end)] + [(a, min(a+2*BLK, near0)) for a in range(0, near0, 2*BLK)]
            top = None
            for (a,b) in chunks:
                s = dot(qt, ka[:, a:b])
                if a == near0:
                    s = s + bias[:, 2*BLK-(b-a):]
                s_ref[:, a:b] = s
                part = s[:, :128]
                for i in range(1,(b-a)//128):
                    part = jnp.maximum(part, s[:, i*128:(i+1)*128])
                top = part if top is None else jnp.maximum(top, part)
            m = jnp.max(top, axis=1, keepdims=True)
            total = None; o = None
            for (a,b) in chunks:
                p = jnp.exp(s_ref[:, a:b] - m)
                part = p[:, :128]
                for i in range(1,(b-a)//128):
                    part = part + p[:, i*128:(i+1)*128]
                total = part if total is None else total + part
                u = dot(p.astype(bf16), vn[a:b, :])
                o = u if o is None else o + u
            l = jnp.sum(total, axis=1, keepdims=True)
            o = o / l
            lane = lax.broadcasted_iota(jnp.int32, (BLK,128), 1)
            o = jnp.where(lane == 64, m + jnp.log(l), o)
            ot = o.T
            src, off = (t*BLK)//rows, (t*BLK)%rows
            o_ref[src, pl.ds(base,size), off:off+BLK] = ot[:size].astype(bf16)
            of_ref[pl.ds(base,size), t*BLK:(t+1)*BLK] = ot[:size]
            lse_ref[pl.ds(h,1), t*BLK:(t+1)*BLK] = ot[size:size+1]
        return carry
    lax.fori_loop(0, heads, head, 0)

def attn_fwd(x, f):
    n, depth, rows = x.shape
    heads = f.shape[0]
    length = n*rows
    return pl.pallas_call(functools.partial(attn_fwd_kernel, heads, n, rows),
        out_shape=[jax.ShapeDtypeStruct((n, heads*64, rows), bf16), jax.ShapeDtypeStruct((heads*64,length), f32), jax.ShapeDtypeStruct((heads,length), f32)],
        in_specs=[pl.BlockSpec(memory_space=pltpu.VMEM)]*2,
        out_specs=[pl.BlockSpec(memory_space=pltpu.VMEM)]*3,
        scratch_shapes=[pltpu.VMEM((length,128),bf16), pltpu.VMEM((128,length),bf16), pltpu.VMEM((length,128),bf16), pltpu.VMEM((BLK,2*BLK),f32), pltpu.VMEM((BLK,length),f32)],
        compiler_params=pltpu.CompilerParams(vmem_limit_bytes=48*1024*1024),
        name="attention_forward",
    )(x, f)

def split3(v):
    hi = v.astype(bf16); rest = v - hi.astype(f32)
    mid = rest.astype(bf16); rest = rest - mid.astype(f32)
    return hi, mid, rest.astype(bf16)

def attn_bwd_kernel(heads, n, rows, x_ref, do_ref, f_ref, of_ref, lse_ref, g_ref, diag_ref, qa, ka, va, da, qn, dn, bias, dq, gsum):
    size = 64
    group = heads*size
    length = n*rows
    def head(h, carry):
        base = pl.multiple_of(h*size, size)
        for s in range(n):
            at = slice(s*rows, (s+1)*rows)
            q = x_ref[s, pl.ds(base, size), :] * jnp.asarray(0.125,bf16)
            k = x_ref[s, pl.ds(base+group, size), :]
            v = x_ref[s, pl.ds(base+2*group, size), :]
            d = do_ref[s, pl.ds(base, size), :]
            seg = x_ref[s, 3*group:3*group+16, :]
            mask, hot = seg_mask_rows(seg)
            which = lax.broadcasted_iota(jnp.int32, (16, rows), 0)
            def rows3(vec):
                hi, mid, lo = split3(jnp.broadcast_to(vec, (16,rows)))
                return jnp.where(which==0, hi, jnp.where(which==1, mid, jnp.where(which==2, lo, jnp.zeros((),bf16))))
            ones = jnp.where(which<3, 1.0, 0.0).astype(bf16)
            zeros = jnp.zeros((32, rows), bf16)
            zeros48 = jnp.zeros((48, rows), bf16)
            lse = lse_ref[pl.ds(h,1), at]
            delta = jnp.sum(of_ref[pl.ds(base,size), at]*d.astype(f32), axis=0, keepdims=True)
            qt = jnp.concatenate([q, mask, rows3(-lse), zeros], axis=0)
            qa[:, at] = qt
            qn[at, :] = qt.T
            ka[at, :] = jnp.concatenate([k, hot, ones, zeros], axis=0).T
            dt = jnp.concatenate([d, rows3(-delta), zeros48], axis=0)
            da[:, at] = dt
            dn[at, :] = dt.T
            va[at, :] = jnp.concatenate([v, ones, zeros48], axis=0).T
        line = jnp.broadcast_to(f_ref[pl.ds(h,1), :], (BLK, 2*BLK))
        rolled = pltpu.roll(line, 0, 1, stride=1, stride_axis=0)
        r = lax.broadcasted_iota(jnp.int32, (BLK,2*BLK), 0)
        c = lax.broadcasted_iota(jnp.int32, (BLK,2*BLK), 1)
        bias[...] = jnp.where(c < r, NEG, rolled)
        gsum[...] = jnp.zeros_like(gsum)
        for j in range(length//BLK):
            a0 = j*BLK
            kj = ka[a0:a0+BLK, :]
            vj = va[a0:a0+BLK, :]
            src, off = a0//rows, a0%rows
            kt = x_ref[src, pl.ds(base+group, size), off:off+BLK]
            dk = dv = None
            for a in range(a0, length, 2*BLK):
                b = min(a+2*BLK, length)
                s = dot(kj, qa[:, a:b])
                if a == a0:
                    s = s + bias[:, :b-a]
                p = jnp.exp(s)
                ds = p * dot(vj, da[:, a:b])
                if a == a0:
                    gsum[:, :b-a] += ds
                pl_, dl = p.astype(bf16), ds.astype(bf16)
                u = dot(pl_, dn[a:b, :]); dv = u if dv is None else dv+u
                u = dot(dl, qn[a:b, :]); dk = u if dk is None else dk+u
                u = dot(kt, dl)
                if j == 0:
                    dq[:, a:b] = u
                else:
                    dq[:, a:b] += u
            g_ref[src, pl.ds(base+group,size), off:off+BLK] = dk.T[:size].astype(bf16)
            g_ref[src, pl.ds(base+2*group,size), off:off+BLK] = dv.T[:size].astype(bf16)
        for s in range(n):
            g_ref[s, pl.ds(base,size), :] = (dq[:, s*rows:(s+1)*rows]*0.125).astype(bf16)
        eight = gsum[0:8, :]
        for i in range(1, BLK//8):
            eight = eight + pltpu.roll(gsum[8*i:8*i+8, :], 2*BLK-8*i, 1)
        line = eight[0:1]
        for i in range(1, 8):
            line = line + pltpu.roll(eight, 2*BLK-i, 1)[i:i+1]
        diag_ref[pl.ds(h,1), :] = line
        return carry
    lax.fori_loop(0, heads, head, 0)

def attn_bwd(x, do, f, of, lse):
    n, depth, rows = x.shape
    heads = f.shape[0]
    length = n*rows
    return pl.pallas_call(functools.partial(attn_bwd_kernel, heads, n, rows),
        out_shape=[jax.ShapeDtypeStruct((n, 3*heads*64, rows), bf16), jax.ShapeDtypeStruct((heads,2*BLK), f32)],
        in_specs=[pl.BlockSpec(memory_space=pltpu.VMEM)]*5,
        out_specs=[pl.BlockSpec(memory_space=pltpu.VMEM)]*2,
        scratch_shapes=[pltpu.VMEM((128,length),bf16), pltpu.VMEM((length,128),bf16), pltpu.VMEM((length,128),bf16), pltpu.VMEM((128,length),bf16), pltpu.VMEM((length,128),bf16), pltpu.VMEM((length,128),bf16),
           pltpu.VMEM((BLK,2*BLK),f32), pltpu.VMEM((64,length),f32), pltpu.VMEM((BLK,2*BLK),f32)],
        compiler_params=pltpu.CompilerParams(vmem_limit_bytes=48*1024*1024),
        name="attention_backward",
    )(x, do, f, of, lse)


def expert_kernel(blocks, rows_ref, cots_ref, inner_ref, outer_ref, made_ref, back_ref, gin_ref, gout_ref, rows_t, cots_t, made, back, act_s, pre_s):
    step = pl.program_id(0)
    total = rows_ref.shape[0]
    piece = total // blocks

    @pl.when(step == 0)
    def _():
        for b in range(blocks):
            at = slice(b * piece, (b + 1) * piece)
            made[at, :] = jnp.zeros((piece, made.shape[1]), f32)
            back[at, :] = jnp.zeros((piece, made.shape[1]), f32)
        for b in range(total // 128):
            at = slice(b * 128, (b + 1) * 128)
            rows_t[:, at] = rows_ref[at, :].T
            cots_t[:, at] = cots_ref[at, :].T

    def part(b, carry):
        at = pl.ds(pl.multiple_of(b * piece, piece), piece)
        pre = dot(rows_ref[at, :], inner_ref[...])
        cot = dot(cots_ref[at, :], outer_ref[...], NT)
        square = pre * pre
        t = jnp.tanh(pre * (ROOT + (ROOT * 0.044715) * square))
        half = 0.5 + 0.5 * t
        act = (pre * half).astype(bf16)
        slope = half + (0.5 * pre) * (1.0 - t * t) * (ROOT + (ROOT * 3 * 0.044715) * square)
        back_pre = (cot * slope).astype(bf16)
        act_s[at, :] = act
        pre_s[at, :] = back_pre
        made[at, :] += dot(act, outer_ref[...])
        back[at, :] += dot(back_pre, inner_ref[...], NT)
        return carry

    lax.fori_loop(0, blocks, part, 0)
    gin_ref[...] = dot(rows_t[...], pre_s[...]).astype(bf16)
    gout_ref[...] = dot(cots_t[...], act_s[...]).astype(bf16).T

    @pl.when(step == pl.num_programs(0) - 1)
    def _():
        for b in range(blocks):
            at = slice(b * piece, (b + 1) * piece)
            made_ref[at, :] = made[at, :].astype(bf16)
            back_ref[at, :] = back[at, :].astype(bf16)


ROOT = 0.7978845608028654


def expert_pass(rows, cots, inner, outer):
    total, width = rows.shape
    hidden = inner.shape[1]
    wide = 384
    whole = pl.BlockSpec((total, width), lambda i: (0, 0))
    return pl.pallas_call(
        partial(expert_kernel, 4),
        grid=(hidden // wide,),
        out_shape=[
            jax.ShapeDtypeStruct((total, width), bf16),
            jax.ShapeDtypeStruct((total, width), bf16),
            jax.ShapeDtypeStruct((width, hidden), bf16),
            jax.ShapeDtypeStruct((hidden, width), bf16),
        ],
        in_specs=[
            whole,
            whole,
            pl.BlockSpec((width, wide), lambda i: (0, i)),
            pl.BlockSpec((wide, width), lambda i: (i, 0)),
        ],
        out_specs=[
            whole,
            whole,
            pl.BlockSpec((width, wide), lambda i: (0, i)),
            pl.BlockSpec((wide, width), lambda i: (i, 0)),
        ],
        scratch_shapes=[
            pltpu.VMEM((width, total), bf16),
            pltpu.VMEM((width, total), bf16),
            pltpu.VMEM((total, width), f32),
            pltpu.VMEM((total, width), f32),
            pltpu.VMEM((total, wide), bf16),
            pltpu.VMEM((total, wide), bf16),
        ],
        compiler_params=pltpu.CompilerParams(vmem_limit_bytes=50 * 1024 * 1024),
        name="expert_pass",
    )(rows, cots, inner, outer)


def rms_norm(values, gain):
    return values * lax.rsqrt(jnp.mean(values * values, axis=-1, keepdims=True) + EPSILON) * gain


def buckets(distance):
    far = 16 + sum(((distance >= limit).astype(jnp.int32) for limit in THRESHOLDS))
    return jnp.where(distance < 16, jnp.maximum(distance, 0), far)


def route_gates(router_logits, chosen):
    chances = jax.nn.softmax(router_logits, axis=-1)
    picks = (
        chosen[:, :, None] == jnp.arange(router_logits.shape[-1], dtype=jnp.int32)[None, None, :]
    ).astype(f32)
    picked = jnp.sum(chances[:, None, :] * picks, axis=2)
    return picked / jnp.sum(picked, axis=1, keepdims=True)


def slot_places(chosen, order, capacity, experts):
    hot = (chosen[:, :, None] == jnp.arange(experts, dtype=jnp.int32)[None, None, :]).astype(bf16)
    before = (order[None, :] < order[:, None]).astype(bf16)
    ahead = dot(before, hot.reshape(chosen.shape[0], 2 * experts)).reshape(hot.shape)
    firsts = jnp.sum(hot[:, 0].astype(f32), axis=0)
    hot = hot.astype(f32)
    slot_first = jnp.sum(ahead[:, 0] * hot[:, 0], axis=1)
    slot_second = jnp.sum((ahead[:, 1] + firsts[None, :]) * hot[:, 1], axis=1)
    slots = jnp.stack([slot_first, slot_second], axis=1).astype(jnp.int32)
    return jnp.where(slots < capacity, chosen * capacity + slots, experts * capacity)


def local(
    layer_input,
    cotangent,
    norm_gain_one,
    w_query,
    w_key,
    w_value,
    w_output,
    rel_table,
    norm_gain_two,
    w_router,
    w_expert_in,
    w_expert_out,
    segment_ids,
    routes,
    priority,
):
    inputs = layer_input[0].astype(f32)
    rows, width = inputs.shape
    heads = rel_table.shape[0]
    head_size = width // heads
    shards = lax.axis_size("ctx")
    experts = lax.axis_size("expert")
    capacity = min(rows, 5 * rows // (2 * experts))
    own_heads = heads // shards
    group = own_heads * head_size

    inner_weight = lax.all_gather(w_expert_in, ("ctx", "dp"), axis=1, tiled=True)[0]
    outer_weight = lax.all_gather(w_expert_out, ("ctx", "dp"), axis=1, tiled=True)[0]

    normed_input, norm_back = jax.vjp(rms_norm, inputs, norm_gain_one)
    normed_low = normed_input.astype(bf16)

    def project(weight):
        made = lax.dot_general(weight, normed_low, (((0,), (1,)), ((), ())), preferred_element_type=f32)
        return made.astype(bf16).reshape(shards, group, rows)

    segment_rows = jnp.broadcast_to(segment_ids.astype(bf16)[None], (shards, 16, rows))
    sent = jnp.concatenate([project(w_query), project(w_key), project(w_value), segment_rows], axis=1)
    held = lax.all_to_all(sent, "ctx", split_axis=0, concat_axis=0, tiled=True)

    table = rel_table.astype(f32)
    table = table - table[:, BUCKETS - 1 :]
    distance = jnp.arange(2 * BLK, dtype=jnp.int32)
    in_bucket = (buckets(distance)[:, None] == jnp.arange(BUCKETS, dtype=jnp.int32)[None, :]) & (
        distance[:, None] < THRESHOLDS[-1]
    )
    in_bucket = in_bucket.astype(f32)
    back_distance = BLK - distance
    in_bucket_front = (
        (buckets(back_distance)[:, None] == jnp.arange(BUCKETS, dtype=jnp.int32)[None, :])
        & (back_distance[:, None] < THRESHOLDS[-1])
        & (back_distance[:, None] >= 0)
    ).astype(f32)
    own_table = lax.dynamic_slice_in_dim(table, lax.axis_index("ctx") * own_heads, own_heads, 0)
    line_front = jnp.sum(own_table[:, None, :] * in_bucket_front[None], axis=2)
    line_back = jnp.sum(own_table[:, None, :] * in_bucket[None], axis=2)
    attended, attended_whole, lse = attn_fwd(held, line_front)
    mixed_t = lax.all_to_all(attended, "ctx", split_axis=0, concat_axis=0, tiled=True).reshape(width, rows)

    hidden = inputs + dot(mixed_t, w_output, TN)
    second_normed, norm_back_two = jax.vjp(rms_norm, hidden, norm_gain_two)
    normed_two_low = second_normed.astype(bf16)
    router_logits = dot(normed_two_low, w_router)
    chosen = routes[0]
    gates, gate_back = jax.vjp(partial(route_gates, chosen=chosen), router_logits)
    places = slot_places(chosen, priority[0, 0], capacity, experts)
    slots = jnp.arange(experts * capacity, dtype=jnp.int32)
    first = (places[:, 0][:, None] == slots[None, :]).astype(bf16)
    second = (places[:, 1][:, None] == slots[None, :]).astype(bf16)
    out_cot = cotangent[0].astype(f32)
    outgoing = dot(first + second, normed_two_low, TN).astype(bf16)
    outgoing_cot = (
        dot(first, (gates[:, 0:1] * out_cot).astype(bf16), TN)
        + dot(second, (gates[:, 1:2] * out_cot).astype(bf16), TN)
    ).astype(bf16)
    outgoing = outgoing.reshape(experts, capacity, width)
    outgoing_cot = outgoing_cot.reshape(experts, capacity, width)
    arrived = lax.all_to_all(outgoing, "expert", split_axis=0, concat_axis=0, tiled=True)
    arrived_cot = lax.all_to_all(outgoing_cot, "expert", split_axis=0, concat_axis=0, tiled=True)
    made, back, inner_grad, outer_grad = expert_pass(
        arrived.reshape(experts * capacity, width),
        arrived_cot.reshape(experts * capacity, width),
        inner_weight,
        outer_weight,
    )
    expert_in_grad = lax.psum_scatter(inner_grad[None], ("ctx", "dp"), scatter_dimension=1, tiled=True)
    expert_out_grad = lax.psum_scatter(outer_grad[None], ("ctx", "dp"), scatter_dimension=1, tiled=True)
    made = lax.all_to_all(
        made.reshape(experts, capacity, width), "expert", split_axis=0, concat_axis=0, tiled=True
    ).reshape(experts * capacity, width)
    back = lax.all_to_all(
        back.reshape(experts, capacity, width), "expert", split_axis=0, concat_axis=0, tiled=True
    ).reshape(experts * capacity, width)
    pair_first = dot(first, made)
    pair_second = dot(second, made)
    layer_output = (hidden + (gates[:, 0:1] * pair_first + gates[:, 1:2] * pair_second)).astype(bf16)
    gate_cot = jnp.stack([jnp.sum(out_cot * pair_first, axis=1), jnp.sum(out_cot * pair_second, axis=1)], axis=1)
    token_cot = dot(first + second, back)
    logit_cot = gate_back(gate_cot)[0]
    normed_two_cot = token_cot + jnp.dot(logit_cot, w_router.astype(f32).T, precision=HIGH_PRECISION)
    router_grad = jnp.dot(normed_two_low.astype(f32).T, logit_cot, precision=HIGH_PRECISION)
    hidden_part, gain_two_grad = norm_back_two(normed_two_cot)
    hidden_cot = out_cot + hidden_part
    hidden_cot_low = hidden_cot.astype(bf16)
    projection_grad = dot(mixed_t, hidden_cot_low)
    mixed_cot = dot(w_output, hidden_cot_low, NT).astype(bf16).reshape(shards, group, rows)
    held_cot = lax.all_to_all(mixed_cot, "ctx", split_axis=0, concat_axis=0, tiled=True)
    grads, diagonals = attn_bwd(held, held_cot, line_back, attended_whole, lse)
    near = jnp.sum(diagonals[:, :, None] * in_bucket[None], axis=1)
    near = jnp.concatenate([near[:, : BUCKETS - 1], -jnp.sum(near, axis=1, keepdims=True)], axis=1)
    table_grad = lax.dynamic_update_slice_in_dim(
        jnp.zeros((heads, BUCKETS), f32), near, lax.axis_index("ctx") * own_heads, 0
    )
    grads = lax.all_to_all(grads, "ctx", split_axis=0, concat_axis=0, tiled=True)
    query_cot = grads[:, :group].reshape(width, rows)
    key_cot = grads[:, group : 2 * group].reshape(width, rows)
    value_cot = grads[:, 2 * group :].reshape(width, rows)

    def turned(weight, cot):
        return lax.dot_general(cot, weight, (((0,), (1,)), ((), ())), preferred_element_type=f32)

    normed_cot = turned(w_query, query_cot) + turned(w_key, key_cot) + turned(w_value, value_cot)

    def weight_grad(cot):
        return lax.dot_general(normed_low, cot, (((0,), (1,)), ((), ())), preferred_element_type=f32).astype(bf16)

    input_part, gain_one_grad = norm_back(normed_cot)
    input_grad = hidden_cot + input_part
    everywhere = ("expert", "ctx", "dp")
    large = lax.psum(
        (weight_grad(query_cot), weight_grad(key_cot), weight_grad(value_cot), projection_grad.astype(bf16)),
        everywhere,
    )
    small = lax.psum((gain_one_grad, table_grad, gain_two_grad, router_grad), everywhere)
    return (
        layer_output[None],
        input_grad[None],
        small[0],
        large[0].astype(f32),
        large[1].astype(f32),
        large[2].astype(f32),
        large[3].astype(f32),
        small[1],
        small[2],
        small[3],
        expert_in_grad.astype(f32),
        expert_out_grad.astype(f32),
    )


def solution(mesh):
    placed = (
        P(("expert", "dp"), "ctx", None),
        P(("expert", "dp"), "ctx", None),
        P(),
        P(),
        P(),
        P(),
        P(),
        P(),
        P(),
        P(),
        P("expert", ("ctx", "dp"), None),
        P("expert", ("ctx", "dp"), None),
        P(("expert", "dp"), "ctx"),
        P(("expert", "dp"), "ctx", None),
        P(("expert", "dp"), "ctx", None),
    )
    return jax.shard_map(
        local,
        mesh=mesh,
        in_specs=placed,
        out_specs=(
            P(("expert", "dp"), "ctx", None),
            P(("expert", "dp"), "ctx", None),
            P(),
            P(),
            P(),
            P(),
            P(),
            P(),
            P(),
            P(),
            P("expert", ("ctx", "dp"), None),
            P("expert", ("ctx", "dp"), None),
        ),
        check_vma=False,
    )
```

time: 2300 us -> 855 us (0.37)
  local copies, waits for them, and re-layouts: 771 us -> 12.4 us
  matrix products: 611 us -> 49 us
  waiting for transfers between devices: 695 us -> 524 us
  Pallas kernels: 0 us -> 105 us
  other arithmetic: 93.5 us -> 21 us
  blocking collectives: 55.8 us -> 91.2 us
  loops' own time: 23 us -> 0 us
    dot_general x89 -> x22, matrix products: 611 us -> 49 us  [the longest x11 26.3 us: dot(): return lax.dot_general(a, b, dims, preferred_element_type=f32)]
    dot_general x16 -> x1, local copies, waits for them, and re-layouts: 283 us -> 0.01 us  [dot(): return lax.dot_general(a, b, dims, preferred_element_type=f32)]
    dynamic_update_slice x16 -> x1, local copies, waits for them, and re-layouts: 276 us -> 0.07 us  [local(): lax.dynamic_update_slice_in_dim(jnp.zeros((heads, BUCKETS), f32), near, l...]
    all_to_all x3 -> x5, waiting for transfers between devices: 12.7 us -> 222 us  [the longest x1 98.3 us: local(): held = lax.all_to_all(sent, 'ctx', split_axis=0, concat_axis=0, tiled=True)]
    reduce_scatter x2 -> x0, waiting for transfers between devices: 204 us -> none  [the longest x1 110 us: local(): lax.psum_scatter(key_whole, 'ctx', scatter_dimension=0, tiled=True)]
    pallas_call x0 -> x3, Pallas kernels: none -> 105 us  [the longest x1 64 us: expert_pass(): pl.pallas_call(partial(expert_kernel, 4), grid=(hidden // wide,), out_sha...]
    reduce_scatter x1, waiting for transfers between devices: 168 us -> 90.6 us  [local(): lax.psum_scatter(inner_grad[None], ('ctx', 'dp'), scatter_dimension=1, ti...]
    reduce_scatter x1, waiting for transfers between devices: 167 us -> 97.2 us  [local(): lax.psum_scatter(outer_grad[None], ('ctx', 'dp'), scatter_dimension=1, ti...]
  transfers between devices with their start and end apart: 13 -> 11, of which waited for: 7 -> 9; matrix products, arithmetic and copies ran while one was open for 24% -> 7% of each run, Pallas kernels for 0% -> 2%
where the time goes in v1:
time: 855 us; the launch traced here: 847 us
  waiting for transfers between devices  524 us (61%)
  Pallas kernels  105 us (12%)
  blocking collectives  91.2 us (11%)
  matrix products  49 us (6%)
  starting transfers between devices  29.4 us (3%)
  other arithmetic  21 us (2%)
  between operations  14.9 us (2%)
  local copies, waits for them, and re-layouts  12.4 us (1%)
    all_to_all x1, waiting for transfers between devices, local(): held = lax.all_to_all(sent, 'ctx', split_axis=0, concat_axis=0, tiled=True)  98.3 us
    reduce_scatter x1, waiting for transfers between devices, local(): lax.psum_scatter(outer_grad[None], ('ctx', 'dp'), scatter_dimension=1, ti...  97.2 us
    psum x1, waiting for transfers between devices, local(): lax.psum((weight_grad(query_cot), weight_grad(key_cot), weight_grad(value...  91.3 us
    reduce_scatter x1, waiting for transfers between devices, local(): lax.psum_scatter(inner_grad[None], ('ctx', 'dp'), scatter_dimension=1, ti...  90.6 us
    pallas_call x1, Pallas kernels, expert_pass(): pl.pallas_call(partial(expert_kernel, 4), grid=(hidden // wide,), out_sha...  64 us
    all_to_all x1, waiting for transfers between devices, local(): lax.all_to_all(grads, 'ctx', split_axis=0, concat_axis=0, tiled=True)  50.4 us
    psum x1, blocking collectives, local(): lax.psum((gain_one_grad, table_grad, gain_two_grad, router_grad), everywh...  38.5 us
    all_to_all x1, waiting for transfers between devices, local(): lax.all_to_all(attended, 'ctx', split_axis=0, concat_axis=0, tiled=True)  32.1 us
  transfers between devices with their start and end apart: 11, of which 9 were waited for; matrix products, arithmetic and copies ran while one was open for 7% of the time, Pallas kernels for 2%

profile of v1, /device:TPU:0, one launch (start us, length us, event | category | flops | bytes accessed | tf_op | source)
XLA Modules:
  0.0 847.0 jit_solution(9098936070626431686)
XLA Ops:
  9.3 2.4 fusion.37
  12.8 3.0 fusion.38
  17.2 1.7 fusion.39
  21.1 1.6 pad_maximum_fusion
  22.7 6.5 all-to-all-start
  30.6 98.3 %all-to-all-done.x_ref = bf16[4,592,512]{2,1,0:T(8,128)(2,1)} async-done(((bf16[4,592,512]{2,1,0:T(8,128)(2,1)}), bf16[4,592,512]{2,1,0:T(8,128)(2,1)}, u32[]{:S(2)}, u32[]{:S(2)}) %all-to-all-start) | async-done | bytes 2424864 | tf_op jit(solution)/shard_map/all_to_all | solution.py:353
  128.9 17.8 %attention_forward.1 = (bf16[4,192,512]{2,1,0:T(8,128)(2,1)}, f32[192,2048]{1,0:T(8,128)S(1)}, f32[3,2048]{1,0:T(4,128)S(1)}) custom-call(bf16[4,592,512]{2,1,0:T(8,128)(2,1)} %all-to-all-done.x_ref, f32[3,512]{1,0:T(4,128)S(1)} %get-tuple-element.41.f_ref), custom_call_target="tpu_custom_call" | custom-call | tf_op jit(solution)/shard_map/attention_forward/pallas_call | solution.py:94
  146.7 4.4 all-to-all-start.1
  151.7 32.1 %all-to-all-done.1 = bf16[4,192,512]{2,1,0:T(8,128)(2,1)} async-done(((bf16[4,192,512]{2,1,0:T(8,128)(2,1)}), bf16[4,192,512]{2,1,0:T(8,128)(2,1)}, u32[]{:S(2)}, u32[]{:S(2)}) %all-to-all-start.1) | async-done | bytes 786464 | tf_op jit(solution)/shard_map/all_to_all | solution.py:372
  183.9 2.7 multiply_reduce_fusion.2
  189.8 2.8 fusion
  192.5 4.4 all-to-all-start.3
  197.0 3.9 convolution_convert_fusion
  200.9 20.4 %all-to-all-done.3 = bf16[4,320,768]{2,1,0:T(8,128)(2,1)} async-done(((bf16[4,320,768]{2,1,0:T(8,128)(2,1)}), bf16[4,320,768]{2,1,0:T(8,128)(2,1)}, u32[]{:S(2)}, u32[]{:S(2)}) %all-to-all-start.3) | async-done | bytes 1966112 | tf_op jit(solution)/shard_map/all_to_all | solution.py:393
  221.3 28.8 %all_to_all.40 = bf16[4,320,768]{2,1,0:T(8,128)(2,1)} all-to-all(bf16[4,320,768]{2,1,0:T(8,128)(2,1)} %bitcast.153), channel_id=1, replica_groups=mesh['expert'=4,'ctx'=4,'dp'=2] {'expert'}, dimensions={0} | all-to-all | bytes 3932160 | tf_op jit(solution)/shard_map/all_to_all | solution.py:392
  250.1 64.0 %expert_pass.1 = (bf16[1280,768]{1,0:T(8,128)(2,1)}, bf16[1280,768]{1,0:T(8,128)(2,1)}, bf16[768,3072]{1,0:T(8,128)(2,1)}, bf16[3072,768]{1,0:T(8,128)(2,1)}) custom-call(bf16[1280,768]{1,0:T(8,128)(2,1)} %bitcast.141, bf16[1280,768]{1,0:T(8,128)(2,1)} %bitcast.25.cots_ref, bf16[768,3072]{1,0:T(8,128)(2,1)} %bitcast.142, bf16[3072,768]{1,0:T(8,128)(2,1)} %bitcast.143), custom_call_target="tpu_custom_call" | custom-call | tf_op jit(solution)/shard_map/expert_pass/pallas_call | solution.py:250
  314.1 4.4 all-to-all-start.4
  318.5 24.3 %all-to-all-done.4 = bf16[4,320,768]{2,1,0:T(8,128)(2,1)} async-done(((bf16[4,320,768]{2,1,0:T(8,128)(2,1)}), bf16[4,320,768]{2,1,0:T(8,128)(2,1)}, u32[]{:S(2)}, u32[]{:S(2)}) %all-to-all-start.4) | async-done | bytes 1966112 | tf_op jit(solution)/shard_map/all_to_all | solution.py:402
  342.9 4.6 all-to-all-start.5
  347.6 3.0 fusion.1
  350.6 4.0 fusion.23
  354.7 17.1 %all-to-all-done.5 = bf16[4,320,768]{2,1,0:T(8,128)(2,1)} async-done(((bf16[4,320,768]{2,1,0:T(8,128)(2,1)}), bf16[4,320,768]{2,1,0:T(8,128)(2,1)}, u32[]{:S(2)}, u32[]{:S(2)}) %all-to-all-start.5) | async-done | bytes 1966112 | tf_op jit(solution)/shard_map/all_to_all | solution.py:405
  371.9 3.2 fusion.26
  375.1 1.8 multiply_reduce_fusion
  378.5 1.7 fusion.40
  380.2 2.3 copy.40
  382.5 23.9 %all_to_all.41.do_ref = bf16[4,192,512]{2,1,0:T(8,128)(2,1)S(1)} all-to-all(bf16[4,192,512]{2,1,0:T(8,128)(2,1)} %bitcast.149), channel_id=1, replica_groups=mesh['expert'=4,'ctx'=4,'dp'=2] {'ctx'}, dimensions={0} | all-to-all | bytes 1572864 | tf_op jit(solution)/shard_map/all_to_all | solution.py:421
  406.4 23.4 %attention_backward.1 = (bf16[4,576,512]{2,1,0:T(8,128)(2,1)}, f32[3,512]{1,0:T(4,128)S(1)}) custom-call(bf16[4,592,512]{2,1,0:T(8,128)(2,1)} %all-to-all-done.x_ref, bf16[4,192,512]{2,1,0:T(8,128)(2,1)S(1)} %all_to_all.41.do_ref, f32[3,512]{1,0:T(4,128)S(1)} %get-tuple-element.40.f_ref, f32[192,2048]{1,0:T(8,128)S(1)} %get-tuple-element.24.of_ref, ...), custom_call_target="tpu_custom_call" | custom-call | tf_op jit(solution)/shard_map/attention_backward/pallas_call | solution.py:187
  429.8 4.6 all-to-all-start.7
  434.5 2.9 convolution_convert_fusion.1
  437.4 50.4 %all-to-all-done.7 = bf16[4,576,512]{2,1,0:T(8,128)(2,1)} async-done(((bf16[4,576,512]{2,1,0:T(8,128)(2,1)}), bf16[4,576,512]{2,1,0:T(8,128)(2,1)}, u32[]{:S(2)}, u32[]{:S(2)}) %all-to-all-start.7) | async-done | bytes 2359328 | tf_op jit(solution)/shard_map/all_to_all | solution.py:428
  487.8 2.0 fusion.96
  489.8 2.0 convolution_convert_fusion.2
  491.8 2.0 convolution_convert_fusion.3
  493.8 2.0 convolution_convert_fusion.4
  499.6 2.6 fusion.100
  503.6 2.9 fusion.14
  506.5 38.5 %all-reduce = (f32[768]{0:T(1024)}, f32[12,32]{1,0:T(8,128)}, f32[768]{0:T(1024)}, f32[768,4]{0,1:T(4,128)}) all-reduce(f32[768]{0:T(1024)} %get-tuple-element.32, f32[12,32]{1,0:T(8,128)} %copy-done.23, f32[768]{0:T(1024)} %get-tuple-element.30, ...), channel_id=1, replica_groups=mesh['expert'=4,'ctx'=4,'dp'=2] {'expert','ctx','dp'}, use_global_device_ids=true, to_apply=%region_19.20 | all-reduce | flops 4992 | bytes 39936 | tf_op jit(solution)/shard_map/psum | solution.py:448
  545.7 3.0 fusion.20
  548.7 91.3 %all-reduce.4.cloned.1.call-done = (bf16[768,768]{1,0:T(8,128)(2,1)}, bf16[768,768]{1,0:T(8,128)(2,1)}, bf16[768,768]{1,0:T(8,128)(2,1)}, bf16[768,768]{1,0:T(8,128)(2,1)}) async-done(((bf16[768,768]{1,0:T(8,128)(2,1)}, bf16[768,768]{1,0:T(8,128)(2,1)}, bf16[768,768]{1,0:T(8,128)(2,1)}, bf16[768,768]{1,0:T(8,128)(2,1)}), (bf16[768,768]{1,0:T(8,128)(2,1)}, bf16[768,768]{1,0:T(8,128)(2,1)}, ...) | async-done | bytes 4718608 | tf_op jit(solution)/shard_map/psum | solution.py:444
  640.0 2.9 convert_element_type.451
  642.9 1.6 convert_element_type.453
  644.6 1.6 convert_element_type.455
  646.3 1.6 convert_element_type.457
  647.8 90.6 %reduce-scatter.3.cloned.1.call-done = bf16[1,96,3072]{2,1,0:T(8,128)(2,1)} async-done(((bf16[1,768,3072]{2,1,0:T(8,128)(2,1)}), bf16[1,96,3072]{2,1,0:T(8,128)(2,1)}) %reduce-scatter.3.cloned.1.call-update) | async-done | bytes 589840 | tf_op jit(solution)/shard_map/reduce_scatter | solution.py:400
  738.4 2.2 convert_element_type.458
  740.6 97.2 %reduce-scatter.5.cloned.1.call-done = bf16[1,384,768]{2,1,0:T(8,128)(2,1)} async-done(((bf16[1,3072,768]{2,1,0:T(8,128)(2,1)}), bf16[1,384,768]{2,1,0:T(8,128)(2,1)}) %reduce-scatter.5.cloned.1.call-update) | async-done | bytes 589840 | tf_op jit(solution)/shard_map/reduce_scatter | solution.py:401
  837.8 2.2 convert_element_type.459
  (136 shorter events, 19.7 us)
Async XLA Ops:
  7.2 10.0 %copy-start = (bf16[768,768]{1,0:T(8,128)(2,1)S(1)}, bf16[768,768]{1,0:T(8,128)(2,1)}, u32[]{:S(2)}) copy-start(bf16[768,768]{1,0:T(8,128)(2,1)} %param.20) | copy-start | bytes 3538948
  7.2 242.9 %all-gather.3.cloned.1.call-start = ((), (), s32[]{:S(2)}) async-start(), calls=%async_computation.10 | async-start | bytes 5308416 | tf_op jit(solution)/shard_map/all_gather | solution.py:341
  9.3 484.5 %copy-start.25 = (f32[512]{0:T(512)}, f32[512]{0:T(512)S(1)}, u32[]{:S(2)}) copy-start(f32[512]{0:T(512)S(1)} %fusion.85) | copy-start | bytes 6148
  11.7 1.1 copy-start.7
  11.7 1.1 copy-start.27
  22.7 7.2 copy-start.29
  22.7 7.2 copy-start.21
  22.7 106.2 %all-to-all-start = ((bf16[4,592,512]{2,1,0:T(8,128)(2,1)}), bf16[4,592,512]{2,1,0:T(8,128)(2,1)}, u32[]{:S(2)}, u32[]{:S(2)}) async-start(bf16[4,592,512]{2,1,0:T(8,128)(2,1)} %pad_maximum_fusion), calls=%async_computation | async-start | bytes 4849664 | tf_op jit(solution)/shard_map/all_to_all | solution.py:353
  29.2 220.9 %all-gather.5.cloned.1.call-start = ((), (), s32[]{:S(2)}) async-start(), calls=%async_computation.11 | async-start | bytes 5308416 | tf_op jit(solution)/shard_map/all_gather | solution.py:342
  128.9 22.2 %copy-start.32 = (s32[1,1,512]{2,1,0:T(1,128)S(1)}, s32[1,1,512]{2,1,0:T(1,128)}, u32[]{:S(2)}) copy-start(s32[1,1,512]{2,1,0:T(1,128)} %param.29) | copy-start | bytes 6148
  146.7 37.2 %all-to-all-start.1 = ((bf16[4,192,512]{2,1,0:T(8,128)(2,1)}), bf16[4,192,512]{2,1,0:T(8,128)(2,1)}, u32[]{:S(2)}, u32[]{:S(2)}) async-start(bf16[4,192,512]{2,1,0:T(8,128)(2,1)} %get-tuple-element.21), calls=%async_computation.1 | async-start | bytes 1572864 | tf_op jit(solution)/shard_map/all_to_all | solution.py:372
  183.9 2.7 copy-start.22
  186.5 1.1 copy-start.3
  186.5 0.7 copy-start.24
  186.6 1.7 copy-start.18
  187.3 0.9 copy-start.6
  192.5 28.8 %all-to-all-start.3 = ((bf16[4,320,768]{2,1,0:T(8,128)(2,1)}), bf16[4,320,768]{2,1,0:T(8,128)(2,1)}, u32[]{:S(2)}, u32[]{:S(2)}) async-start(bf16[4,320,768]{2,1,0:T(8,128)(2,1)} %bitcast.152), calls=%async_computation.3 | async-start | bytes 3932160 | tf_op jit(solution)/shard_map/all_to_all | solution.py:393
  314.1 28.8 %all-to-all-start.4 = ((bf16[4,320,768]{2,1,0:T(8,128)(2,1)}), bf16[4,320,768]{2,1,0:T(8,128)(2,1)}, u32[]{:S(2)}, u32[]{:S(2)}) async-start(bf16[4,320,768]{2,1,0:T(8,128)(2,1)} %bitcast.28), calls=%async_computation.4 | async-start | bytes 3932160 | tf_op jit(solution)/shard_map/all_to_all | solution.py:402
  342.9 29.0 %all-to-all-start.5 = ((bf16[4,320,768]{2,1,0:T(8,128)(2,1)}), bf16[4,320,768]{2,1,0:T(8,128)(2,1)}, u32[]{:S(2)}, u32[]{:S(2)}) async-start(bf16[4,320,768]{2,1,0:T(8,128)(2,1)} %bitcast.31), calls=%async_computation.5 | async-start | bytes 3932160 | tf_op jit(solution)/shard_map/all_to_all | solution.py:405
  347.5 3.0 copy-start.4
  347.6 3.0 copy-start.19
  371.9 3.2 copy-start.5
  375.1 1.8 copy-start.20
  376.9 1.6 copy-start.30
  377.3 1.1 copy-start.1
  429.8 4.7 copy-start.2
  429.8 58.0 %all-to-all-start.7 = ((bf16[4,576,512]{2,1,0:T(8,128)(2,1)}), bf16[4,576,512]{2,1,0:T(8,128)(2,1)}, u32[]{:S(2)}, u32[]{:S(2)}) async-start(bf16[4,576,512]{2,1,0:T(8,128)(2,1)} %get-tuple-element.26), calls=%async_computation.7 | async-start | bytes 4718592 | tf_op jit(solution)/shard_map/all_to_all | solution.py:428
  434.4 205.5 %all-reduce.4.cloned.1.call-start = ((), (), s32[]{:S(2)}) async-start(), calls=%async_computation.14 | async-start | bytes 9437184 | tf_op jit(solution)/shard_map/psum | solution.py:444
  487.8 2.0 copy-start.8
  489.8 2.0 copy-start.10
  489.8 2.0 copy-start.15
  489.8 4.0 copy-start.17
  495.9 242.5 %reduce-scatter.3.cloned.1.call-start = ((), (), s32[]{:S(2)}) async-start(), calls=%async_computation.12 | async-start | bytes 5308416 | tf_op jit(solution)/shard_map/reduce_scatter | solution.py:400
  496.5 341.3 %reduce-scatter.5.cloned.1.call-start = ((), (), s32[]{:S(2)}) async-start(), calls=%async_computation.13 | async-start | bytes 5308416 | tf_op jit(solution)/shard_map/reduce_scatter | solution.py:401
  499.0 0.6 copy-start.23
  499.6 2.6 copy-start.16
  499.6 2.6 copy-start.31
  502.2 1.1 copy-start.9
  502.2 1.4 copy-start.11
  502.2 1.4 copy-start.26
  502.3 1.3 copy-start.28
  640.0 2.9 copy-start.14
  642.9 1.7 copy-start.13
  644.6 1.7 copy-start.12
Sparse Core Ops, SparseCore 0:
  10.2 124.4 all-gather.2
  136.9 93.1 all-gather.4
  496.0 143.9 all-reduce.3
  643.9 94.4 reduce-scatter.2
  742.4 95.3 reduce-scatter.4

commit v2 on v1

v2 whole, which is shorter than its diff:
```python
import functools
from functools import partial

import jax
import jax.numpy as jnp
from jax import lax
from jax.experimental import pallas as pl
from jax.experimental.pallas import tpu as pltpu
from jax.sharding import PartitionSpec as P

bf16 = jnp.bfloat16
f32 = jnp.float32
HIGH_PRECISION = lax.Precision.HIGHEST
EPSILON = 1e-06
THRESHOLDS = (19, 21, 24, 27, 31, 35, 40, 46, 52, 59, 67, 77, 87, 99, 113)
BUCKETS=32
NEG=-1e30
BLK=256
NT=(((1,),(1,)),((),()))
TN=(((0,),(0,)),((),()))

def dot(a,b,dims=(((1,),(0,)),((),()))):
    return lax.dot_general(a,b,dims,preferred_element_type=f32)

def seg_mask_rows(seg):
    which = lax.broadcasted_iota(jnp.int32, seg.shape, 0).astype(f32)
    same = seg.astype(f32) == which
    return jnp.where(same, 0.0, NEG).astype(bf16), jnp.where(same, 1.0, 0.0).astype(bf16)

def split3(v):
    hi = v.astype(bf16); rest = v - hi.astype(f32)
    mid = rest.astype(bf16); rest = rest - mid.astype(f32)
    return hi, mid, rest.astype(bf16)

ROOT = 0.7978845608028654


def remote(src, dst, send_sem, recv_sem, where):
    return pltpu.make_async_remote_copy(
        src_ref=src,
        dst_ref=dst,
        send_sem=send_sem,
        recv_sem=recv_sem,
        device_id=where,
        device_id_type=pl.DeviceIdType.MESH,
    )


def expert_split():
    experts = lax.axis_size("expert")
    me = lax.axis_index("expert")
    return experts // 2, lax.div(me, 2), lax.rem(me, 2)


def gather_start(piece, whole, near_sems, far_sems, rows=None):
    lanes, lane, core = expert_split()
    me = lane * 2 + core
    view = whole.at[me] if rows is None else whole.at[me, rows]
    copies = [remote(piece, view, near_sems.at[0], near_sems.at[1], {"expert": lane * 2 + 1 - core})]
    for k in range(1, lanes):
        copies.append(
            remote(piece, view, far_sems.at[0, k - 1], far_sems.at[1, k - 1], {"expert": lax.rem(lane + k, lanes) * 2 + core})
        )
    for copy in copies:
        copy.start()
    return copies


def relay(k, whole, sems):
    lanes, lane, core = expert_split()
    source = lax.rem(lane - k + lanes, lanes) * 2 + core
    return remote(whole.at[source], whole.at[source], sems.at[0, k - 1], sems.at[1, k - 1], {"expert": lane * 2 + 1 - core})


def greet(names):
    barrier = pltpu.get_barrier_semaphore()
    total = 0
    for name in names:
        count, at = lax.axis_size(name), lax.axis_index(name)
        for k in range(1, count):
            pl.semaphore_signal(
                barrier, inc=1, device_id={name: lax.rem(at + k, count)}, device_id_type=pl.DeviceIdType.MESH
            )
        total += count - 1
    return barrier, total


def moe_kernel(
    capacity, mixed_t, w_output, x_ref, cot_ref, gain_ref, router_ref, info_ref, cots_hbm, inner_hbm, outer_hbm,
    base_ref, far_ref, hidden_cot_ref, mixed_cot_ref, small_ref, gin_hbm, gout_hbm,
    nt, cots, inner, outer, act_all, pre_all, rows_all, cots_all, made, back, part, pair_in, total,
    core_in, far_in, gate_out, gate_in,
    load_sems, cot_sems, near_sems, far_sems, relay_sems, pair_sems, core_sems, back_sems, gate_sems, stage_sems, free_sem,
):
    experts = lax.axis_size("expert")
    lanes, lane, core = expert_split()
    me = lane * 2 + core
    other = lane * 2 + 1 - core
    rows, width = x_ref.shape
    hidden_size = inner.shape[1]
    wide = width
    hidden = hidden_cot_ref
    pieces = 2
    step_rows = rows // pieces

    loads = [
        pltpu.make_async_copy(inner_hbm, inner, load_sems.at[0]),
        pltpu.make_async_copy(outer_hbm, outer, load_sems.at[1]),
    ]
    for copy in loads:
        copy.start()
    barrier, peers = greet(("expert",))
    sent = []
    for p in range(pieces):
        at = slice(p * step_rows, (p + 1) * step_rows)
        now = x_ref[at, :].astype(f32) + dot(mixed_t[:, at], w_output[...], TN)
        hidden[at, :] = now
        scale = lax.rsqrt(jnp.mean(now * now, axis=1, keepdims=True) + EPSILON)
        nt[me, at, :] = (now * scale * gain_ref[...].reshape(1, width)).astype(bf16)
        if p == 0:
            pl.semaphore_wait(barrier, peers)
        sent.append(gather_start(nt.at[me, at], nt, near_sems.at[p], far_sems.at[p], at))

    def gate_rows(source):
        logits = dot(router_ref[...], nt[source], NT)
        which = lax.broadcasted_iota(jnp.int32, logits.shape, 0)
        info = info_ref[source]
        chosen = (which == info[0:1]) | (which == info[1:2])
        top = jnp.max(jnp.where(chosen, logits, NEG), axis=0, keepdims=True)
        power = jnp.where(chosen, jnp.exp(jnp.minimum(logits - top, 0.0)), 0.0)
        return power / jnp.sum(power, axis=0, keepdims=True)

    order = [me, other] + [
        lax.rem(lane - k + lanes, lanes) * 2 + sc for k in range(1, lanes) for sc in range(2)
    ]

    def fetch(i):
        return pltpu.make_async_copy(cots_hbm.at[order[i]], cots.at[i % 2], cot_sems.at[i % 2])

    fetch(0).start()

    def process(i, target, middle=None):
        source = order[i]
        fetch(i).wait()
        if i + 1 < len(order):
            fetch(i + 1).start()
        block = slice(i * capacity, (i + 1) * capacity)
        info = info_ref[source]
        place = jnp.where(info[0:1] == me, info[2:3], jnp.where(info[1:2] == me, info[3:4], -1))
        slot = lax.broadcasted_iota(jnp.int32, (capacity, rows), 0)
        hot = slot == place
        pick = jnp.where(hot, 1.0, 0.0)
        pick_low = pick.astype(bf16)
        gates = gate_rows(source)
        which = lax.broadcasted_iota(jnp.int32, gates.shape, 0)
        own_gate = jnp.sum(jnp.where(which == me, gates, 0.0), axis=0, keepdims=True)
        slot_gate = jnp.sum(pick * own_gate, axis=1, keepdims=True)
        rows_all[block, :] = dot(pick_low, nt[source]).astype(bf16)
        cots_all[block, :] = (slot_gate * dot(pick_low, cots[i % 2])).astype(bf16)
        made[...] = jnp.zeros_like(made)
        back[...] = jnp.zeros_like(back)

        def part_of(f, carry):
            at = pl.ds(pl.multiple_of(f * wide, wide), wide)
            pre = dot(rows_all[block, :], inner[:, at])
            cot = dot(cots_all[block, :], outer[at, :], NT)
            square = pre * pre
            t = jnp.tanh(pre * (ROOT + (ROOT * 0.044715) * square))
            half = 0.5 + 0.5 * t
            act = (pre * half).astype(bf16)
            slope = half + (0.5 * pre) * (1.0 - t * t) * (ROOT + (ROOT * 3 * 0.044715) * square)
            back_pre = (cot * slope).astype(bf16)
            act_all[block, at] = act
            pre_all[block, at] = back_pre
            made[...] += dot(act, outer[at, :])
            back[...] += dot(back_pre, inner[:, at], NT)
            return carry

        steps = hidden_size // wide
        if middle is None:
            lax.fori_loop(0, steps, part_of, 0)
        else:
            lax.fori_loop(0, steps // 2, part_of, 0)
            middle()
            lax.fori_loop(steps // 2, steps, part_of, 0)
        gated = slot_gate * made[...].astype(bf16).astype(f32)
        picked_cot = dot(pick_low, cots[i % 2])
        slot_cot = jnp.sum(picked_cot * made[...].astype(bf16).astype(f32), axis=1, keepdims=True)
        gate_out[source] = jnp.broadcast_to(jnp.sum(pick * slot_cot, axis=0, keepdims=True), (8, rows))
        column = jnp.broadcast_to(place.astype(f32), (128, rows)).T[:, 0:1]
        lane_at = lax.broadcasted_iota(jnp.int32, (rows, capacity), 1).astype(f32)
        put = jnp.where(lane_at == column, 1.0, 0.0).astype(bf16)
        target[0] = dot(put, back[...].astype(bf16)).astype(bf16)
        target[1] = dot(put, gated.astype(bf16)).astype(bf16)

    for copy in loads:
        copy.wait()
    process(0, total)
    for p in range(pieces):
        sent[p][0].wait_recv()
    process(1, part.at[0])
    core_copies = [
        remote(part.at[0, v], core_in.at[v], core_sems.at[0, v], core_sems.at[1, v], {"expert": other}) for v in range(2)
    ]
    for copy in core_copies:
        copy.start()

    def gate_copy(k):
        to = lax.rem(me + k, experts)
        return remote(gate_out.at[to], gate_in.at[me], gate_sems.at[0, k - 1], gate_sems.at[1, k - 1], {"expert": to})

    relays, pairs, ready = [], [], []
    for k in range(1, lanes):
        for p in range(pieces):
            sent[p][k].wait_recv()
        passed = relay(k, nt, relay_sems)
        passed.start()
        relays.append(passed)
        from_lane = lax.rem(lane - k + lanes, lanes)
        if k == 1:
            for copy in core_copies:
                copy.wait_send()
        for sc in range(2):
            @pl.when(core != sc)
            def _():
                passed.wait_recv()

            process(2 + 2 * (k - 1) + sc, part.at[sc], ready.pop() if ready else None)
            pair = [
                remote(part.at[sc, v], pair_in.at[v], pair_sems.at[0, v, k - 1], pair_sems.at[1, v, k - 1], {"expert": other})
                for v in range(2)
            ]
            home = [
                remote(part.at[sc, 0], far_in.at[k - 1], back_sems.at[0, k - 1], back_sems.at[1, k - 1], {"expert": from_lane * 2 + sc})
            ]

            @pl.when(core != sc)
            def _():
                if k > 1:
                    pl.semaphore_wait(free_sem, 1)
                for copy in pair:
                    copy.start()

            def finish(k=k, sc=sc, pair=pair, home=home):
                @pl.when(core == sc)
                def _():
                    pair[0].wait_recv()
                    part[sc, 0] = (part[sc, 0].astype(f32) + pair_in[0].astype(f32)).astype(bf16)
                    home[0].start()
                    pair[1].wait_recv()
                    far_ref[k - 1] = (part[sc, 1].astype(f32) + pair_in[1].astype(f32)).astype(bf16)
                    if k + 1 < lanes:
                        pl.semaphore_signal(
                            free_sem, inc=1, device_id={"expert": other}, device_id_type=pl.DeviceIdType.MESH
                        )

            ready.append(finish)
            pairs.append((sc, pair, home))
        if k + 1 < lanes:
            ready.pop()()
            for sc, pair, home in pairs[-2:]:
                @pl.when(core != sc)
                def _():
                    for copy in pair:
                        copy.wait_send()

                @pl.when(core == sc)
                def _():
                    for copy in home:
                        copy.wait_send()
    if ready:
        ready.pop()()
    gate_copies = [gate_copy(k) for k in range(1, experts)]
    for copy in gate_copies:
        copy.start()
    count = rows_all.shape[0]
    for b in range(count // 128):
        at = slice(b * 128, (b + 1) * 128)
        inner[:, at] = rows_all[at, :].T
        inner[:, slice(count + b * 128, count + (b + 1) * 128)] = cots_all[at, :].T
    steps = hidden_size // wide

    def store(f, v):
        at = pl.ds(pl.multiple_of(f * wide, wide), wide)
        return pltpu.make_async_copy(outer.at[v * width : (v + 1) * width], gin_hbm.at[:, at] if v == 0 else gout_hbm.at[at, :], stage_sems.at[v])

    def grads(f, carry):
        at = pl.ds(pl.multiple_of(f * wide, wide), wide)

        @pl.when(f > 0)
        def _():
            store(f - 1, 0).wait()

        outer[:width, :] = dot(inner[:, :count], pre_all[:, at]).astype(bf16)
        store(f, 0).start()

        @pl.when(f > 0)
        def _():
            store(f - 1, 1).wait()

        outer[width : 2 * width, :] = dot(inner[:, count : 2 * count], act_all[:, at]).astype(bf16).T
        store(f, 1).start()
        return carry

    lax.fori_loop(0, steps, grads, 0)
    for copy in gate_copies:
        copy.wait()
    core_copies[0].wait_recv()
    token_cot = total[0].astype(f32) + core_in[0].astype(f32)
    for k in range(1, lanes):
        remote(part.at[0, 0], far_in.at[k - 1], back_sems.at[0, k - 1], back_sems.at[1, k - 1], {"expert": other}).wait_recv()
        token_cot = token_cot + far_in[k - 1].astype(f32)
    gates = gate_rows(me)
    pad = gates.shape[0]
    which = lax.broadcasted_iota(jnp.int32, gates.shape, 0)
    gate_cot = jnp.where(which == me, gate_out[me][0:1], 0.0)
    for k in range(1, experts):
        source = lax.rem(me + k, experts)
        gate_cot = gate_cot + jnp.where(which == source, gate_in[source][0:1], 0.0)
    logit_cot = gates * (gate_cot - jnp.sum(gates * gate_cot, axis=0, keepdims=True))
    three = jnp.concatenate(split3(logit_cot), axis=0)
    router_three = jnp.concatenate([router_ref[...]] * 3, axis=0)
    normed_cot = token_cot + dot(three, router_three, TN)
    router_grad = dot(three, nt[me])
    router_grad = router_grad[:pad] + router_grad[pad : 2 * pad] + router_grad[2 * pad :]
    now = hidden[...]
    scale = lax.rsqrt(jnp.mean(now * now, axis=1, keepdims=True) + EPSILON)
    unit = now * scale
    gained = normed_cot * gain_ref[...].reshape(1, width)
    hidden_cot = cot_ref[...].astype(f32) + scale * (gained - unit * jnp.mean(unit * gained, axis=1, keepdims=True))
    hidden_cot_ref[...] = hidden_cot
    mixed_cot_ref[...] = dot(w_output[...], hidden_cot.astype(bf16), NT).astype(bf16)
    small_ref[0:8, :] = jnp.broadcast_to(jnp.sum(unit * normed_cot, axis=0, keepdims=True), (8, width))
    small_ref[8:, :] = router_grad
    core_copies[1].wait_recv()
    base_ref[...] = now + (total[1].astype(f32) + core_in[1].astype(f32))
    store(steps - 1, 0).wait()
    store(steps - 1, 1).wait()
    for sc, pair, home in pairs[-2:]:
        @pl.when(core != sc)
        def _():
            for copy in pair:
                copy.wait_send()

        @pl.when(core == sc)
        def _():
            for copy in home:
                copy.wait_send()
    for copy in relays:
        copy.wait_send()
    for p in range(pieces):
        for copy in sent[p]:
            copy.wait_send()


def moe_pass(capacity, mixed_t, w_output, x, cot, gain, router, info, cots, inner, outer):
    rows, width = x.shape
    experts = cots.shape[0]
    lanes = experts // 2
    hidden_size = inner.shape[1]
    total = experts * capacity
    vmem = pl.BlockSpec(memory_space=pltpu.VMEM)
    hbm = pl.BlockSpec(memory_space=pl.ANY)
    dma = pltpu.SemaphoreType.DMA
    far = max(lanes - 1, 1)
    return pl.pallas_call(
        partial(moe_kernel, capacity),
        out_shape=[
            jax.ShapeDtypeStruct((rows, width), f32),
            jax.ShapeDtypeStruct((far, rows, width), bf16),
            jax.ShapeDtypeStruct((rows, width), f32),
            jax.ShapeDtypeStruct((width, rows), bf16),
            jax.ShapeDtypeStruct((8 + router.shape[0], width), f32),
            jax.ShapeDtypeStruct((width, hidden_size), bf16),
            jax.ShapeDtypeStruct((hidden_size, width), bf16),
        ],
        in_specs=[vmem] * 7 + [hbm] * 3,
        out_specs=[vmem] * 5 + [hbm] * 2,
        scratch_shapes=[
            pltpu.VMEM((experts, rows, width), bf16),
            pltpu.VMEM((2, rows, width), bf16),
            pltpu.VMEM((width, hidden_size), bf16),
            pltpu.VMEM((hidden_size, width), bf16),
            pltpu.VMEM((total, hidden_size), bf16),
            pltpu.VMEM((total, hidden_size), bf16),
            pltpu.VMEM((total, width), bf16),
            pltpu.VMEM((total, width), bf16),
            pltpu.VMEM((capacity, width), f32),
            pltpu.VMEM((capacity, width), f32),
            pltpu.VMEM((2, 2, rows, width), bf16),
            pltpu.VMEM((2, rows, width), bf16),
            pltpu.VMEM((2, rows, width), bf16),
            pltpu.VMEM((2, rows, width), bf16),
            pltpu.VMEM((far, rows, width), bf16),
            pltpu.VMEM((experts, 8, rows), f32),
            pltpu.VMEM((experts, 8, rows), f32),
            dma((2,)),
            dma((2,)),
            dma((2, 2)),
            dma((2, 2, far)),
            dma((2, far)),
            dma((2, 2, far)),
            dma((2, 2)),
            dma((2, far)),
            dma((2, experts - 1)),
            dma((2,)),
            pltpu.SemaphoreType.REGULAR,
        ],
        compiler_params=pltpu.CompilerParams(
            collective_id=1, has_side_effects=True, vmem_limit_bytes=65000 * 1024
        ),
        name="moe_pass",
    )(mixed_t, w_output, x, cot, gain, router, info, cots, inner, outer)


def bias_line(distance, table):
    far = jnp.full(distance.shape, BUCKETS // 2, jnp.int32)
    for limit in THRESHOLDS:
        far = far + jnp.where(distance >= limit, 1, 0)
    bucket = jnp.where(distance < BUCKETS // 2, distance, far)
    own = (distance >= 0) & (distance < THRESHOLDS[-1])
    which = lax.broadcasted_iota(jnp.int32, (BUCKETS, distance.shape[1]), 0)
    hot = jnp.where(own & (which == bucket), 1.0, 0.0).astype(bf16)
    last = table[:, BUCKETS - 1 :].astype(f32)
    return dot(table, hot) - jnp.where(own, last, 0.0)


def column_of(row):
    return jnp.broadcast_to(row, (128, row.shape[1])).T


def front_kernel(
    heads, n, rows, x_ref, gain_ref, wq, wk, wv, table_ref, segment_ref, routes_ref, order_ref, cot_hbm, win_hbm, wout_hbm,
    held, mixed, of_ref, lse_ref, normed_t, infos, cots_hbm, win_all, wout_all,
    made, given, qa, ka, vn, bias, s_ref, lines,
    held_sems, mixed_sems, near_sems, far_sems, relay_sems, info_sems, own_sems, line_sems, side_sems,
):
    size = 64
    group = heads * size
    width = n * group
    length = n * rows
    sides = lax.axis_size("dp")
    me = lax.axis_index("ctx")
    side = lax.axis_index("dp")
    experts = lax.axis_size("expert")
    expert = lax.axis_index("expert")
    barrier = pltpu.get_barrier_semaphore()
    for name, count, at in (("ctx", n, me), ("dp", sides, side), ("expert", experts, expert)):
        for k in range(1, count):
            pl.semaphore_signal(
                barrier, inc=1, device_id={name: lax.rem(at + k, count)}, device_id_type=pl.DeviceIdType.MESH
            )
    owns = [
        pltpu.make_async_copy(cot_hbm, cots_hbm.at[expert], own_sems.at[0]),
        pltpu.make_async_copy(win_hbm, win_all.at[me * sides + side], own_sems.at[1]),
        pltpu.make_async_copy(wout_hbm, wout_all.at[me * sides + side], own_sems.at[2]),
    ]
    for copy in owns:
        copy.start()
    pl.semaphore_wait(barrier, n + sides + experts - 3)
    shard = (win_hbm, wout_hbm)
    whole = (win_all, wout_all)

    def along(way, s, v):
        j = me - s if way == 0 else me + s
        to = me + 1 if way == 0 else me - 1
        at = j * sides + side
        source = shard[v] if s == 0 else whole[v].at[at]
        return remote(source, whole[v].at[at], line_sems.at[0, way, v, s], line_sems.at[1, way, v, s], {"ctx": to})

    def across(way, s, v):
        j = me - s if way == 0 else me + s
        at = j * sides + side
        source = shard[v] if s == 0 else whole[v].at[at]
        return [
            remote(
                source, whole[v].at[at], side_sems.at[0, way, v, k - 1, s], side_sems.at[1, way, v, k - 1, s],
                {"dp": lax.rem(side + k, sides)},
            )
            for k in range(1, sides)
        ]

    def holds(way, s):
        return me - s >= 0 if way == 0 else me + s < n

    def passes(way, s):
        return (me - s >= 0) & (me < n - 1) if way == 0 else (me + s < n) & (me > 0)

    def advance(s, v):
        for way in range(2):
            if s > 0:
                @pl.when(holds(way, s))
                def _():
                    along(way, s - 1, v).wait_recv()

            @pl.when(passes(way, s))
            def _():
                along(way, s, v).start()

            if s > 0:
                @pl.when(holds(way, s))
                def _():
                    for copy in across(way, s, v):
                        copy.start()

    for v in range(2):
        for copy in across(0, 0, v):
            copy.start()
        advance(0, v)
    sent = gather_start(cot_hbm, cots_hbm, near_sems, far_sems)

    x = x_ref[...].astype(f32)
    normed = x * lax.rsqrt(jnp.mean(x * x, axis=1, keepdims=True) + EPSILON) * gain_ref[...].reshape(1, width)
    normed = normed.astype(bf16)
    held_copies = []
    here = pl.ds(pl.multiple_of(me * group, 16), group)
    seg = jnp.broadcast_to(segment_ref[...].astype(f32), (16, rows)).astype(bf16)
    made[3, 0:16, :] = seg
    held[me, 3 * group : 3 * group + 16, :] = seg
    for kind, weight in enumerate((wq, wk, wv)):
        made[kind] = dot(normed, weight[...]).astype(bf16).T
        for k in range(1, n):
            to = lax.rem(me + k, n)
            copy = remote(
                made.at[kind, pl.ds(pl.multiple_of(to * group, 16), group)],
                held.at[me, kind * group : (kind + 1) * group],
                held_sems.at[0, kind, k - 1], held_sems.at[1, kind, k - 1], {"ctx": to},
            )
            copy.start()
            held_copies.append(copy)
        held[me, kind * group : (kind + 1) * group, :] = made[kind, here, :]
    for k in range(1, n):
        copy = remote(
            made.at[3, 0:16], held.at[me, 3 * group : 3 * group + 16], held_sems.at[0, 3, k - 1], held_sems.at[1, 3, k - 1],
            {"ctx": lax.rem(me + k, n)},
        )
        copy.start()
        held_copies.append(copy)
    normed_t[...] = normed.T

    order_row = order_ref[...].astype(f32)
    before = jnp.where(column_of(order_row)[:, 0:1] < order_row, 1.0, 0.0).astype(bf16)
    kinds = 16
    which = lax.broadcasted_iota(jnp.int32, (kinds, rows), 0)
    chosen = [routes_ref[c : c + 1, :] for c in range(2)]
    hot = [jnp.where(which == c, 1.0, 0.0) for c in chosen]
    ahead = [dot(h.astype(bf16), before) for h in hot]
    firsts = jnp.sum(hot[0], axis=1, keepdims=True)
    slots = [jnp.sum(hot[0] * ahead[0], axis=0, keepdims=True), jnp.sum(hot[1] * (ahead[1] + firsts), axis=0, keepdims=True)]
    infos[expert] = jnp.concatenate(chosen + [s.astype(jnp.int32) for s in slots] + [jnp.zeros((4, rows), jnp.int32)], axis=0)
    info_copies = [
        remote(infos.at[expert], infos.at[expert], info_sems.at[0, k - 1], info_sems.at[1, k - 1], {"expert": lax.rem(expert + k, experts)})
        for k in range(1, experts)
    ]
    for copy in info_copies:
        copy.start()
    lines[...] = bias_line(BLK - lax.broadcasted_iota(jnp.int32, (1, 2 * BLK), 1), table_ref[...])

    advance(1, 0)
    advance(1, 1)
    for copy in held_copies:
        copy.wait_recv()

    def mixed_copy(h, k):
        to = lax.rem(me + k, n)
        base = pl.multiple_of(h * size, size)
        return remote(
            given.at[to, pl.ds(base, size)], mixed.at[pl.ds(pl.multiple_of(me * group + base, 16), size)],
            mixed_sems.at[0, h, k - 1], mixed_sems.at[1, h, k - 1], {"ctx": to},
        )

    def head(h, carry):
        base = pl.multiple_of(h * size, size)
        for s in range(n):
            at = slice(s * rows, (s + 1) * rows)
            q = held[s, pl.ds(base, size), :]
            k = held[s, pl.ds(base + group, size), :]
            v = held[s, pl.ds(base + 2 * group, size), :]
            mask, hot = seg_mask_rows(held[s, 3 * group : 3 * group + 16, :])
            zeros = jnp.zeros((48, rows), bf16)
            qa[at, :] = jnp.concatenate([q * jnp.asarray(0.125, bf16), mask, zeros], axis=0).T
            ka[:, at] = jnp.concatenate([k, hot, zeros], axis=0)
            vn[at, :] = jnp.concatenate([v, jnp.zeros((64, rows), bf16)], axis=0).T
        line = jnp.broadcast_to(lines[pl.ds(me * heads + h, 1), :], (BLK, 2 * BLK))
        rolled = pltpu.roll(line, 0, 1, stride=1, stride_axis=0)
        r = lax.broadcasted_iota(jnp.int32, (BLK, 2 * BLK), 0)
        c = lax.broadcasted_iota(jnp.int32, (BLK, 2 * BLK), 1)
        bias[...] = jnp.where(c - r > BLK, NEG, rolled)
        for t in range(length // BLK):
            qt = qa[t * BLK : (t + 1) * BLK, :]
            near0 = max(t - 1, 0) * BLK
            end = (t + 1) * BLK
            chunks = [(near0, end)] + [(a, min(a + 2 * BLK, near0)) for a in range(0, near0, 2 * BLK)]
            top = None
            for a, b in chunks:
                s = dot(qt, ka[:, a:b])
                if a == near0:
                    s = s + bias[:, 2 * BLK - (b - a) :]
                s_ref[:, a:b] = s
                part = s[:, :128]
                for i in range(1, (b - a) // 128):
                    part = jnp.maximum(part, s[:, i * 128 : (i + 1) * 128])
                top = part if top is None else jnp.maximum(top, part)
            m = jnp.max(top, axis=1, keepdims=True)
            total = None
            o = None
            for a, b in chunks:
                p = jnp.exp(s_ref[:, a:b] - m)
                part = p[:, :128]
                for i in range(1, (b - a) // 128):
                    part = part + p[:, i * 128 : (i + 1) * 128]
                total = part if total is None else total + part
                u = dot(p.astype(bf16), vn[a:b, :])
                o = u if o is None else o + u
            l = jnp.sum(total, axis=1, keepdims=True)
            o = o / l
            lane = lax.broadcasted_iota(jnp.int32, (BLK, 128), 1)
            o = jnp.where(lane == 64, m + jnp.log(l), o)
            ot = o.T
            src, off = (t * BLK) // rows, (t * BLK) % rows
            given[src, pl.ds(base, size), off : off + BLK] = ot[:size].astype(bf16)
            of_ref[pl.ds(base, size), t * BLK : (t + 1) * BLK] = ot[:size]
            lse_ref[pl.ds(h, 1), t * BLK : (t + 1) * BLK] = ot[size : size + 1]
        for k in range(1, n):
            mixed_copy(h, k).start()
        mixed[pl.ds(pl.multiple_of(me * group + base, 16), size), :] = given[me, pl.ds(base, size), :]

        @pl.when(h == 0)
        def _():
            advance(2, 0)

        @pl.when(h == 1)
        def _():
            advance(2, 1)

        return carry

    lax.fori_loop(0, heads, head, 0)
    for s in range(3, n):
        for v in range(2):
            advance(s, v)
    relays = []
    for k in range(1, experts // 2):
        sent[k].wait_recv()
        passed = relay(k, cots_hbm, relay_sems)
        passed.start()
        relays.append(passed)
    sent[0].wait_recv()
    for h in range(heads):
        for k in range(1, n):
            mixed_copy(h, k).wait()
    for copy in held_copies + sent:
        copy.wait_send()
    for copy in relays + info_copies + owns:
        copy.wait()
    for v in range(2):
        for s in range(n):
            for way in range(2):
                @pl.when(passes(way, s))
                def _():
                    along(way, s, v).wait_send()

                if s > 0 or way == 0:
                    @pl.when(holds(way, s))
                    def _():
                        for copy in across(way, s, v):
                            copy.wait()


def front_pass(x, gain, wq, wk, wv, table, segments, routes, order, cot, win, wout):
    rows, width = x.shape
    n = lax.axis_size("ctx")
    sides = lax.axis_size("dp")
    experts = lax.axis_size("expert")
    heads = table.shape[0] // n
    group = heads * 64
    length = n * rows
    blocks = n * sides
    vmem = pl.BlockSpec(memory_space=pltpu.VMEM)
    hbm = pl.BlockSpec(memory_space=pl.ANY)
    dma = pltpu.SemaphoreType.DMA
    far = max(experts // 2 - 1, 1)
    some = max(sides - 1, 1)
    return pl.pallas_call(
        partial(front_kernel, heads, n, rows),
        out_shape=[
            jax.ShapeDtypeStruct((n, 3 * group + 16, rows), bf16),
            jax.ShapeDtypeStruct((width, rows), bf16),
            jax.ShapeDtypeStruct((group, length), f32),
            jax.ShapeDtypeStruct((heads, length), f32),
            jax.ShapeDtypeStruct((width, rows), bf16),
            jax.ShapeDtypeStruct((experts, 8, rows), jnp.int32),
            jax.ShapeDtypeStruct((experts, rows, width), bf16),
            jax.ShapeDtypeStruct((blocks,) + win.shape, bf16),
            jax.ShapeDtypeStruct((blocks,) + wout.shape, bf16),
        ],
        in_specs=[vmem] * 9 + [hbm] * 3,
        out_specs=[vmem] * 6 + [hbm] * 3,
        scratch_shapes=[
            pltpu.VMEM((4, width, rows), bf16),
            pltpu.VMEM((n, group, rows), bf16),
            pltpu.VMEM((length, 128), bf16),
            pltpu.VMEM((128, length), bf16),
            pltpu.VMEM((length, 128), bf16),
            pltpu.VMEM((BLK, 2 * BLK), f32),
            pltpu.VMEM((BLK, length), f32),
            pltpu.VMEM((table.shape[0], 2 * BLK), f32),
            dma((2, 4, n - 1)),
            dma((2, heads, n - 1)),
            dma((2,)),
            dma((2, far)),
            dma((2, far)),
            dma((2, experts - 1)),
            dma((3,)),
            dma((2, 2, 2, n)),
            dma((2, 2, 2, some, n)),
        ],
        compiler_params=pltpu.CompilerParams(
            collective_id=2, has_side_effects=True, vmem_limit_bytes=60 * 1024 * 1024
        ),
        name="front_pass",
    )(x, gain, wq, wk, wv, table, segments, routes, order, cot, win, wout)


def line_order(n):
    order = []
    for i in range((n + 1) // 2):
        order.append(n - 1 - i)
        if i != n - 1 - i:
            order.append(i)
    return order


def line_scatter(n, own, right, left, right_sems, left_sems, ready):
    me = lax.axis_index("ctx")
    items = {}
    for j in line_order(n):
        for r in range(j):
            items.setdefault(ready[j] + r, []).append((0, r, j))
        for r in range(n - 1, j, -1):
            items.setdefault(ready[j] + n - 1 - r, []).append((1, r, j))
    steps = max(items) + 1

    def pass_on(way, r, j):
        taken, sems = (right, right_sems) if way == 0 else (left, left_sems)
        first = 0 if way == 0 else n - 1
        return remote(
            own.at[j] if r == first else taken.at[j], taken.at[j], sems.at[0, j], sems.at[1, j],
            {"ctx": r + 1 if way == 0 else r - 1},
        )

    def advance(step):
        for way, r, j in items.get(step, []):
            @pl.when(me == r)
            def _():
                copy = pass_on(way, r, j)
                if r != (0 if way == 0 else n - 1):
                    taken = right if way == 0 else left
                    copy.wait_recv()
                    taken[j] = (taken[j].astype(f32) + own[j].astype(f32)).astype(bf16)
                copy.start()

    def finish(out):
        for j in range(n):
            @pl.when(me == j)
            def _():
                total = own[j].astype(f32)
                if j > 0:
                    pass_on(0, j - 1, j).wait_recv()
                    total = total + right[j].astype(f32)
                if j < n - 1:
                    pass_on(1, j + 1, j).wait_recv()
                    total = total + left[j].astype(f32)
                out[...] = total.astype(bf16)

    def drain():
        for step in range(steps):
            for way, r, j in items.get(step, []):
                @pl.when(me == r)
                def _():
                    pass_on(way, r, j).wait_send()

    return advance, finish, drain, steps


def back_kernel(
    heads, n, rows, x_ref, do_ref, table_ref, of_ref, lse_ref, base_ref, far_ref, gin_hbm, gout_hbm,
    cots_ref, diag_ref, ein_ref, own_b, out_ref,
    do_in, g_ref, qa, ka, va, da, qn, dn, bias, dq, gsum,
    own_a, side_a, side_b, right_a, left_a,
    do_sems, out_sems, own_sems, side_sems, right_sems, left_sems, lines, far_in, far_sems,
):
    size = 64
    group = heads * size
    length = n * rows
    sides = lax.axis_size("dp")
    me = lax.axis_index("ctx")
    side = lax.axis_index("dp")
    barrier, peers = greet(("ctx", "dp", "expert"))
    order = line_order(n)
    advance, finish, drain, steps = line_scatter(
        n, own_a, right_a, left_a, right_sems, left_sems, {j: i for i, j in enumerate(order)}
    )
    loads = {}
    for j in order:
        at = j * sides + side
        loads[j] = [
            pltpu.make_async_copy(gin_hbm.at[at], own_a.at[j], own_sems.at[0, j]),
            pltpu.make_async_copy(gout_hbm.at[at], own_b.at[j], own_sems.at[1, j]),
        ]
        for copy in loads[j]:
            copy.start()
    pl.semaphore_wait(barrier, peers)
    lanes, lane, core = expert_split()
    homes = [
        remote(
            far_ref.at[k - 1], far_in.at[k - 1], far_sems.at[0, k - 1], far_sems.at[1, k - 1],
            {"expert": lax.rem(lane - k + lanes, lanes) * 2 + core},
        )
        for k in range(1, lanes)
    ]
    for copy in homes:
        copy.start()
    lines[...] = bias_line(lax.broadcasted_iota(jnp.int32, (1, 2 * BLK), 1), table_ref[...])
    arriving = []
    for k in range(1, n):
        to = lax.rem(me + k, n)
        copy = remote(
            do_ref.at[pl.ds(pl.multiple_of(to * group, 16), group)], do_in.at[me], do_sems.at[0, k - 1], do_sems.at[1, k - 1], {"ctx": to}
        )
        copy.start()
        arriving.append(copy)
    beside = {}
    for v, gone, taken in ((0, gin_hbm, side_a), (1, gout_hbm, side_b)):
        for j in order:
            beside[v, j] = []
            for k in range(1, sides):
                to = lax.rem(side + k, sides)
                beside[v, j].append(
                    remote(
                        gone.at[j * sides + to], taken.at[k - 1, j],
                        side_sems.at[0, v, k - 1, j], side_sems.at[1, v, k - 1, j], {"dp": to},
                    )
                )
                beside[v, j][-1].start()

    def sum_sides(v, j):
        own, taken = ((own_a, side_a), (own_b, side_b))[v]
        loads[j][v].wait()
        total = own[j].astype(f32)
        for k in range(1, sides):
            beside[v, j][k - 1].wait_recv()
            total = total + taken[k - 1, j].astype(f32)
        own[j] = total.astype(bf16)

    do_in[me] = do_ref[pl.ds(pl.multiple_of(me * group, 16), group), :]

    for copy in arriving:
        copy.wait_recv()

    def out_copy(h, kind, k):
        to = lax.rem(me + k, n)
        base = pl.multiple_of(h * size, size)
        return remote(
            g_ref.at[to, pl.ds(kind * group + base, size)],
            cots_ref.at[pl.ds(pl.multiple_of(kind * n * group + me * group + base, 16), size)],
            out_sems.at[0, h, kind, k - 1],
            out_sems.at[1, h, kind, k - 1],
            {"ctx": to},
        )

    def head(h, carry):
        base = pl.multiple_of(h * size, size)
        for s in range(n):
            at = slice(s * rows, (s + 1) * rows)
            q = x_ref[s, pl.ds(base, size), :] * jnp.asarray(0.125, bf16)
            k = x_ref[s, pl.ds(base + group, size), :]
            v = x_ref[s, pl.ds(base + 2 * group, size), :]
            d = do_in[s, pl.ds(base, size), :]
            seg = x_ref[s, 3 * group : 3 * group + 16, :]
            mask, hot = seg_mask_rows(seg)
            which = lax.broadcasted_iota(jnp.int32, (16, rows), 0)

            def rows3(vec):
                hi, mid, lo = split3(jnp.broadcast_to(vec, (16, rows)))
                return jnp.where(which == 0, hi, jnp.where(which == 1, mid, jnp.where(which == 2, lo, jnp.zeros((), bf16))))

            ones = jnp.where(which < 3, 1.0, 0.0).astype(bf16)
            zeros = jnp.zeros((32, rows), bf16)
            zeros48 = jnp.zeros((48, rows), bf16)
            lse = lse_ref[pl.ds(h, 1), at]
            delta = jnp.sum(of_ref[pl.ds(base, size), at] * d.astype(f32), axis=0, keepdims=True)
            qt = jnp.concatenate([q, mask, rows3(-lse), zeros], axis=0)
            qa[:, at] = qt
            qn[at, :] = qt.T
            ka[at, :] = jnp.concatenate([k, hot, ones, zeros], axis=0).T
            dt = jnp.concatenate([d, rows3(-delta), zeros48], axis=0)
            da[:, at] = dt
            dn[at, :] = dt.T
            va[at, :] = jnp.concatenate([v, ones, zeros48], axis=0).T
        line = jnp.broadcast_to(lines[pl.ds(me * heads + h, 1), :], (BLK, 2 * BLK))
        rolled = pltpu.roll(line, 0, 1, stride=1, stride_axis=0)
        r = lax.broadcasted_iota(jnp.int32, (BLK, 2 * BLK), 0)
        c = lax.broadcasted_iota(jnp.int32, (BLK, 2 * BLK), 1)
        bias[...] = jnp.where(c < r, NEG, rolled)
        gsum[...] = jnp.zeros_like(gsum)
        for j in range(length // BLK):
            a0 = j * BLK
            kj = ka[a0 : a0 + BLK, :]
            vj = va[a0 : a0 + BLK, :]
            src, off = a0 // rows, a0 % rows
            kt = x_ref[src, pl.ds(base + group, size), off : off + BLK]
            dk = dv = None
            for a in range(a0, length, 2 * BLK):
                b = min(a + 2 * BLK, length)
                s = dot(kj, qa[:, a:b])
                if a == a0:
                    s = s + bias[:, : b - a]
                p = jnp.exp(s)
                ds = p * dot(vj, da[:, a:b])
                if a == a0:
                    gsum[:, : b - a] += ds
                p_low, ds_low = p.astype(bf16), ds.astype(bf16)
                u = dot(p_low, dn[a:b, :])
                dv = u if dv is None else dv + u
                u = dot(ds_low, qn[a:b, :])
                dk = u if dk is None else dk + u
                u = dot(kt, ds_low)
                if j == 0:
                    dq[:, a:b] = u
                else:
                    dq[:, a:b] += u
            g_ref[src, pl.ds(base + group, size), off : off + BLK] = dk.T[:size].astype(bf16)
            g_ref[src, pl.ds(base + 2 * group, size), off : off + BLK] = dv.T[:size].astype(bf16)
        for s in range(n):
            g_ref[s, pl.ds(base, size), :] = (dq[:, s * rows : (s + 1) * rows] * 0.125).astype(bf16)
        for kind in range(3):
            for k in range(1, n):
                out_copy(h, kind, k).start()
            cots_ref[pl.ds(pl.multiple_of(kind * n * group + me * group + base, 16), size), :] = g_ref[
                me, pl.ds(kind * group + base, size), :
            ]
        eight = gsum[0:8, :]
        for i in range(1, BLK // 8):
            eight = eight + pltpu.roll(gsum[8 * i : 8 * i + 8, :], 2 * BLK - 8 * i, 1)
        line = eight[0:1]
        for i in range(1, 8):
            line = line + pltpu.roll(eight, 2 * BLK - i, 1)[i : i + 1]
        diag_ref[pl.ds(h, 1), :] = line
        return carry

    lax.fori_loop(0, 1, head, 0)
    sum_sides(0, order[0])
    advance(0)
    lax.fori_loop(1, heads, head, 0)
    for step in range(1, steps):
        if step < n:
            sum_sides(0, order[step])
        advance(step)
        if step >= n and step - n < n:
            sum_sides(1, order[step - n])
    for i in range(max(steps - n, 0), n):
        sum_sides(1, order[i])
    mixture = base_ref[...]
    for k in range(1, lanes):
        homes[k - 1].wait()
        mixture = mixture + far_in[k - 1].astype(f32)
    out_ref[...] = mixture.astype(bf16)
    finish(ein_ref)
    for h in range(heads):
        for kind in range(3):
            for k in range(1, n):
                out_copy(h, kind, k).wait()
    for copy in arriving:
        copy.wait_send()
    for copies in beside.values():
        for copy in copies:
            copy.wait_send()
    drain()


def back_pass(x, do, table, of, lse, base, far, gin, gout):
    n, depth, rows = x.shape
    heads = table.shape[0] // n
    group = heads * 64
    length = n * rows
    sides = lax.axis_size("dp")
    _, high_a, wide_a = gin.shape
    _, high_b, wide_b = gout.shape
    vmem = pl.BlockSpec(memory_space=pltpu.VMEM)
    hbm = pl.BlockSpec(memory_space=pl.ANY)
    dma = pltpu.SemaphoreType.DMA
    some = max(sides - 1, 1)
    return pl.pallas_call(
        partial(back_kernel, heads, n, rows),
        out_shape=[
            jax.ShapeDtypeStruct((3 * n * group, rows), bf16),
            jax.ShapeDtypeStruct((heads, 2 * BLK), f32),
            jax.ShapeDtypeStruct((high_a, wide_a), bf16),
            jax.ShapeDtypeStruct((n, high_b, wide_b), bf16),
            jax.ShapeDtypeStruct(base.shape, bf16),
        ],
        in_specs=[vmem] * 7 + [hbm] * 2,
        out_specs=[vmem] * 5,
        scratch_shapes=[
            pltpu.VMEM((n, group, rows), bf16),
            pltpu.VMEM((n, 3 * group, rows), bf16),
            pltpu.VMEM((128, length), bf16),
            pltpu.VMEM((length, 128), bf16),
            pltpu.VMEM((length, 128), bf16),
            pltpu.VMEM((128, length), bf16),
            pltpu.VMEM((length, 128), bf16),
            pltpu.VMEM((length, 128), bf16),
            pltpu.VMEM((BLK, 2 * BLK), f32),
            pltpu.VMEM((64, length), f32),
            pltpu.VMEM((BLK, 2 * BLK), f32),
            pltpu.VMEM((n, high_a, wide_a), bf16),
            pltpu.VMEM((some, n, high_a, wide_a), bf16),
            pltpu.VMEM((some, n, high_b, wide_b), bf16),
            pltpu.VMEM((n, high_a, wide_a), bf16),
            pltpu.VMEM((n, high_a, wide_a), bf16),
            dma((2, n - 1)),
            dma((2, heads, 3, n - 1)),
            dma((2, n)),
            dma((2, 2, some, n)),
            dma((2, n)),
            dma((2, n)),
            pltpu.VMEM((table.shape[0], 2 * BLK), f32),
            pltpu.VMEM(far.shape, bf16),
            dma((2, far.shape[0])),
        ],
        compiler_params=pltpu.CompilerParams(
            collective_id=3, has_side_effects=True, vmem_limit_bytes=60 * 1024 * 1024
        ),
        name="back_pass",
    )(x, do, table, of, lse, base, far, gin, gout)


def add_all(parts):
    return functools.reduce(lambda a, b: a + b, parts)


def axis_stages():
    experts = lax.axis_size("expert")
    me = lax.axis_index("expert")
    core, lane = lax.rem(me, 2), lax.div(me, 2)
    return {
        "core": (2, core, lambda j: {"expert": lane * 2 + j}),
        "lane": (experts // 2, lane, lambda j: {"expert": j * 2 + core}),
        "dp": (lax.axis_size("dp"), lax.axis_index("dp"), lambda j: {"dp": j}),
        "ctx": (lax.axis_size("ctx"), lax.axis_index("ctx"), lambda j: {"ctx": j}),
    }


ORDERS = (("core", "lane", "dp", "ctx"), ("core", "dp", "lane", "ctx"))
SLICES = 2


def sum_plan(sizes, rows):
    plans = []
    for order in ORDERS:
        length, plan = rows // 2, []
        for name in order:
            count = sizes[name]
            split = length % count == 0 and (length // count) % 16 == 0
            plan.append((name, count, length, split))
            if split:
                length = length // count
        plans.append(plan)
    return plans


def received_rows(plans):
    return [
        [(count - 1) * (length // count if split else length) for (_, count, length, split) in plan]
        for plan in plans
    ]


def sizes_of():
    return {
        "core": 2,
        "lane": lax.axis_size("expert") // 2,
        "dp": lax.axis_size("dp"),
        "ctx": lax.axis_size("ctx"),
    }


def tail_kernel(
    plans, normed_t, cots, mixed_t, wq, wk, wv, x_ref, gain_ref, hidden_cot_ref, moe_small_ref, diag_ref, sums_ref,
    grads_ref, input_grad_ref, small_out_ref, eout_ref,
    acc, whole, taken_a, taken_b, small, small_taken, send, recv, back_send, back_recv, small_send, small_recv,
    right, left, right_sems, left_sems,
):
    stages = axis_stages()
    width = wq.shape[0]
    rows = x_ref.shape[0]
    barrier = pltpu.get_barrier_semaphore()
    peers = 0
    for name, (count, me, at) in stages.items():
        for k in range(1, count):
            pl.semaphore_signal(barrier, inc=1, device_id=at(lax.rem(me + k, count)), device_id_type=pl.DeviceIdType.MESH)
            peers += 1

    def make(k):
        if k < 3:
            acc[k * width : (k + 1) * width, :] = dot(
                normed_t[...], cots[k * width : (k + 1) * width, :], NT
            ).astype(bf16)
        else:
            acc[3 * width :, :] = dot(mixed_t[...], hidden_cot_ref[...].astype(bf16)).astype(bf16)

    taken = (taken_a, taken_b)
    half = 2 * width
    piece = width // SLICES
    parts = [(h, c) for c in range(SLICES) for h in range(2)]
    spans = {}
    for part in parts:
        spans[part] = [part[0] * half]

    def columns(part):
        return pl.ds(part[1] * piece, piece)

    def rows_at(start, size):
        return pl.ds(pl.multiple_of(start, 16), size)

    flying = {}

    def send_stage(part, step):
        h, c = part
        name, count, length, split = plans[h][step]
        _, me, at = stages[name]
        start = spans[part][-1]
        size = length // count if split else length
        base = sum(received[h][:step])
        copies = []
        for k in range(1, count):
            peer = lax.rem(me + k, count)
            copies.append(
                pltpu.make_async_remote_copy(
                    src_ref=acc.at[rows_at(start + peer * size if split else start, size), columns(part)],
                    dst_ref=taken[h].at[pl.ds(base + (k - 1) * size, size), columns(part)],
                    send_sem=send.at[h * SLICES + c, step, k - 1],
                    recv_sem=recv.at[h * SLICES + c, step, k - 1],
                    device_id=at(peer),
                    device_id_type=pl.DeviceIdType.MESH,
                )
            )
        for copy in copies:
            copy.start()
        flying[part] = copies

    def add_stage(part, step):
        h, c = part
        name, count, length, split = plans[h][step]
        _, me, at = stages[name]
        size = length // count if split else length
        start = spans[part][-1] + me * size if split else spans[part][-1]
        base = sum(received[h][:step])
        for copy in flying[part]:
            copy.wait()
        total = acc[rows_at(start, size), columns(part)].astype(f32)
        for k in range(1, count):
            total = total + taken[h][base + (k - 1) * size : base + k * size, columns(part)].astype(f32)
        if step == len(plans[h]) - 1:
            whole[rows_at(start, size), columns(part)] = total.astype(bf16)
        else:
            acc[rows_at(start, size), columns(part)] = total.astype(bf16)
        spans[part].append(start)

    def give_stage(part, step):
        h, c = part
        name, count, length, split = plans[h][step]
        if not split:
            flying[part] = []
            return
        _, me, at = stages[name]
        size = length // count
        start = spans[part][step + 1]
        copies = []
        for k in range(1, count):
            peer = lax.rem(me + k, count)
            copies.append(
                pltpu.make_async_remote_copy(
                    src_ref=whole.at[rows_at(start, size), columns(part)],
                    dst_ref=whole.at[rows_at(start, size), columns(part)],
                    send_sem=back_send.at[h * SLICES + c, step, k - 1],
                    recv_sem=back_recv.at[h * SLICES + c, step, k - 1],
                    device_id=at(peer),
                    device_id_type=pl.DeviceIdType.MESH,
                )
            )
        for copy in copies:
            copy.start()
        flying[part] = copies

    n = sums_ref.shape[0]
    advance, finish, drain, line_steps = line_scatter(n, sums_ref, right, left, right_sems, left_sems, [0] * n)
    received = received_rows(plans)
    make(2)
    make(3)
    pl.semaphore_wait(barrier, peers)
    for c in range(SLICES):
        send_stage((1, c), 0)
    advance(0)
    make(0)
    make(1)
    for c in range(SLICES):
        send_stage((0, c), 0)
    parts = [(1, 0), (0, 0), (1, 1), (0, 1)]

    turned = dot(wq[...], cots[:width, :]) + dot(wk[...], cots[width : 2 * width, :]) + dot(wv[...], cots[2 * width :, :])
    cot = turned.T
    x = x_ref[...].astype(f32)
    gain = gain_ref[...].reshape(1, width)
    scale = lax.rsqrt(jnp.mean(x * x, axis=1, keepdims=True) + EPSILON)
    unit = x * scale
    gained = cot * gain
    input_grad_ref[...] = hidden_cot_ref[...] + scale * (gained - unit * jnp.mean(unit * gained, axis=1, keepdims=True))
    gain_grad = jnp.sum(unit * cot, axis=0, keepdims=True)
    which = lax.broadcasted_iota(jnp.int32, (8, width), 0)
    low = jnp.where(which == 0, gain_grad, jnp.where(which == 1, moe_small_ref[0:8, :], 0.0))
    distance = lax.broadcasted_iota(jnp.int32, (2 * BLK, width), 0)
    lane = lax.broadcasted_iota(jnp.int32, (2 * BLK, width), 1)
    far = jnp.full(distance.shape, BUCKETS // 2, jnp.int32)
    for limit in THRESHOLDS:
        far = far + jnp.where(distance >= limit, 1, 0)
    bucket = jnp.where(distance < BUCKETS // 2, distance, far)
    own = distance < THRESHOLDS[-1]
    which = lax.broadcasted_iota(jnp.int32, (8, width), 0)
    lane_row = lax.broadcasted_iota(jnp.int32, (8, width), 1)
    heads = diag_ref.shape[0]
    for h in range(heads):
        at = lax.axis_index("ctx") * heads + h
        start = lax.div(at, 6) * 128
        hot = jnp.where(own & (bucket + start == lane), 1.0, 0.0).astype(bf16)
        three = split3(jnp.broadcast_to(diag_ref[h : h + 1, :], (16, 2 * BLK)))
        near = (dot(three[0], hot) + dot(three[1], hot) + dot(three[2], hot))[0:1]
        near = jnp.where(lane_row[0:1] == start + BUCKETS - 1, -jnp.sum(near, axis=1, keepdims=True), near)
        low = low + jnp.where(which == 2 + lax.rem(at, 6), near, 0.0)
    small[0:8, :] = low
    small[8:16, :] = moe_small_ref[8:16, :]

    def send_small(step):
        name = ORDERS[0][step]
        count, me, at = stages[name]
        base = sum(stages[n][0] - 1 for n in ORDERS[0][:step])
        copies = [
            pltpu.make_async_remote_copy(
                src_ref=small,
                dst_ref=small_taken.at[base + k - 1],
                send_sem=small_send.at[base + k - 1],
                recv_sem=small_recv.at[base + k - 1],
                device_id=at(lax.rem(me + k, count)),
                device_id_type=pl.DeviceIdType.MESH,
            )
            for k in range(1, count)
        ]
        for copy in copies:
            copy.start()
        flying["small"] = copies

    def add_small(step):
        base = sum(stages[n][0] - 1 for n in ORDERS[0][:step])
        for copy in flying["small"]:
            copy.wait()
        total = small[...]
        for k in range(len(flying["small"])):
            total = total + small_taken[base + k]
        small[...] = total

    last = len(ORDERS[0])
    send_small(0)
    for step in range(last):
        for part in parts:
            add_stage(part, step)
            if step + 1 < last:
                send_stage(part, step + 1)
            else:
                give_stage(part, step)
        add_small(step)
        if step + 1 < last:
            send_small(step + 1)
        advance(step + 1)
    small_out_ref[...] = small[...]
    for step in range(last - 1, -1, -1):
        for part in parts:
            for copy in flying[part]:
                copy.wait()
            if step > 0:
                give_stage(part, step - 1)
    for step in range(last + 1, line_steps):
        advance(step)
    finish(eout_ref)
    drain()
    grads_ref[...] = whole[...]


def tail_pass(normed_t, cots, mixed_t, wq, wk, wv, x, gain, hidden_cot, moe_small, diag, sums):
    rows, width = x.shape
    sizes = sizes_of()
    plans = sum_plan(sizes, 4 * width)
    received = [sum(r) for r in received_rows(plans)]
    most = max(sizes.values()) - 1
    few = sum(n - 1 for n in sizes.values())
    small = jax.ShapeDtypeStruct((16, width), f32)
    return pl.pallas_call(
        partial(tail_kernel, plans),
        out_shape=[
            jax.ShapeDtypeStruct((4 * width, width), bf16),
            jax.ShapeDtypeStruct((rows, width), f32),
            jax.ShapeDtypeStruct(small.shape, f32),
            jax.ShapeDtypeStruct(sums.shape[1:], bf16),
        ],
        in_specs=[pl.BlockSpec(memory_space=pltpu.VMEM)] * 12,
        out_specs=[pl.BlockSpec(memory_space=pltpu.VMEM)] * 4,
        scratch_shapes=[
            pltpu.VMEM((4 * width, width), bf16),
            pltpu.VMEM((4 * width, width), bf16),
            pltpu.VMEM((received[0], width), bf16),
            pltpu.VMEM((received[1], width), bf16),
            pltpu.VMEM(small.shape, f32),
            pltpu.VMEM((few,) + small.shape, f32),
            pltpu.SemaphoreType.DMA((2 * SLICES, 4, most)),
            pltpu.SemaphoreType.DMA((2 * SLICES, 4, most)),
            pltpu.SemaphoreType.DMA((2 * SLICES, 4, most)),
            pltpu.SemaphoreType.DMA((2 * SLICES, 4, most)),
            pltpu.SemaphoreType.DMA((few,)),
            pltpu.SemaphoreType.DMA((few,)),
            pltpu.VMEM(sums.shape, bf16),
            pltpu.VMEM(sums.shape, bf16),
            pltpu.SemaphoreType.DMA((2, sums.shape[0])),
            pltpu.SemaphoreType.DMA((2, sums.shape[0])),
        ],
        compiler_params=pltpu.CompilerParams(
            collective_id=0, has_side_effects=True, vmem_limit_bytes=56 * 1024 * 1024
        ),
        name="tail_pass",
    )(normed_t, cots, mixed_t, wq, wk, wv, x, gain, hidden_cot, moe_small, diag, sums)


def local(
    layer_input,
    cotangent,
    norm_gain_one,
    w_query,
    w_key,
    w_value,
    w_output,
    rel_table,
    norm_gain_two,
    w_router,
    w_expert_in,
    w_expert_out,
    segment_ids,
    routes,
    priority,
):
    rows, width = layer_input.shape[1:]
    heads = rel_table.shape[0]
    shards = lax.axis_size("ctx")
    experts = lax.axis_size("expert")
    capacity = min(rows, 5 * rows // (2 * experts))
    blocks = shards * lax.axis_size("dp")

    def padded(array):
        return jnp.pad(array, ((0, 0), (0, -array.shape[1] % 16), (0, 0)))

    held, mixed_t, attended_whole, lse, normed_t, info_all, cots_all, inner_weight, outer_weight = front_pass(
        layer_input[0], norm_gain_one, w_query, w_key, w_value, rel_table, segment_ids, routes[0].T, priority[0],
        cotangent[0], padded(w_expert_in)[0], padded(w_expert_out)[0],
    )
    inner_weight = inner_weight[:, : w_expert_in.shape[1]].reshape(width, -1)
    outer_weight = outer_weight[:, : w_expert_out.shape[1]].reshape(-1, width)
    router_t = jnp.pad(w_router.T, ((0, 16 - experts), (0, 0)))
    base, far, hidden_cot, mixed_cot, moe_small, inner_grad, outer_grad = moe_pass(
        capacity, mixed_t, w_output, layer_input[0], cotangent[0], norm_gain_two, router_t, info_all, cots_all, inner_weight, outer_weight
    )

    def cut(array):
        return padded(array.reshape(blocks, array.shape[0] // blocks, array.shape[1]))

    cots, diagonals, expert_in_grad, expert_out_sums, layer_output = back_pass(
        held, mixed_cot, rel_table, attended_whole, lse, base, far, cut(inner_grad), cut(outer_grad)
    )
    expert_in_grad = expert_in_grad[None, : w_expert_in.shape[1]]
    large, input_grad, small, expert_out_grad = tail_pass(
        normed_t, cots, mixed_t, w_query, w_key, w_value, layer_input[0], norm_gain_one, hidden_cot, moe_small, diagonals, expert_out_sums
    )
    expert_out_grad = expert_out_grad[None, : w_expert_out.shape[1]]
    large = large.reshape(4, width, width)
    return (
        layer_output[None],
        input_grad[None],
        small[0],
        large[0].astype(f32),
        large[1].astype(f32),
        large[2].astype(f32),
        large[3].astype(f32),
        jnp.concatenate([small[2:8, a : a + BUCKETS] for a in range(0, heads * 128 // 6, 128)], axis=0),
        small[1],
        small[8 : 8 + experts].T,
        expert_in_grad.astype(f32),
        expert_out_grad.astype(f32),
    )


def solution(mesh):
    placed = (
        P(("expert", "dp"), "ctx", None),
        P(("expert", "dp"), "ctx", None),
        P(),
        P(),
        P(),
        P(),
        P(),
        P(),
        P(),
        P(),
        P("expert", ("ctx", "dp"), None),
        P("expert", ("ctx", "dp"), None),
        P(("expert", "dp"), "ctx"),
        P(("expert", "dp"), "ctx", None),
        P(("expert", "dp"), "ctx", None),
    )
    return jax.shard_map(
        local,
        mesh=mesh,
        in_specs=placed,
        out_specs=(
            P(("expert", "dp"), "ctx", None),
            P(("expert", "dp"), "ctx", None),
            P(),
            P(),
            P(),
            P(),
            P(),
            P(),
            P(),
            P(),
            P("expert", ("ctx", "dp"), None),
            P("expert", ("ctx", "dp"), None),
        ),
        check_vma=False,
    )
```

time: 855 us -> 492 us (0.58)
  waiting for transfers between devices: 524 us -> 0 us
  Pallas kernels: 105 us -> 468 us
  blocking collectives: 91.2 us -> 0 us
  matrix products: 49 us -> 0 us
  starting transfers between devices: 29.4 us -> 0 us
  between operations: 14.9 us -> 1.12 us
  other arithmetic: 21 us -> 11.2 us
    pallas_call x3 -> x4, Pallas kernels: 105 us -> 468 us  [the longest x1 157 us: front_pass(): pl.pallas_call(partial(front_kernel, heads, n, rows), out_shape=[jax.Shap...]
    all_to_all x6 -> x0, waiting for transfers between devices: 243 us -> none  [the longest x1 98.3 us: local(): held = lax.all_to_all(sent, 'ctx', split_axis=0, concat_axis=0, tiled=True)]
    reduce_scatter x2 -> x0, waiting for transfers between devices: 188 us -> none  [the longest x1 97.2 us: local(): lax.psum_scatter(outer_grad[None], ('ctx', 'dp'), scatter_dimension=1, ti...]
    psum x1 -> x0, waiting for transfers between devices: 91.3 us -> none  [local(): lax.psum((weight_grad(query_cot), weight_grad(key_cot), weight_grad(value...]
    all_to_all x2 -> x0, blocking collectives: 52.7 us -> none  [the longest x1 28.8 us: local(): lax.all_to_all(outgoing, 'expert', split_axis=0, concat_axis=0, tiled=True)]
    dot_general x22 -> x0, matrix products: 49 us -> none  [the longest x11 26.3 us: dot(): return lax.dot_general(a, b, dims, preferred_element_type=f32)]
    psum x1 -> x0, blocking collectives: 38.5 us -> none  [local(): lax.psum((gain_one_grad, table_grad, gain_two_grad, router_grad), everywh...]
    all_to_all x6 -> x0, starting transfers between devices: 28.9 us -> none  [the longest x1 6.48 us: local(): held = lax.all_to_all(sent, 'ctx', split_axis=0, concat_axis=0, tiled=True)]
  transfers between devices with their start and end apart: 11 -> 0, of which waited for: 9 -> 0; matrix products, arithmetic and copies ran while one was open for 7% -> 0% of each run, Pallas kernels for 2% -> 0%
where the time goes in v2:
time: 492 us; the launch traced here: 488 us
  Pallas kernels  468 us (95%)
  other arithmetic  11.2 us (2%)
  local copies, waits for them, and re-layouts  7.59 us (2%)
    pallas_call x1, Pallas kernels, front_pass(): pl.pallas_call(partial(front_kernel, heads, n, rows), out_shape=[jax.Shap...  157 us
    pallas_call x1, Pallas kernels, back_pass(): pl.pallas_call(partial(back_kernel, heads, n, rows), out_shape=[jax.Shape...  124 us
    pallas_call x1, Pallas kernels, tail_pass(): pl.pallas_call(partial(tail_kernel, plans), out_shape=[jax.ShapeDtypeStru...  114 us
    pallas_call x1, Pallas kernels, moe_pass(): pl.pallas_call(partial(moe_kernel, capacity), out_shape=[jax.ShapeDtypeSt...  74 us

profile of v2, /device:TPU:0, one launch (start us, length us, event | category | flops | bytes accessed | tf_op | source)
XLA Modules:
  0.0 488.4 jit_solution(15879372208692194892)
XLA Ops:
  0.6 1.3 pad.4.router_ref
  1.9 156.6 %front_pass.1 = (bf16[4,592,512]{2,1,0:T(8,128)(2,1)}, bf16[768,512]{1,0:T(8,128)(2,1)}, f32[192,2048]{1,0:T(8,128)}, f32[3,2048]{1,0:T(4,128)}, bf16[768,512]{1...) custom-call(bf16[512,768]{1,0:T(8,128)(2,1)} %bitcast.23, ...), custom_call_target="tpu_custom_call" | custom-call | tf_op jit(solution)/shard_map/front_pass/pallas_call | solution.py:684
  158.5 74.0 %moe_pass.1 = (f32[512,768]{1,0:T(8,128)}, bf16[1,512,768]{2,1,0:T(8,128)(2,1)}, f32[512,768]{1,0:T(8,128)}, bf16[768,512]{1,0:T(8,128)(2,1)}, f32[24,768]{1,0:T...) custom-call(bf16[768,512]{1,0:T(8,128)(2,1)} %get-tuple-element.38.mixed_t, bf16[768,768]{1,0:T(8,128)(2,1)} %w_output.1, ...), custom_call_target="tpu_custom_call" | custom-call | tf_op jit(solution)/shard_map/moe_pass/pallas_call | solution.py:366
  232.5 124.4 %back_pass.1 = (bf16[2304,512]{1,0:T(8,128)(2,1)}, f32[3,512]{1,0:T(4,128)}, bf16[96,3072]{1,0:T(8,128)(2,1)}, bf16[4,384,768]{2,1,0:T(8,128)(2,1)}, bf16[512,768]{1,0:T(8,128)(2,1)}) custom-call(bf16[4,592,512]{2,1,0:T(8,128)(2,1)} %get-tuple-element.37.x_ref, bf16[768,512]{1,0:T(8,128)(2,1)} %get-tuple-element.43.do_ref, bf16[12,32]{1,0:T(8,128)(2,1)} %table_ref.3, ...), custom_call_target="tpu_custom_call" | custom-call | tf_op jit(solution)/shard_map/back_pass/pallas_call | solution.py:994
  356.9 2.2 bitcast_convert_fusion.1
  359.1 113.6 %tail_pass.1 = (bf16[3072,768]{1,0:T(8,128)(2,1)}, f32[512,768]{1,0:T(8,128)}, f32[16,768]{1,0:T(8,128)}, bf16[384,768]{1,0:T(8,128)(2,1)}) custom-call(bf16[768,512]{1,0:T(8,128)(2,1)} %get-tuple-element.51.normed_t, bf16[2304,512]{1,0:T(8,128)(2,1)} %get-tuple-element.52.cots, bf16[768,512]{1,0:T(8,128)(2,1)} %get-tuple-element.38.mixed_t, ...), custom_call_target="tpu_custom_call" | custom-call | tf_op jit(solution)/shard_map/tail_pass/pallas_call | solution.py:1307
  472.6 1.4 slice_reduce_fusion
  474.1 0.7 fusion
  474.8 1.3 slice_bitcast_fusion
  476.1 0.6 pad_maximum_fusion
  476.7 2.2 bitcast_convert_fusion
  478.8 0.0 copy-start.1
  478.9 6.2 %slice_convert_fusion = (f32[768,768]{1,0:T(8,128)}, f32[768,768]{1,0:T(8,128)}, f32[768,768]{1,0:T(8,128)}, f32[768,768]{1,0:T(8,128)}) fusion(bf16[3072,768]{1,0:T(8,128)(2,1)} %get-tuple-element.59), kind=kLoop, calls=%fused_computation | loop fusion | flops 2359296 | bytes 14155776 | tf_op jit(solution)/shard_map/convert_element_type | solution.py:1399
  485.1 0.0 copy-start
  485.1 0.0 copy-done.1
  485.1 0.9 copy.29
  486.0 0.8 copy-done
  486.8 1.1 copy.30
Async XLA Ops:
  478.8 6.3 %copy-start.1 = (bf16[512,768]{1,0:T(8,128)(2,1)S(1)}, bf16[512,768]{1,0:T(8,128)(2,1)}, u32[]{:S(2)}) copy-start(bf16[512,768]{1,0:T(8,128)(2,1)} %get-tuple-element.50) | copy-start | bytes 2359300
  485.1 1.7 copy-start

commit v3 on v2

--- a/solution.py
+++ b/solution.py
@@ -90,26 +90,60 @@
     base_ref, far_ref, hidden_cot_ref, mixed_cot_ref, small_ref, gin_hbm, gout_hbm,
     nt, cots, inner, outer, act_all, pre_all, rows_all, cots_all, made, back, part, pair_in, total,
     core_in, far_in, gate_out, gate_in,
-    load_sems, cot_sems, near_sems, far_sems, relay_sems, pair_sems, core_sems, back_sems, gate_sems, stage_sems, free_sem,
+    load_sems, cot_sems, near_sems, far_sems, relay_sems, pair_sems, core_sems, back_sems, gate_sems, stage_sems, free_sem, late_sems,
 ):
     experts = lax.axis_size("expert")
     lanes, lane, core = expert_split()
     me = lane * 2 + core
     other = lane * 2 + 1 - core
-    rows, width = x_ref.shape
-    hidden_size = inner.shape[1]
-    wide = width
+    rows, width = cot_ref.shape
     hidden = hidden_cot_ref
     pieces = 2
     step_rows = rows // pieces
-
-    loads = [
-        pltpu.make_async_copy(inner_hbm, inner, load_sems.at[0]),
-        pltpu.make_async_copy(outer_hbm, outer, load_sems.at[1]),
-    ]
-    for copy in loads:
-        copy.start()
-    barrier, peers = greet(("expert",))
+    hidden_size = inner.shape[1]
+    n = lax.axis_size("ctx")
+    place_z = lax.axis_index("ctx")
+    wide = hidden_size // n
+
+    first = pltpu.make_async_copy(inner_hbm, inner, load_sems.at[n])
+    first.start()
+
+    def chunk_rows(j):
+        return pl.ds(pl.multiple_of(j * wide, wide), wide)
+
+    def chunk_at(f):
+        return jnp.where(place_z == n - 1, n - 1 - f, f)
+
+    def has(f):
+        return (f < n - 1) | ((place_z > 0) & (place_z < n - 1))
+
+    def load(f):
+        at = chunk_rows(chunk_at(f))
+        return pltpu.make_async_copy(outer_hbm.at[at], outer.at[at], load_sems.at[f])
+
+    for f in range(n):
+        @pl.when(has(f))
+        def _():
+            load(f).start()
+
+    def late(up):
+        at = chunk_rows(0 if up else n - 1)
+        return remote(
+            outer_hbm.at[at], outer.at[at], late_sems.at[0, int(up)], late_sems.at[1, int(up)],
+            {"ctx": n - 1 if up else 0},
+        )
+
+    barrier, peers = greet(("expert", "ctx"))
+    pl.semaphore_wait(barrier, peers)
+
+    @pl.when(place_z == n - 2)
+    def _():
+        late(True).start()
+
+    @pl.when(place_z == 1)
+    def _():
+        late(False).start()
+
     sent = []
     for p in range(pieces):
         at = slice(p * step_rows, (p + 1) * step_rows)
@@ -117,8 +151,6 @@
         hidden[at, :] = now
         scale = lax.rsqrt(jnp.mean(now * now, axis=1, keepdims=True) + EPSILON)
         nt[me, at, :] = (now * scale * gain_ref[...].reshape(1, width)).astype(bf16)
-        if p == 0:
-            pl.semaphore_wait(barrier, peers)
         sent.append(gather_start(nt.at[me, at], nt, near_sems.at[p], far_sems.at[p], at))
 
     def gate_rows(source):
@@ -130,146 +162,203 @@
         power = jnp.where(chosen, jnp.exp(jnp.minimum(logits - top, 0.0)), 0.0)
         return power / jnp.sum(power, axis=0, keepdims=True)
 
-    order = [me, other] + [
-        lax.rem(lane - k + lanes, lanes) * 2 + sc for k in range(1, lanes) for sc in range(2)
-    ]
+    def pair_of(k):
+        return [lax.rem(lane - k + lanes, lanes) * 2 + sc for sc in range(2)]
+
+    order = pair_of(1) + [me, other]
+    for k in range(2, lanes):
+        order += pair_of(k)
+    first_group = 4
 
     def fetch(i):
-        return pltpu.make_async_copy(cots_hbm.at[order[i]], cots.at[i % 2], cot_sems.at[i % 2])
-
-    fetch(0).start()
-
-    def process(i, target, middle=None):
-        source = order[i]
-        fetch(i).wait()
-        if i + 1 < len(order):
-            fetch(i + 1).start()
-        block = slice(i * capacity, (i + 1) * capacity)
-        info = info_ref[source]
+        return pltpu.make_async_copy(cots_hbm.at[order[i]], cots.at[i % first_group], cot_sems.at[i % first_group])
+
+    for i in range(first_group):
+        fetch(i).start()
+
+    def place_of(i):
+        info = info_ref[order[i]]
         place = jnp.where(info[0:1] == me, info[2:3], jnp.where(info[1:2] == me, info[3:4], -1))
         slot = lax.broadcasted_iota(jnp.int32, (capacity, rows), 0)
-        hot = slot == place
-        pick = jnp.where(hot, 1.0, 0.0)
-        pick_low = pick.astype(bf16)
-        gates = gate_rows(source)
+        pick = jnp.where(slot == place, 1.0, 0.0)
+        gates = gate_rows(order[i])
         which = lax.broadcasted_iota(jnp.int32, gates.shape, 0)
         own_gate = jnp.sum(jnp.where(which == me, gates, 0.0), axis=0, keepdims=True)
-        slot_gate = jnp.sum(pick * own_gate, axis=1, keepdims=True)
-        rows_all[block, :] = dot(pick_low, nt[source]).astype(bf16)
-        cots_all[block, :] = (slot_gate * dot(pick_low, cots[i % 2])).astype(bf16)
-        made[...] = jnp.zeros_like(made)
-        back[...] = jnp.zeros_like(back)
-
-        def part_of(f, carry):
-            at = pl.ds(pl.multiple_of(f * wide, wide), wide)
-            pre = dot(rows_all[block, :], inner[:, at])
-            cot = dot(cots_all[block, :], outer[at, :], NT)
-            square = pre * pre
-            t = jnp.tanh(pre * (ROOT + (ROOT * 0.044715) * square))
-            half = 0.5 + 0.5 * t
-            act = (pre * half).astype(bf16)
-            slope = half + (0.5 * pre) * (1.0 - t * t) * (ROOT + (ROOT * 3 * 0.044715) * square)
-            back_pre = (cot * slope).astype(bf16)
-            act_all[block, at] = act
-            pre_all[block, at] = back_pre
-            made[...] += dot(act, outer[at, :])
-            back[...] += dot(back_pre, inner[:, at], NT)
-            return carry
-
-        steps = hidden_size // wide
-        if middle is None:
-            lax.fori_loop(0, steps, part_of, 0)
-        else:
-            lax.fori_loop(0, steps // 2, part_of, 0)
-            middle()
-            lax.fori_loop(steps // 2, steps, part_of, 0)
-        gated = slot_gate * made[...].astype(bf16).astype(f32)
-        picked_cot = dot(pick_low, cots[i % 2])
-        slot_cot = jnp.sum(picked_cot * made[...].astype(bf16).astype(f32), axis=1, keepdims=True)
-        gate_out[source] = jnp.broadcast_to(jnp.sum(pick * slot_cot, axis=0, keepdims=True), (8, rows))
+        return place, pick, jnp.sum(pick * own_gate, axis=1, keepdims=True)
+
+    def dispatch(i):
+        fetch(i).wait()
+        _, pick, slot_gate = place_of(i)
+        block = slice(i * capacity, (i + 1) * capacity)
+        rows_all[block, :] = dot(pick.astype(bf16), nt[order[i]]).astype(bf16)
+        cots_all[block, :] = (slot_gate * dot(pick.astype(bf16), cots[i % first_group])).astype(bf16)
+        made[i % first_group] = jnp.zeros((capacity, width), f32)
+        back[i % first_group] = jnp.zeros((capacity, width), f32)
+
+    def part_of(i, f):
+        block = pl.ds(i * capacity if isinstance(i, int) else pl.multiple_of(i * capacity, 16), capacity)
+        at = chunk_rows(chunk_at(f))
+        turn = i % first_group if isinstance(i, int) else i
+        pre = dot(rows_all[block, :], inner[:, at])
+        cot = dot(cots_all[block, :], outer[at, :], NT)
+        square = pre * pre
+        t = jnp.tanh(pre * (ROOT + (ROOT * 0.044715) * square))
+        half = 0.5 + 0.5 * t
+        act = (pre * half).astype(bf16)
+        slope = half + (0.5 * pre) * (1.0 - t * t) * (ROOT + (ROOT * 3 * 0.044715) * square)
+        back_pre = (cot * slope).astype(bf16)
+        act_all[block, at] = act
+        pre_all[block, at] = back_pre
+        made[turn] += dot(act, outer[at, :])
+        back[turn] += dot(back_pre, inner[:, at], NT)
+
+    def finish_source(i, target):
+        place, pick, slot_gate = place_of(i)
+        outcome = made[i % first_group].astype(bf16).astype(f32)
+        slot_cot = jnp.sum(dot(pick.astype(bf16), cots[i % first_group]) * outcome, axis=1, keepdims=True)
+        gate_out[order[i]] = jnp.broadcast_to(jnp.sum(pick * slot_cot, axis=0, keepdims=True), (8, rows))
         column = jnp.broadcast_to(place.astype(f32), (128, rows)).T[:, 0:1]
         lane_at = lax.broadcasted_iota(jnp.int32, (rows, capacity), 1).astype(f32)
         put = jnp.where(lane_at == column, 1.0, 0.0).astype(bf16)
-        target[0] = dot(put, back[...].astype(bf16)).astype(bf16)
-        target[1] = dot(put, gated.astype(bf16)).astype(bf16)
-
-    for copy in loads:
-        copy.wait()
-    process(0, total)
+        target[0] = dot(put, back[i % first_group].astype(bf16)).astype(bf16)
+        target[1] = dot(put, (slot_gate * outcome).astype(bf16)).astype(bf16)
+        if i + first_group < len(order):
+            fetch(i + first_group).start()
+
+    def process(i, target):
+        dispatch(i)
+
+        def step(f, carry):
+            part_of(i, f)
+            return carry
+
+        lax.fori_loop(0, n, step, 0)
+        finish_source(i, target)
+
+    def pair_copies(k, sc):
+        return [
+            remote(part.at[sc, v], pair_in.at[v], pair_sems.at[0, v, k - 1], pair_sems.at[1, v, k - 1], {"expert": other})
+            for v in range(2)
+        ]
+
+    def home_copy(k, sc):
+        to = lax.rem(lane - k + lanes, lanes) * 2 + sc
+        return remote(part.at[sc, 0], far_in.at[k - 1], back_sems.at[0, k - 1], back_sems.at[1, k - 1], {"expert": to})
+
+    def begin_pair(k, sc):
+        @pl.when(core != sc)
+        def _():
+            if k > 1:
+                pl.semaphore_wait(free_sem, 1)
+            for copy in pair_copies(k, sc):
+                copy.start()
+
+    def end_pair(k, sc):
+        @pl.when(core == sc)
+        def _():
+            pair = pair_copies(k, sc)
+            pair[0].wait_recv()
+            part[sc, 0] = (part[sc, 0].astype(f32) + pair_in[0].astype(f32)).astype(bf16)
+            home_copy(k, sc).start()
+            pair[1].wait_recv()
+            far_ref[k - 1] = (part[sc, 1].astype(f32) + pair_in[1].astype(f32)).astype(bf16)
+            if k + 1 < lanes:
+                pl.semaphore_signal(
+                    free_sem, inc=1, device_id={"expert": other}, device_id_type=pl.DeviceIdType.MESH
+                )
+
+    def pair_sent(k):
+        for sc in range(2):
+            @pl.when(core != sc)
+            def _():
+                for copy in pair_copies(k, sc):
+                    copy.wait_send()
+
+    def home_sent(k):
+        for sc in range(2):
+            @pl.when(core == sc)
+            def _():
+                home_copy(k, sc).wait_send()
+
+    dispatch(2)
     for p in range(pieces):
         sent[p][0].wait_recv()
-    process(1, part.at[0])
-    core_copies = [
-        remote(part.at[0, v], core_in.at[v], core_sems.at[0, v], core_sems.at[1, v], {"expert": other}) for v in range(2)
-    ]
-    for copy in core_copies:
-        copy.start()
-
-    def gate_copy(k):
-        to = lax.rem(me + k, experts)
-        return remote(gate_out.at[to], gate_in.at[me], gate_sems.at[0, k - 1], gate_sems.at[1, k - 1], {"expert": to})
-
-    relays, pairs, ready = [], [], []
+    dispatch(3)
+    first.wait()
+    for f in range(n - 1):
+        load(f).wait()
+
+    def steps_of(start):
+        def step(at, carry):
+            part_of(start + lax.rem(at, 2), lax.div(at, 2))
+            return carry
+
+        return step
+
+    lax.fori_loop(0, 2 * (n - 1), steps_of(2), 0)
+    passed_on = []
     for k in range(1, lanes):
         for p in range(pieces):
             sent[p][k].wait_recv()
         passed = relay(k, nt, relay_sems)
         passed.start()
-        relays.append(passed)
-        from_lane = lax.rem(lane - k + lanes, lanes)
-        if k == 1:
+        passed_on.append(passed)
+
+    def relayed(k, sc):
+        @pl.when(core != sc)
+        def _():
+            passed_on[k - 1].wait_recv()
+
+    for sc in range(2):
+        relayed(1, sc)
+        dispatch(sc)
+    lax.fori_loop(0, 2 * (n - 1), steps_of(0), 0)
+
+    @pl.when(has(n - 1))
+    def _():
+        load(n - 1).wait()
+
+    @pl.when(place_z == n - 1)
+    def _():
+        late(True).wait_recv()
+
+    @pl.when(place_z == 0)
+    def _():
+        late(False).wait_recv()
+
+    lax.fori_loop(2 * (n - 1), 2 * n, steps_of(0), 0)
+    finish_source(0, part.at[0])
+    begin_pair(1, 0)
+    finish_source(1, part.at[1])
+    begin_pair(1, 1)
+    end_pair(1, 0)
+    lax.fori_loop(2 * (n - 1), 2 * n, steps_of(2), 0)
+    end_pair(1, 1)
+    pair_sent(1)
+    finish_source(3, part.at[1 - core])
+    core_copies = [
+        remote(part.at[1 - core, v], core_in.at[v], core_sems.at[0, v], core_sems.at[1, v], {"expert": other}) for v in range(2)
+    ]
+    for copy in core_copies:
+        copy.start()
+    finish_source(2, total)
+
+    def gate_copy(k):
+        to = lax.rem(me + k, experts)
+        return remote(gate_out.at[to], gate_in.at[me], gate_sems.at[0, k - 1], gate_sems.at[1, k - 1], {"expert": to})
+
+    for k in range(2, lanes):
+        if k == 2:
             for copy in core_copies:
                 copy.wait_send()
+        home_sent(k - 1)
         for sc in range(2):
-            @pl.when(core != sc)
-            def _():
-                passed.wait_recv()
-
-            process(2 + 2 * (k - 1) + sc, part.at[sc], ready.pop() if ready else None)
-            pair = [
-                remote(part.at[sc, v], pair_in.at[v], pair_sems.at[0, v, k - 1], pair_sems.at[1, v, k - 1], {"expert": other})
-                for v in range(2)
-            ]
-            home = [
-                remote(part.at[sc, 0], far_in.at[k - 1], back_sems.at[0, k - 1], back_sems.at[1, k - 1], {"expert": from_lane * 2 + sc})
-            ]
-
-            @pl.when(core != sc)
-            def _():
-                if k > 1:
-                    pl.semaphore_wait(free_sem, 1)
-                for copy in pair:
-                    copy.start()
-
-            def finish(k=k, sc=sc, pair=pair, home=home):
-                @pl.when(core == sc)
-                def _():
-                    pair[0].wait_recv()
-                    part[sc, 0] = (part[sc, 0].astype(f32) + pair_in[0].astype(f32)).astype(bf16)
-                    home[0].start()
-                    pair[1].wait_recv()
-                    far_ref[k - 1] = (part[sc, 1].astype(f32) + pair_in[1].astype(f32)).astype(bf16)
-                    if k + 1 < lanes:
-                        pl.semaphore_signal(
-                            free_sem, inc=1, device_id={"expert": other}, device_id_type=pl.DeviceIdType.MESH
-                        )
-
-            ready.append(finish)
-            pairs.append((sc, pair, home))
-        if k + 1 < lanes:
-            ready.pop()()
-            for sc, pair, home in pairs[-2:]:
-                @pl.when(core != sc)
-                def _():
-                    for copy in pair:
-                        copy.wait_send()
-
-                @pl.when(core == sc)
-                def _():
-                    for copy in home:
-                        copy.wait_send()
-    if ready:
-        ready.pop()()
+            relayed(k, sc)
+            process(2 * k + sc, part.at[sc])
+            begin_pair(k, sc)
+        for sc in range(2):
+            end_pair(k, sc)
+        pair_sent(k)
     gate_copies = [gate_copy(k) for k in range(1, experts)]
     for copy in gate_copies:
         copy.start()
@@ -278,6 +367,7 @@
         at = slice(b * 128, (b + 1) * 128)
         inner[:, at] = rows_all[at, :].T
         inner[:, slice(count + b * 128, count + (b + 1) * 128)] = cots_all[at, :].T
+    wide = width
     steps = hidden_size // wide
 
     def store(f, v):
@@ -305,11 +395,6 @@
     lax.fori_loop(0, steps, grads, 0)
     for copy in gate_copies:
         copy.wait()
-    core_copies[0].wait_recv()
-    token_cot = total[0].astype(f32) + core_in[0].astype(f32)
-    for k in range(1, lanes):
-        remote(part.at[0, 0], far_in.at[k - 1], back_sems.at[0, k - 1], back_sems.at[1, k - 1], {"expert": other}).wait_recv()
-        token_cot = token_cot + far_in[k - 1].astype(f32)
     gates = gate_rows(me)
     pad = gates.shape[0]
     which = lax.broadcasted_iota(jnp.int32, gates.shape, 0)
@@ -320,41 +405,53 @@
     logit_cot = gates * (gate_cot - jnp.sum(gates * gate_cot, axis=0, keepdims=True))
     three = jnp.concatenate(split3(logit_cot), axis=0)
     router_three = jnp.concatenate([router_ref[...]] * 3, axis=0)
-    normed_cot = token_cot + dot(three, router_three, TN)
     router_grad = dot(three, nt[me])
-    router_grad = router_grad[:pad] + router_grad[pad : 2 * pad] + router_grad[2 * pad :]
-    now = hidden[...]
-    scale = lax.rsqrt(jnp.mean(now * now, axis=1, keepdims=True) + EPSILON)
-    unit = now * scale
-    gained = normed_cot * gain_ref[...].reshape(1, width)
-    hidden_cot = cot_ref[...].astype(f32) + scale * (gained - unit * jnp.mean(unit * gained, axis=1, keepdims=True))
-    hidden_cot_ref[...] = hidden_cot
-    mixed_cot_ref[...] = dot(w_output[...], hidden_cot.astype(bf16), NT).astype(bf16)
-    small_ref[0:8, :] = jnp.broadcast_to(jnp.sum(unit * normed_cot, axis=0, keepdims=True), (8, width))
-    small_ref[8:, :] = router_grad
-    core_copies[1].wait_recv()
-    base_ref[...] = now + (total[1].astype(f32) + core_in[1].astype(f32))
+    small_ref[8:, :] = router_grad[:pad] + router_grad[pad : 2 * pad] + router_grad[2 * pad :]
+    for copy in core_copies:
+        copy.wait_recv()
+    for k in range(1, lanes):
+        remote(part.at[0, 0], far_in.at[k - 1], back_sems.at[0, k - 1], back_sems.at[1, k - 1], {"expert": other}).wait_recv()
+    gain = gain_ref[...].reshape(1, width)
+    gain_grad = jnp.zeros((1, width), f32)
+    for start in range(0, rows, 128):
+        at = slice(start, start + 128)
+        normed_cot = total[0, at, :].astype(f32) + core_in[0, at, :].astype(f32)
+        for k in range(1, lanes):
+            normed_cot = normed_cot + far_in[k - 1, at, :].astype(f32)
+        normed_cot = normed_cot + dot(three[:, at], router_three, TN)
+        now = hidden[at, :]
+        scale = lax.rsqrt(jnp.mean(now * now, axis=1, keepdims=True) + EPSILON)
+        unit = now * scale
+        gained = normed_cot * gain
+        hidden_cot = cot_ref[at, :].astype(f32) + scale * (gained - unit * jnp.mean(unit * gained, axis=1, keepdims=True))
+        hidden_cot_ref[at, :] = hidden_cot
+        mixed_cot_ref[:, at] = dot(w_output[...], hidden_cot.astype(bf16), NT).astype(bf16)
+        gain_grad = gain_grad + jnp.sum(unit * normed_cot, axis=0, keepdims=True)
+        base_ref[at, :] = now + (total[1, at, :].astype(f32) + core_in[1, at, :].astype(f32))
+    small_ref[0:8, :] = jnp.broadcast_to(gain_grad, (8, width))
     store(steps - 1, 0).wait()
     store(steps - 1, 1).wait()
-    for sc, pair, home in pairs[-2:]:
-        @pl.when(core != sc)
-        def _():
-            for copy in pair:
-                copy.wait_send()
-
-        @pl.when(core == sc)
-        def _():
-            for copy in home:
-                copy.wait_send()
-    for copy in relays:
+    home_sent(lanes - 1)
+    if lanes == 2:
+        for copy in core_copies:
+            copy.wait_send()
+    for copy in passed_on:
         copy.wait_send()
     for p in range(pieces):
         for copy in sent[p]:
             copy.wait_send()
 
+    @pl.when(place_z == n - 2)
+    def _():
+        late(True).wait_send()
+
+    @pl.when(place_z == 1)
+    def _():
+        late(False).wait_send()
+
 
 def moe_pass(capacity, mixed_t, w_output, x, cot, gain, router, info, cots, inner, outer):
-    rows, width = x.shape
+    rows, width = cot.shape
     experts = cots.shape[0]
     lanes = experts // 2
     hidden_size = inner.shape[1]
@@ -378,15 +475,15 @@
         out_specs=[vmem] * 5 + [hbm] * 2,
         scratch_shapes=[
             pltpu.VMEM((experts, rows, width), bf16),
-            pltpu.VMEM((2, rows, width), bf16),
+            pltpu.VMEM((4, rows, width), bf16),
             pltpu.VMEM((width, hidden_size), bf16),
             pltpu.VMEM((hidden_size, width), bf16),
             pltpu.VMEM((total, hidden_size), bf16),
             pltpu.VMEM((total, hidden_size), bf16),
             pltpu.VMEM((total, width), bf16),
             pltpu.VMEM((total, width), bf16),
-            pltpu.VMEM((capacity, width), f32),
-            pltpu.VMEM((capacity, width), f32),
+            pltpu.VMEM((4, capacity, width), f32),
+            pltpu.VMEM((4, capacity, width), f32),
             pltpu.VMEM((2, 2, rows, width), bf16),
             pltpu.VMEM((2, rows, width), bf16),
             pltpu.VMEM((2, rows, width), bf16),
@@ -394,8 +491,8 @@
             pltpu.VMEM((far, rows, width), bf16),
             pltpu.VMEM((experts, 8, rows), f32),
             pltpu.VMEM((experts, 8, rows), f32),
-            dma((2,)),
-            dma((2,)),
+            dma((lax.axis_size("ctx") + 1,)),
+            dma((4,)),
             dma((2, 2)),
             dma((2, 2, far)),
             dma((2, far)),
@@ -405,6 +502,7 @@
             dma((2, experts - 1)),
             dma((2,)),
             pltpu.SemaphoreType.REGULAR,
+            dma((2, 2)),
         ],
         compiler_params=pltpu.CompilerParams(
             collective_id=1, has_side_effects=True, vmem_limit_bytes=65000 * 1024
@@ -483,7 +581,9 @@
     def holds(way, s):
         return me - s >= 0 if way == 0 else me + s < n
 
-    def passes(way, s):
+    def passes(way, s, v):
+        if v == 1 and s == n - 2:
+            return None
         return (me - s >= 0) & (me < n - 1) if way == 0 else (me + s < n) & (me > 0)
 
     def advance(s, v):
@@ -493,9 +593,10 @@
                 def _():
                     along(way, s - 1, v).wait_recv()
 
-            @pl.when(passes(way, s))
-            def _():
-                along(way, s, v).start()
+            if passes(way, s, v) is not None:
+                @pl.when(passes(way, s, v))
+                def _():
+                    along(way, s, v).start()
 
             if s > 0:
                 @pl.when(holds(way, s))
@@ -558,6 +659,7 @@
 
     advance(1, 0)
     advance(1, 1)
+    advance(2, 0)
     for copy in held_copies:
         copy.wait_recv()
 
@@ -627,18 +729,16 @@
 
         @pl.when(h == 0)
         def _():
-            advance(2, 0)
+            advance(2, 1)
 
         @pl.when(h == 1)
         def _():
-            advance(2, 1)
+            for s in range(3, n):
+                advance(s, 0)
 
         return carry
 
     lax.fori_loop(0, heads, head, 0)
-    for s in range(3, n):
-        for v in range(2):
-            advance(s, v)
     relays = []
     for k in range(1, experts // 2):
         sent[k].wait_recv()
@@ -656,9 +756,12 @@
     for v in range(2):
         for s in range(n):
             for way in range(2):
-                @pl.when(passes(way, s))
-                def _():
-                    along(way, s, v).wait_send()
+                if v == 1 and s == n - 1:
+                    continue
+                if passes(way, s, v) is not None:
+                    @pl.when(passes(way, s, v))
+                    def _():
+                        along(way, s, v).wait_send()
 
                 if s > 0 or way == 0:
                     @pl.when(holds(way, s))
@@ -855,6 +958,8 @@
 
     do_in[me] = do_ref[pl.ds(pl.multiple_of(me * group, 16), group), :]
 
+    sum_sides(0, order[0])
+    advance(0)
     for copy in arriving:
         copy.wait_recv()
 
@@ -947,13 +1052,17 @@
         for i in range(1, 8):
             line = line + pltpu.roll(eight, 2 * BLK - i, 1)[i : i + 1]
         diag_ref[pl.ds(h, 1), :] = line
+        for step in range(1, heads):
+            @pl.when(h == step - 1)
+            def _():
+                if step < n:
+                    sum_sides(0, order[step])
+                advance(step)
+
         return carry
 
-    lax.fori_loop(0, 1, head, 0)
-    sum_sides(0, order[0])
-    advance(0)
-    lax.fori_loop(1, heads, head, 0)
-    for step in range(1, steps):
+    lax.fori_loop(0, heads, head, 0)
+    for step in range(heads, steps):
         if step < n:
             sum_sides(0, order[step])
         advance(step)

time: 492 us -> 469 us (0.953)
  Pallas kernels: 468 us -> 446 us
    pallas_call x1, Pallas kernels: 157 us -> 136 us  [front_pass(): pl.pallas_call(partial(front_kernel, heads, n, rows), out_shape=[jax.Shap...]
    pallas_call x1, Pallas kernels: 124 us -> 113 us  [back_pass(): pl.pallas_call(partial(back_kernel, heads, n, rows), out_shape=[jax.Shape...]
    pallas_call x1, Pallas kernels: 74 us -> 79.6 us  [moe_pass(): pl.pallas_call(partial(moe_kernel, capacity), out_shape=[jax.ShapeDtypeSt...]
where the time goes in v3:
time: 469 us; the launch traced here: 466 us
  Pallas kernels  446 us (95%)
  other arithmetic  11.2 us (2%)
  local copies, waits for them, and re-layouts  7.59 us (2%)
    pallas_call x1, Pallas kernels, front_pass(): pl.pallas_call(partial(front_kernel, heads, n, rows), out_shape=[jax.Shap...  136 us
    pallas_call x1, Pallas kernels, tail_pass(): pl.pallas_call(partial(tail_kernel, plans), out_shape=[jax.ShapeDtypeStru...  118 us
    pallas_call x1, Pallas kernels, back_pass(): pl.pallas_call(partial(back_kernel, heads, n, rows), out_shape=[jax.Shape...  113 us
    pallas_call x1, Pallas kernels, moe_pass(): pl.pallas_call(partial(moe_kernel, capacity), out_shape=[jax.ShapeDtypeSt...  79.6 us

profile of v3, /device:TPU:0, one launch (start us, length us, event | category | flops | bytes accessed | tf_op | source)
XLA Modules:
  0.0 466.2 jit_solution(15289124404626557008)
XLA Ops:
  0.6 1.3 pad.4.router_ref
  1.9 135.7 %front_pass.1 = (bf16[4,592,512]{2,1,0:T(8,128)(2,1)}, bf16[768,512]{1,0:T(8,128)(2,1)}, f32[192,2048]{1,0:T(8,128)}, f32[3,2048]{1,0:T(4,128)}, bf16[768,512]{1...) custom-call(bf16[512,768]{1,0:T(8,128)(2,1)} %bitcast.23, ...), custom_call_target="tpu_custom_call" | custom-call | tf_op jit(solution)/shard_map/front_pass/pallas_call | solution.py:787
  137.6 79.6 %moe_pass.1 = (f32[512,768]{1,0:T(8,128)}, bf16[1,512,768]{2,1,0:T(8,128)(2,1)}, f32[512,768]{1,0:T(8,128)}, bf16[768,512]{1,0:T(8,128)(2,1)}, f32[24,768]{1,0:T...) custom-call(bf16[768,512]{1,0:T(8,128)(2,1)} %get-tuple-element.38.mixed_t, bf16[768,768]{1,0:T(8,128)(2,1)} %w_output.1, ...), custom_call_target="tpu_custom_call" | custom-call | tf_op jit(solution)/shard_map/moe_pass/pallas_call | solution.py:463
  217.3 113.0 %back_pass.1 = (bf16[2304,512]{1,0:T(8,128)(2,1)}, f32[3,512]{1,0:T(4,128)}, bf16[96,3072]{1,0:T(8,128)(2,1)}, bf16[4,384,768]{2,1,0:T(8,128)(2,1)}, bf16[512,768]{1,0:T(8,128)(2,1)}) custom-call(bf16[4,592,512]{2,1,0:T(8,128)(2,1)} %get-tuple-element.37.x_ref, bf16[768,512]{1,0:T(8,128)(2,1)} %get-tuple-element.43.do_ref, bf16[12,32]{1,0:T(8,128)(2,1)} %table_ref.3, ...), custom_call_target="tpu_custom_call" | custom-call | tf_op jit(solution)/shard_map/back_pass/pallas_call | solution.py:1103
  330.3 2.2 bitcast_convert_fusion.1
  332.5 118.2 %tail_pass.1 = (bf16[3072,768]{1,0:T(8,128)(2,1)}, f32[512,768]{1,0:T(8,128)}, f32[16,768]{1,0:T(8,128)}, bf16[384,768]{1,0:T(8,128)(2,1)}) custom-call(bf16[768,512]{1,0:T(8,128)(2,1)} %get-tuple-element.51.normed_t, bf16[2304,512]{1,0:T(8,128)(2,1)} %get-tuple-element.52.cots, bf16[768,512]{1,0:T(8,128)(2,1)} %get-tuple-element.38.mixed_t, ...), custom_call_target="tpu_custom_call" | custom-call | tf_op jit(solution)/shard_map/tail_pass/pallas_call | solution.py:1416
  450.7 1.4 slice_reduce_fusion
  452.1 0.7 fusion
  452.8 1.3 slice_bitcast_fusion
  454.1 0.6 pad_maximum_fusion
  454.7 2.2 bitcast_convert_fusion
  456.9 0.0 copy-start.1
  456.9 6.2 %slice_convert_fusion = (f32[768,768]{1,0:T(8,128)}, f32[768,768]{1,0:T(8,128)}, f32[768,768]{1,0:T(8,128)}, f32[768,768]{1,0:T(8,128)}) fusion(bf16[3072,768]{1,0:T(8,128)(2,1)} %get-tuple-element.59), kind=kLoop, calls=%fused_computation | loop fusion | flops 2359296 | bytes 14155776 | tf_op jit(solution)/shard_map/convert_element_type | solution.py:1508
  463.1 0.0 copy-start
  463.1 0.0 copy-done.1
  463.1 0.9 copy.29
  464.0 0.8 copy-done
  464.8 1.1 copy.30
Async XLA Ops:
  456.9 6.3 %copy-start.1 = (bf16[512,768]{1,0:T(8,128)(2,1)S(1)}, bf16[512,768]{1,0:T(8,128)(2,1)}, u32[]{:S(2)}) copy-start(bf16[512,768]{1,0:T(8,128)(2,1)} %get-tuple-element.50) | copy-start | bytes 2359300
  463.1 1.7 copy-start

commit v4 on v3

--- a/solution.py
+++ b/solution.py
@@ -1318,37 +1318,41 @@
         send_stage((0, c), 0)
     parts = [(1, 0), (0, 0), (1, 1), (0, 1)]
 
-    turned = dot(wq[...], cots[:width, :]) + dot(wk[...], cots[width : 2 * width, :]) + dot(wv[...], cots[2 * width :, :])
-    cot = turned.T
-    x = x_ref[...].astype(f32)
-    gain = gain_ref[...].reshape(1, width)
-    scale = lax.rsqrt(jnp.mean(x * x, axis=1, keepdims=True) + EPSILON)
-    unit = x * scale
-    gained = cot * gain
-    input_grad_ref[...] = hidden_cot_ref[...] + scale * (gained - unit * jnp.mean(unit * gained, axis=1, keepdims=True))
-    gain_grad = jnp.sum(unit * cot, axis=0, keepdims=True)
-    which = lax.broadcasted_iota(jnp.int32, (8, width), 0)
-    low = jnp.where(which == 0, gain_grad, jnp.where(which == 1, moe_small_ref[0:8, :], 0.0))
-    distance = lax.broadcasted_iota(jnp.int32, (2 * BLK, width), 0)
-    lane = lax.broadcasted_iota(jnp.int32, (2 * BLK, width), 1)
-    far = jnp.full(distance.shape, BUCKETS // 2, jnp.int32)
-    for limit in THRESHOLDS:
-        far = far + jnp.where(distance >= limit, 1, 0)
-    bucket = jnp.where(distance < BUCKETS // 2, distance, far)
-    own = distance < THRESHOLDS[-1]
-    which = lax.broadcasted_iota(jnp.int32, (8, width), 0)
-    lane_row = lax.broadcasted_iota(jnp.int32, (8, width), 1)
-    heads = diag_ref.shape[0]
-    for h in range(heads):
-        at = lax.axis_index("ctx") * heads + h
-        start = lax.div(at, 6) * 128
-        hot = jnp.where(own & (bucket + start == lane), 1.0, 0.0).astype(bf16)
-        three = split3(jnp.broadcast_to(diag_ref[h : h + 1, :], (16, 2 * BLK)))
-        near = (dot(three[0], hot) + dot(three[1], hot) + dot(three[2], hot))[0:1]
-        near = jnp.where(lane_row[0:1] == start + BUCKETS - 1, -jnp.sum(near, axis=1, keepdims=True), near)
-        low = low + jnp.where(which == 2 + lax.rem(at, 6), near, 0.0)
-    small[0:8, :] = low
-    small[8:16, :] = moe_small_ref[8:16, :]
+    def make_small():
+        turned = dot(wq[...], cots[:width, :]) + dot(wk[...], cots[width : 2 * width, :]) + dot(wv[...], cots[2 * width :, :])
+        cot = turned.T
+        x = x_ref[...].astype(f32)
+        gain = gain_ref[...].reshape(1, width)
+        scale = lax.rsqrt(jnp.mean(x * x, axis=1, keepdims=True) + EPSILON)
+        unit = x * scale
+        gained = cot * gain
+        input_grad_ref[...] = hidden_cot_ref[...] + scale * (gained - unit * jnp.mean(unit * gained, axis=1, keepdims=True))
+        gain_grad = jnp.sum(unit * cot, axis=0, keepdims=True)
+        which = lax.broadcasted_iota(jnp.int32, (8, width), 0)
+        low = jnp.where(which == 0, gain_grad, jnp.where(which == 1, moe_small_ref[0:8, :], 0.0))
+        near_rows, near_lanes = 128, 256
+        distance = lax.broadcasted_iota(jnp.int32, (near_rows, near_lanes), 0)
+        lane = lax.broadcasted_iota(jnp.int32, (near_rows, near_lanes), 1)
+        far = jnp.full(distance.shape, BUCKETS // 2, jnp.int32)
+        for limit in THRESHOLDS:
+            far = far + jnp.where(distance >= limit, 1, 0)
+        bucket = jnp.where(distance < BUCKETS // 2, distance, far)
+        own = distance < THRESHOLDS[-1]
+        lane_row = lax.broadcasted_iota(jnp.int32, (1, near_lanes), 1)
+        which = lax.broadcasted_iota(jnp.int32, (8, near_lanes), 0)
+        sums = jnp.zeros((8, near_lanes), f32)
+        heads = diag_ref.shape[0]
+        for h in range(heads):
+            at = lax.axis_index("ctx") * heads + h
+            start = lax.div(at, 6) * 128
+            hot = jnp.where(own & (bucket + start == lane), 1.0, 0.0).astype(bf16)
+            three = split3(jnp.broadcast_to(diag_ref[h : h + 1, :near_rows], (16, near_rows)))
+            near = (dot(three[0], hot) + dot(three[1], hot) + dot(three[2], hot))[0:1]
+            near = jnp.where(lane_row == start + BUCKETS - 1, -jnp.sum(near, axis=1, keepdims=True), near)
+            sums = sums + jnp.where(which == 2 + lax.rem(at, 6), near, 0.0)
+        low = low + jnp.concatenate([sums, jnp.zeros((8, width - near_lanes), f32)], axis=1)
+        small[0:8, :] = low
+        small[8:16, :] = moe_small_ref[8:16, :]
 
     def send_small(step):
         name = ORDERS[0][step]
@@ -1379,7 +1383,6 @@
         small[...] = total
 
     last = len(ORDERS[0])
-    send_small(0)
     for step in range(last):
         for part in parts:
             add_stage(part, step)
@@ -1387,19 +1390,24 @@
                 send_stage(part, step + 1)
             else:
                 give_stage(part, step)
-        add_small(step)
-        if step + 1 < last:
-            send_small(step + 1)
-        advance(step + 1)
-    small_out_ref[...] = small[...]
+        if step == 0:
+            make_small()
+        else:
+            add_small(step - 1)
+        send_small(step)
+        if step == 1:
+            advance(1)
+    for step in range(2, line_steps):
+        advance(step)
     for step in range(last - 1, -1, -1):
         for part in parts:
             for copy in flying[part]:
                 copy.wait()
             if step > 0:
                 give_stage(part, step - 1)
-    for step in range(last + 1, line_steps):
-        advance(step)
+        if step == last - 1:
+            add_small(last - 1)
+            small_out_ref[...] = small[...]
     finish(eout_ref)
     drain()
     grads_ref[...] = whole[...]
@@ -1448,6 +1456,49 @@
     )(normed_t, cots, mixed_t, wq, wk, wv, x, gain, hidden_cot, moe_small, diag, sums)
 
 
+def finish_kernel(heads, width, large_ref, small_ref, *refs):
+    extra = (len(refs) - 7) // 2
+    ins, outs, others = refs[:extra], refs[extra : extra + 7], refs[extra + 7 :]
+    for k in range(4):
+        outs[k][...] = large_ref[k].astype(f32)
+    for source, out in zip(ins, others):
+        out[...] = source[...].astype(f32)
+
+    @pl.when(pl.program_id(0) == 0)
+    def _():
+        outs[4][...] = small_ref[0:1, :].reshape(width)
+        outs[5][...] = small_ref[1:2, :].reshape(width)
+        for a in range(0, heads, 6):
+            outs[6][a : a + 6, :] = small_ref[2:8, a // 6 * 128 : a // 6 * 128 + BUCKETS]
+
+
+def finish_pass(large, small, heads, extra):
+    _, width, _ = large.shape
+    steps = 6
+    tall = width // steps
+    whole = pl.BlockSpec(small.shape, lambda i: (0, 0))
+
+    def cut(array):
+        return pl.BlockSpec((array.shape[0] // steps, array.shape[1]), lambda i: (i, 0))
+
+    flat = pl.BlockSpec((width,), lambda i: (0,))
+    return pl.pallas_call(
+        partial(finish_kernel, heads, width),
+        grid=(steps,),
+        out_shape=[jax.ShapeDtypeStruct((width, width), f32)] * 4
+        + [jax.ShapeDtypeStruct((width,), f32)] * 2
+        + [jax.ShapeDtypeStruct((heads, BUCKETS), f32)]
+        + [jax.ShapeDtypeStruct(array.shape, f32) for array in extra],
+        in_specs=[pl.BlockSpec((4, tall, width), lambda i: (0, i, 0)), whole] + [cut(array) for array in extra],
+        out_specs=[pl.BlockSpec((tall, width), lambda i: (i, 0))] * 4
+        + [flat] * 2
+        + [pl.BlockSpec((heads, BUCKETS), lambda i: (0, 0))]
+        + [cut(array) for array in extra],
+        compiler_params=pltpu.CompilerParams(vmem_limit_bytes=32 * 1024 * 1024),
+        name="finish_pass",
+    )(large, small, *extra)
+
+
 def local(
     layer_input,
     cotangent,
@@ -1492,25 +1543,29 @@
     cots, diagonals, expert_in_grad, expert_out_sums, layer_output = back_pass(
         held, mixed_cot, rel_table, attended_whole, lse, base, far, cut(inner_grad), cut(outer_grad)
     )
-    expert_in_grad = expert_in_grad[None, : w_expert_in.shape[1]]
     large, input_grad, small, expert_out_grad = tail_pass(
         normed_t, cots, mixed_t, w_query, w_key, w_value, layer_input[0], norm_gain_one, hidden_cot, moe_small, diagonals, expert_out_sums
     )
-    expert_out_grad = expert_out_grad[None, : w_expert_out.shape[1]]
-    large = large.reshape(4, width, width)
+    extra = [expert_in_grad, expert_out_grad]
+    fits = [array.shape[0] % 96 == 0 for array in extra]
+    finished = finish_pass(
+        large.reshape(4, width, width), small, heads, [array for array, fit in zip(extra, fits) if fit]
+    )
+    converted = list(finished[7:])
+    extra = [converted.pop(0) if fit else array.astype(f32) for array, fit in zip(extra, fits)]
     return (
         layer_output[None],
         input_grad[None],
-        small[0],
-        large[0].astype(f32),
-        large[1].astype(f32),
-        large[2].astype(f32),
-        large[3].astype(f32),
-        jnp.concatenate([small[2:8, a : a + BUCKETS] for a in range(0, heads * 128 // 6, 128)], axis=0),
-        small[1],
+        finished[4],
+        finished[0],
+        finished[1],
+        finished[2],
+        finished[3],
+        finished[6],
+        finished[5],
         small[8 : 8 + experts].T,
-        expert_in_grad.astype(f32),
-        expert_out_grad.astype(f32),
+        extra[0][None, : w_expert_in.shape[1]],
+        extra[1][None, : w_expert_out.shape[1]],
     )
 
 

time: 469 us -> 463 us (0.987)
  other arithmetic: 11.2 us -> 0 us
    convert_element_type x3 -> x0, other arithmetic: 10.6 us -> none  [the longest x1 6.25 us: local(): large[3].astype(f32)]
    pallas_call x0 -> x1, Pallas kernels: none -> 4.94 us  [finish_pass(): pl.pallas_call(partial(finish_kernel, heads, width), grid=(steps,), out_s...]
where the time goes in v4:
time: 463 us; the launch traced here: 460 us
  Pallas kernels  450 us (97%)
  local copies, waits for them, and re-layouts  8.88 us (2%)
    pallas_call x1, Pallas kernels, front_pass(): pl.pallas_call(partial(front_kernel, heads, n, rows), out_shape=[jax.Shap...  136 us
    pallas_call x1, Pallas kernels, tail_pass(): pl.pallas_call(partial(tail_kernel, plans), out_shape=[jax.ShapeDtypeStru...  117 us
    pallas_call x1, Pallas kernels, back_pass(): pl.pallas_call(partial(back_kernel, heads, n, rows), out_shape=[jax.Shape...  113 us
    pallas_call x1, Pallas kernels, moe_pass(): pl.pallas_call(partial(moe_kernel, capacity), out_shape=[jax.ShapeDtypeSt...  79.6 us

profile of v4, /device:TPU:0, one launch (start us, length us, event | category | flops | bytes accessed | tf_op | source)
XLA Modules:
  0.0 459.9 jit_solution(15435664335514567746)
XLA Ops:
  0.6 1.3 pad.4.router_ref
  1.9 135.7 %front_pass.1 = (bf16[4,592,512]{2,1,0:T(8,128)(2,1)}, bf16[768,512]{1,0:T(8,128)(2,1)}, f32[192,2048]{1,0:T(8,128)}, f32[3,2048]{1,0:T(4,128)}, bf16[768,512]{1...) custom-call(bf16[512,768]{1,0:T(8,128)(2,1)} %bitcast.21, ...), custom_call_target="tpu_custom_call" | custom-call | tf_op jit(solution)/shard_map/front_pass/pallas_call | solution.py:787
  137.6 79.6 %moe_pass.1 = (f32[512,768]{1,0:T(8,128)}, bf16[1,512,768]{2,1,0:T(8,128)(2,1)}, f32[512,768]{1,0:T(8,128)}, bf16[768,512]{1,0:T(8,128)(2,1)}, f32[24,768]{1,0:T...) custom-call(bf16[768,512]{1,0:T(8,128)(2,1)} %get-tuple-element.47.mixed_t, bf16[768,768]{1,0:T(8,128)(2,1)} %w_output.1, ...), custom_call_target="tpu_custom_call" | custom-call | tf_op jit(solution)/shard_map/moe_pass/pallas_call | solution.py:463
  217.2 113.1 %back_pass.1 = (bf16[2304,512]{1,0:T(8,128)(2,1)}, f32[3,512]{1,0:T(4,128)}, bf16[96,3072]{1,0:T(8,128)(2,1)}, bf16[4,384,768]{2,1,0:T(8,128)(2,1)}, bf16[512,768]{1,0:T(8,128)(2,1)}) custom-call(bf16[4,592,512]{2,1,0:T(8,128)(2,1)} %get-tuple-element.46.x_ref, bf16[768,512]{1,0:T(8,128)(2,1)} %get-tuple-element.52.do_ref, bf16[12,32]{1,0:T(8,128)(2,1)} %table_ref.3, ...), custom_call_target="tpu_custom_call" | custom-call | tf_op jit(solution)/shard_map/back_pass/pallas_call | solution.py:1103
  330.3 0.0 copy-start.1
  330.3 116.8 %tail_pass.1 = (bf16[3072,768]{1,0:T(8,128)(2,1)}, f32[512,768]{1,0:T(8,128)}, f32[16,768]{1,0:T(8,128)}, bf16[384,768]{1,0:T(8,128)(2,1)}) custom-call(bf16[768,512]{1,0:T(8,128)(2,1)} %get-tuple-element.60.normed_t, bf16[2304,512]{1,0:T(8,128)(2,1)} %get-tuple-element.61.cots, bf16[768,512]{1,0:T(8,128)(2,1)} %get-tuple-element.47.mixed_t, ...), custom_call_target="tpu_custom_call" | custom-call | tf_op jit(solution)/shard_map/tail_pass/pallas_call | solution.py:1424
  447.1 1.3 slice_bitcast_fusion
  448.4 0.0 copy-done.1
  448.4 0.0 copy-start
  448.4 2.3 copy-done
  450.8 0.0 copy-start.2
  450.8 1.1 copy-done.2
  451.8 0.0 copy-start.3
  451.8 0.8 copy-done.3
  452.6 0.0 copy-start.5
  452.6 0.0 copy-start.4
  452.6 4.9 %finish_pass.1 = (f32[768,768]{1,0:T(8,128)}, f32[768,768]{1,0:T(8,128)}, f32[768,768]{1,0:T(8,128)}, f32[768,768]{1,0:T(8,128)}, f32[768]{0:T(1024)}, /*index=5...) custom-call(bf16[4,768,768]{2,1,0:T(8,128)(2,1)S(1)} %bitcast.20, f32[16,768]{1,0:T(8,128)S(1)} %copy-done.3, ...), custom_call_target="tpu_custom_call" | custom-call | tf_op jit(solution)/shard_map/finish_pass/pallas_call | solution.py:1485
  457.6 0.0 copy-done.5
  457.6 0.9 copy.29
  458.4 0.0 copy-done.4
  458.5 1.1 copy.30
Async XLA Ops:
  330.3 118.1 %copy-start.1 = (bf16[96,3072]{1,0:T(8,128)(2,1)S(1)}, bf16[96,3072]{1,0:T(8,128)(2,1)}, u32[]{:S(2)}) copy-start(bf16[96,3072]{1,0:T(8,128)(2,1)} %get-tuple-element.69.refs_0_) | copy-start | bytes 1769476
  448.4 2.3 copy-start
  450.8 1.1 copy-start.2
  451.8 0.8 copy-start.3
  452.6 4.9 %copy-start.5 = (bf16[512,768]{1,0:T(8,128)(2,1)S(1)}, bf16[512,768]{1,0:T(8,128)(2,1)}, u32[]{:S(2)}) copy-start(bf16[512,768]{1,0:T(8,128)(2,1)} %get-tuple-element.59) | copy-start | bytes 2359300
  452.6 5.8 %copy-start.4 = (f32[512,768]{1,0:T(8,128)S(1)}, f32[512,768]{1,0:T(8,128)}, u32[]{:S(2)}) copy-start(f32[512,768]{1,0:T(8,128)} %get-tuple-element.66) | copy-start | bytes 4718596

commit v5 on v4

--- a/solution.py
+++ b/solution.py
@@ -90,7 +90,7 @@
     base_ref, far_ref, hidden_cot_ref, mixed_cot_ref, small_ref, gin_hbm, gout_hbm,
     nt, cots, inner, outer, act_all, pre_all, rows_all, cots_all, made, back, part, pair_in, total,
     core_in, far_in, gate_out, gate_in,
-    load_sems, cot_sems, near_sems, far_sems, relay_sems, pair_sems, core_sems, back_sems, gate_sems, stage_sems, free_sem, late_sems,
+    load_sems, cot_sems, near_sems, far_sems, relay_sems, pair_sems, core_sems, back_sems, gate_sems, stage_sems, free_sem, late_sems, router_rows,
 ):
     experts = lax.axis_size("expert")
     lanes, lane, core = expert_split()
@@ -153,8 +153,12 @@
         nt[me, at, :] = (now * scale * gain_ref[...].reshape(1, width)).astype(bf16)
         sent.append(gather_start(nt.at[me, at], nt, near_sems.at[p], far_sems.at[p], at))
 
+    router_rows[...] = jnp.zeros_like(router_rows)
+    router_rows[0:experts, :] = router_ref[...].astype(f32)
+    router = router_rows[...].astype(bf16)
+
     def gate_rows(source):
-        logits = dot(router_ref[...], nt[source], NT)
+        logits = dot(router, nt[source], NT)
         which = lax.broadcasted_iota(jnp.int32, logits.shape, 0)
         info = info_ref[source]
         chosen = (which == info[0:1]) | (which == info[1:2])
@@ -404,7 +408,7 @@
         gate_cot = gate_cot + jnp.where(which == source, gate_in[source][0:1], 0.0)
     logit_cot = gates * (gate_cot - jnp.sum(gates * gate_cot, axis=0, keepdims=True))
     three = jnp.concatenate(split3(logit_cot), axis=0)
-    router_three = jnp.concatenate([router_ref[...]] * 3, axis=0)
+    router_three = jnp.concatenate([router] * 3, axis=0)
     router_grad = dot(three, nt[me])
     small_ref[8:, :] = router_grad[:pad] + router_grad[pad : 2 * pad] + router_grad[2 * pad :]
     for copy in core_copies:
@@ -467,7 +471,7 @@
             jax.ShapeDtypeStruct((far, rows, width), bf16),
             jax.ShapeDtypeStruct((rows, width), f32),
             jax.ShapeDtypeStruct((width, rows), bf16),
-            jax.ShapeDtypeStruct((8 + router.shape[0], width), f32),
+            jax.ShapeDtypeStruct((24, width), f32),
             jax.ShapeDtypeStruct((width, hidden_size), bf16),
             jax.ShapeDtypeStruct((hidden_size, width), bf16),
         ],
@@ -503,6 +507,7 @@
             dma((2,)),
             pltpu.SemaphoreType.REGULAR,
             dma((2, 2)),
+            pltpu.VMEM((16, width), f32),
         ],
         compiler_params=pltpu.CompilerParams(
             collective_id=1, has_side_effects=True, vmem_limit_bytes=65000 * 1024
@@ -1494,7 +1499,7 @@
         + [flat] * 2
         + [pl.BlockSpec((heads, BUCKETS), lambda i: (0, 0))]
         + [cut(array) for array in extra],
-        compiler_params=pltpu.CompilerParams(vmem_limit_bytes=32 * 1024 * 1024),
+        compiler_params=pltpu.CompilerParams(vmem_limit_bytes=60 * 1024 * 1024),
         name="finish_pass",
     )(large, small, *extra)
 
@@ -1532,7 +1537,7 @@
     )
     inner_weight = inner_weight[:, : w_expert_in.shape[1]].reshape(width, -1)
     outer_weight = outer_weight[:, : w_expert_out.shape[1]].reshape(-1, width)
-    router_t = jnp.pad(w_router.T, ((0, 16 - experts), (0, 0)))
+    router_t = w_router.T
     base, far, hidden_cot, mixed_cot, moe_small, inner_grad, outer_grad = moe_pass(
         capacity, mixed_t, w_output, layer_input[0], cotangent[0], norm_gain_two, router_t, info_all, cots_all, inner_weight, outer_weight
     )

time: 463 us -> 460 us (level)
  local copies, waits for them, and re-layouts: 8.88 us -> 3.37 us
where the time goes in v5:
time: 460 us; the launch traced here: 457 us
  Pallas kernels  453 us (98%)
    pallas_call x1, Pallas kernels, front_pass(): pl.pallas_call(partial(front_kernel, heads, n, rows), out_shape=[jax.Shap...  136 us
    pallas_call x1, Pallas kernels, tail_pass(): pl.pallas_call(partial(tail_kernel, plans), out_shape=[jax.ShapeDtypeStru...  117 us
    pallas_call x1, Pallas kernels, back_pass(): pl.pallas_call(partial(back_kernel, heads, n, rows), out_shape=[jax.Shape...  113 us
    pallas_call x1, Pallas kernels, moe_pass(): pl.pallas_call(partial(moe_kernel, capacity), out_shape=[jax.ShapeDtypeSt...  79.7 us

profile of v5, /device:TPU:0, one launch (start us, length us, event | category | flops | bytes accessed | tf_op | source)
XLA Modules:
  0.0 457.1 jit_solution(3720399807047616678)
XLA Ops:
  0.6 135.7 %front_pass.1 = (bf16[4,592,512]{2,1,0:T(8,128)(2,1)}, bf16[768,512]{1,0:T(8,128)(2,1)}, f32[192,2048]{1,0:T(8,128)}, f32[3,2048]{1,0:T(4,128)}, bf16[768,512]{1...) custom-call(bf16[512,768]{1,0:T(8,128)(2,1)} %bitcast.20, ...), custom_call_target="tpu_custom_call" | custom-call | tf_op jit(solution)/shard_map/front_pass/pallas_call | solution.py:792
  136.4 79.7 %moe_pass.1 = (f32[512,768]{1,0:T(8,128)}, bf16[1,512,768]{2,1,0:T(8,128)(2,1)}, f32[512,768]{1,0:T(8,128)}, bf16[768,512]{1,0:T(8,128)(2,1)}, f32[24,768]{1,0:T...) custom-call(bf16[768,512]{1,0:T(8,128)(2,1)} %get-tuple-element.47.mixed_t, bf16[768,768]{1,0:T(8,128)(2,1)} %w_output.1, ...), custom_call_target="tpu_custom_call" | custom-call | tf_op jit(solution)/shard_map/moe_pass/pallas_call | solution.py:467
  216.0 113.0 %back_pass.1 = (bf16[2304,512]{1,0:T(8,128)(2,1)}, f32[3,512]{1,0:T(4,128)}, bf16[96,3072]{1,0:T(8,128)(2,1)}, bf16[4,384,768]{2,1,0:T(8,128)(2,1)}, bf16[512,768]{1,0:T(8,128)(2,1)}) custom-call(bf16[4,592,512]{2,1,0:T(8,128)(2,1)} %get-tuple-element.46.x_ref, bf16[768,512]{1,0:T(8,128)(2,1)} %get-tuple-element.52.do_ref, bf16[12,32]{1,0:T(8,128)(2,1)} %table_ref.3, ...), custom_call_target="tpu_custom_call" | custom-call | tf_op jit(solution)/shard_map/back_pass/pallas_call | solution.py:1108
  329.1 116.5 %tail_pass.1 = (bf16[3072,768]{1,0:T(8,128)(2,1)}, f32[512,768]{1,0:T(8,128)}, f32[16,768]{1,0:T(8,128)}, bf16[384,768]{1,0:T(8,128)(2,1)}) custom-call(bf16[768,512]{1,0:T(8,128)(2,1)} %get-tuple-element.60.normed_t, bf16[2304,512]{1,0:T(8,128)(2,1)} %get-tuple-element.61.cots, bf16[768,512]{1,0:T(8,128)(2,1)} %get-tuple-element.47.mixed_t, ...), custom_call_target="tpu_custom_call" | custom-call | tf_op jit(solution)/shard_map/tail_pass/pallas_call | solution.py:1429
  445.6 1.3 slice_bitcast_fusion
  446.9 0.0 copy-start.1
  446.9 0.0 copy-start
  446.9 7.9 %finish_pass.1 = (f32[768,768]{1,0:T(8,128)}, f32[768,768]{1,0:T(8,128)}, f32[768,768]{1,0:T(8,128)}, f32[768,768]{1,0:T(8,128)}, f32[768]{0:T(1024)}, /*index=5...) custom-call(bf16[4,768,768]{2,1,0:T(8,128)(2,1)} %bitcast.25, ...), custom_call_target="tpu_custom_call" | custom-call | tf_op jit(solution)/shard_map/finish_pass/pallas_call | solution.py:1490
  454.8 0.0 copy-done.1
  454.8 0.9 copy.29
  455.7 0.0 copy-done
  455.7 1.1 copy.30
Async XLA Ops:
  446.9 7.9 %copy-start.1 = (bf16[512,768]{1,0:T(8,128)(2,1)S(1)}, bf16[512,768]{1,0:T(8,128)(2,1)}, u32[]{:S(2)}) copy-start(bf16[512,768]{1,0:T(8,128)(2,1)} %get-tuple-element.59) | copy-start | bytes 2359300
  446.9 8.8 %copy-start = (f32[512,768]{1,0:T(8,128)S(1)}, f32[512,768]{1,0:T(8,128)}, u32[]{:S(2)}) copy-start(f32[512,768]{1,0:T(8,128)} %get-tuple-element.66) | copy-start | bytes 4718596

commit v6 on v5

--- a/solution.py
+++ b/solution.py
@@ -1402,8 +1402,6 @@
         send_small(step)
         if step == 1:
             advance(1)
-    for step in range(2, line_steps):
-        advance(step)
     for step in range(last - 1, -1, -1):
         for part in parts:
             for copy in flying[part]:
@@ -1413,6 +1411,8 @@
         if step == last - 1:
             add_small(last - 1)
             small_out_ref[...] = small[...]
+            for slot in range(2, line_steps):
+                advance(slot)
     finish(eout_ref)
     drain()
     grads_ref[...] = whole[...]

time: 460 us -> 460 us (level)
  no operation moved by 1% of the time
where the time goes in v6:
time: 460 us; the launch traced here: 457 us
  Pallas kernels  453 us (98%)
    pallas_call x1, Pallas kernels, front_pass(): pl.pallas_call(partial(front_kernel, heads, n, rows), out_shape=[jax.Shap...  136 us
    pallas_call x1, Pallas kernels, tail_pass(): pl.pallas_call(partial(tail_kernel, plans), out_shape=[jax.ShapeDtypeStru...  117 us
    pallas_call x1, Pallas kernels, back_pass(): pl.pallas_call(partial(back_kernel, heads, n, rows), out_shape=[jax.Shape...  113 us
    pallas_call x1, Pallas kernels, moe_pass(): pl.pallas_call(partial(moe_kernel, capacity), out_shape=[jax.ShapeDtypeSt...  79.7 us

profile of v6, /device:TPU:0, one launch (start us, length us, event | category | flops | bytes accessed | tf_op | source)
XLA Modules:
  0.0 457.1 jit_solution(13096391159006974818)
XLA Ops:
  0.6 135.7 %front_pass.1 = (bf16[4,592,512]{2,1,0:T(8,128)(2,1)}, bf16[768,512]{1,0:T(8,128)(2,1)}, f32[192,2048]{1,0:T(8,128)}, f32[3,2048]{1,0:T(4,128)}, bf16[768,512]{1...) custom-call(bf16[512,768]{1,0:T(8,128)(2,1)} %bitcast.20, ...), custom_call_target="tpu_custom_call" | custom-call | tf_op jit(solution)/shard_map/front_pass/pallas_call | solution.py:792
  136.4 79.7 %moe_pass.1 = (f32[512,768]{1,0:T(8,128)}, bf16[1,512,768]{2,1,0:T(8,128)(2,1)}, f32[512,768]{1,0:T(8,128)}, bf16[768,512]{1,0:T(8,128)(2,1)}, f32[24,768]{1,0:T...) custom-call(bf16[768,512]{1,0:T(8,128)(2,1)} %get-tuple-element.47.mixed_t, bf16[768,768]{1,0:T(8,128)(2,1)} %w_output.1, ...), custom_call_target="tpu_custom_call" | custom-call | tf_op jit(solution)/shard_map/moe_pass/pallas_call | solution.py:467
  216.0 113.0 %back_pass.1 = (bf16[2304,512]{1,0:T(8,128)(2,1)}, f32[3,512]{1,0:T(4,128)}, bf16[96,3072]{1,0:T(8,128)(2,1)}, bf16[4,384,768]{2,1,0:T(8,128)(2,1)}, bf16[512,768]{1,0:T(8,128)(2,1)}) custom-call(bf16[4,592,512]{2,1,0:T(8,128)(2,1)} %get-tuple-element.46.x_ref, bf16[768,512]{1,0:T(8,128)(2,1)} %get-tuple-element.52.do_ref, bf16[12,32]{1,0:T(8,128)(2,1)} %table_ref.3, ...), custom_call_target="tpu_custom_call" | custom-call | tf_op jit(solution)/shard_map/back_pass/pallas_call | solution.py:1108
  329.1 116.5 %tail_pass.1 = (bf16[3072,768]{1,0:T(8,128)(2,1)}, f32[512,768]{1,0:T(8,128)}, f32[16,768]{1,0:T(8,128)}, bf16[384,768]{1,0:T(8,128)(2,1)}) custom-call(bf16[768,512]{1,0:T(8,128)(2,1)} %get-tuple-element.60.normed_t, bf16[2304,512]{1,0:T(8,128)(2,1)} %get-tuple-element.61.cots, bf16[768,512]{1,0:T(8,128)(2,1)} %get-tuple-element.47.mixed_t, ...), custom_call_target="tpu_custom_call" | custom-call | tf_op jit(solution)/shard_map/tail_pass/pallas_call | solution.py:1429
  445.6 1.3 slice_bitcast_fusion
  446.9 0.0 copy-start.1
  446.9 0.0 copy-start
  446.9 7.9 %finish_pass.1 = (f32[768,768]{1,0:T(8,128)}, f32[768,768]{1,0:T(8,128)}, f32[768,768]{1,0:T(8,128)}, f32[768,768]{1,0:T(8,128)}, f32[768]{0:T(1024)}, /*index=5...) custom-call(bf16[4,768,768]{2,1,0:T(8,128)(2,1)} %bitcast.25, ...), custom_call_target="tpu_custom_call" | custom-call | tf_op jit(solution)/shard_map/finish_pass/pallas_call | solution.py:1490
  454.8 0.0 copy-done.1
  454.8 0.9 copy.29
  455.7 0.0 copy-done
  455.7 1.1 copy.30
Async XLA Ops:
  446.9 7.9 %copy-start.1 = (bf16[512,768]{1,0:T(8,128)(2,1)S(1)}, bf16[512,768]{1,0:T(8,128)(2,1)}, u32[]{:S(2)}) copy-start(bf16[512,768]{1,0:T(8,128)(2,1)} %get-tuple-element.59) | copy-start | bytes 2359300
  446.9 8.8 %copy-start = (f32[512,768]{1,0:T(8,128)S(1)}, f32[512,768]{1,0:T(8,128)}, u32[]{:S(2)}) copy-start(f32[512,768]{1,0:T(8,128)} %get-tuple-element.66) | copy-start | bytes 4718596
